TPU v7x, 32 devices: a whole 2x2x4 slice. The times are simulated.
32 devices in a mesh: dp: 8 (over z, x), tensor: 4 (over y, core).
Axes of the slice: x: 2, y: 2, z: 4, core: 2. Of those that a mesh axis runs over, the one named last changes fastest.
Arguments:
- hidden_in: bfloat16 [4096, 1024], P('dp'), may hold values from -6 to 6
- logits_in: bfloat16 [8, 16, 512, 512], P('dp', 'tensor'), may hold values from -5 to 5
- cotangent: bfloat16 [4096, 1024], P(('dp', 'tensor')), may hold values from -6 to 6
- bucket_ids: int32 [8], P('dp'), may hold values from 0 to 2, as said below
- seq_counts: int32 [8], P('dp'), may hold values from 1 to 4, as said below
- key_mask: int32 [4096], P('dp'), may hold values from 0 to 1, as said below
- w_qkv: float32 [2, 3, 1024, 1024], P(None, None, 'dp', 'tensor'), may hold values from -0.1875 to 0.1875
- w_out: float32 [2, 1024, 1024], P(None, 'tensor', 'dp'), may hold values from -1 to 1
- w_in: float32 [2, 1024, 4096], P(None, 'dp', 'tensor'), may hold values from -0.1875 to 0.1875
- w_back: float32 [2, 4096, 1024], P(None, 'tensor', 'dp'), may hold values from -0.09375 to 0.09375
- vectors: float32 [2, 8, 1024], P(None, None, ('dp', 'tensor')), may hold values from -0.4 to 1.4, as said below
- bias_in: float32 [2, 4096], P(None, ('dp', 'tensor')), may hold values from -1 to 1
- m_qkv: float32 [2, 3, 1024, 1024], P(None, None, 'dp', 'tensor'), may hold values from -6 to 6
- m_out: float32 [2, 1024, 1024], P(None, 'tensor', 'dp'), may hold values from -6 to 6
- m_in: float32 [2, 1024, 4096], P(None, 'dp', 'tensor'), may hold values from -6 to 6
- m_back: float32 [2, 4096, 1024], P(None, 'tensor', 'dp'), may hold values from -6 to 6
- m_vectors: float32 [2, 8, 1024], P(None, None, ('dp', 'tensor')), may hold values from -6 to 6
- m_bias: float32 [2, 4096], P(None, ('dp', 'tensor')), may hold values from -6 to 6
- v_qkv: float32 [2, 3, 1024, 1024], P(None, None, 'dp', 'tensor'), may hold values from 0.5 to 50
- v_out: float32 [2, 1024, 1024], P(None, 'tensor', 'dp'), may hold values from 0.5 to 50
- v_in: float32 [2, 1024, 4096], P(None, 'dp', 'tensor'), may hold values from 0.5 to 50
- v_back: float32 [2, 4096, 1024], P(None, 'tensor', 'dp'), may hold values from 0.5 to 50
- v_vectors: float32 [2, 8, 1024], P(None, None, ('dp', 'tensor')), may hold values from 0.5 to 50
- v_bias: float32 [2, 4096], P(None, ('dp', 'tensor')), may hold values from 0.5 to 50
Outputs:
- hidden_out: bfloat16 [4096, 1024], P(('dp', 'tensor'))
- logits_out: bfloat16 [8, 16, 512, 512], P('dp', 'tensor')
- grad_hidden: float32 [4096, 1024], P(('dp', 'tensor'))
- grad_logits: float32 [8, 16, 512, 512], P('dp', 'tensor')
- grad_qkv: float32 [2, 3, 1024, 1024], P(None, None, 'dp', 'tensor')
- grad_wout: float32 [2, 1024, 1024], P(None, 'tensor', 'dp')
- grad_win: float32 [2, 1024, 4096], P(None, 'dp', 'tensor')
- grad_wback: float32 [2, 4096, 1024], P(None, 'tensor', 'dp')
- grad_vectors: float32 [2, 8, 1024], P(None, None, ('dp', 'tensor'))
- grad_bias: float32 [2, 4096], P(None, ('dp', 'tensor'))
- new_qkv: float32 [2, 3, 1024, 1024], P(None, None, 'dp', 'tensor')
- new_wout: float32 [2, 1024, 1024], P(None, 'tensor', 'dp')
- new_win: float32 [2, 1024, 4096], P(None, 'dp', 'tensor')
- new_wback: float32 [2, 4096, 1024], P(None, 'tensor', 'dp')
- new_vectors: float32 [2, 8, 1024], P(None, None, ('dp', 'tensor'))
- new_bias: float32 [2, 4096], P(None, ('dp', 'tensor'))
- first_qkv: float32 [2, 3, 1024, 1024], P(None, None, 'dp', 'tensor')
- first_wout: float32 [2, 1024, 1024], P(None, 'tensor', 'dp')
- first_win: float32 [2, 1024, 4096], P(None, 'dp', 'tensor')
- first_wback: float32 [2, 4096, 1024], P(None, 'tensor', 'dp')
- first_vectors: float32 [2, 8, 1024], P(None, None, ('dp', 'tensor'))
- first_bias: float32 [2, 4096], P(None, ('dp', 'tensor'))
- trust_ratios: float32 [2, 6], replicated
Inputs may be any that keep to these rules, and one draw needn't show every extreme that they name: The tokens of dp index d form sequences of 512 / 4 * 2**bucket_ids[d] tokens each, one after another. `seq_counts`: at least half of the sequences of a dp index are in use; the others are empty. `key_mask`: within each sequence the ones form a prefix of more than half of its tokens. `vectors`: rows 0 and 1 of each layer are gains, rows 2 to 7 biases.
All inputs are finite; a program needn't handle non-finite values.
Results may differ from a plain program's by a relative error of at most 0.038.
Values may be sent and summed in bfloat16 or wider, within the bound.
A program may use at most 192 MiB of HBM per device.

v0:
```python
import jax
import jax.numpy as jnp
from jax import lax
from jax.sharding import PartitionSpec as P

LAYERS = 2


NORM_EPS = 1e-05
ADAM_EPS = 1e-06
BETA_ONE = 0.9
BETA_TWO = 0.999
CORRECT_ONE = 1.0
CORRECT_TWO = 0.632304575228943
LEARN_RATE = 0.3
DECAY_RATE = 0.01
NEG_FILL = -1e30


def layer_norm(values, gain, shift):
    center = values - jnp.mean(values, axis=-1, keepdims=True)
    spread = jnp.mean(center * center, axis=-1, keepdims=True)
    return center * lax.rsqrt(spread + NORM_EPS) * gain + shift


def gelu_exact(values):
    return jax.nn.gelu(values, approximate=False)


def shards(
    hidden_in,
    logits_in,
    cotangent,
    bucket_ids,
    seq_counts,
    key_mask,
    w_qkv,
    w_out,
    w_in,
    w_back,
    vectors,
    bias_in,
    m_qkv,
    m_out,
    m_in,
    m_back,
    m_vectors,
    m_bias,
    v_qkv,
    v_out,
    v_in,
    v_back,
    v_vectors,
    v_bias,
):
    tensor_parts = lax.axis_size("tensor")
    tensor_index = lax.axis_index("tensor")
    data_parts = lax.axis_size("dp")
    tokens_here = hidden_in.shape[0]
    share_rows = tokens_here // tensor_parts
    first_row = tensor_index * share_rows
    block_count = logits_in.shape[0]
    heads_here = logits_in.shape[1]
    block_len = logits_in.shape[2]
    model_width = hidden_in.shape[1]
    head_cols = w_qkv.shape[3]
    head_size = head_cols // heads_here
    hidden_cols = w_in.shape[2]
    score_scale = head_size ** (-0.5)
    bucket = bucket_ids[0]
    seq_span = jnp.where(
        bucket == 0, block_len // 4, jnp.where(bucket == 1, block_len // 2, block_len)
    )
    position = jnp.arange(tokens_here, dtype=jnp.int32)
    seq_flat = position // seq_span
    seq_of = seq_flat.reshape(block_count, block_len)
    live_keys = ((key_mask == 1) & (seq_flat < seq_counts[0])).reshape(block_count, block_len)
    allowed = (seq_of[:, :, None] == seq_of[:, None, :]) & live_keys[:, None, :]
    vec_all, bin_all = (
        lax.all_gather(vectors.astype(jnp.bfloat16), ("dp", "tensor"), axis=2, tiled=True),
        lax.all_gather(bias_in.astype(jnp.bfloat16), ("dp", "tensor"), axis=1, tiled=True),
    )
    vec_all = vec_all.astype(jnp.float32)
    bin_all = bin_all.astype(jnp.float32)

    def sum_forward(term_fn):
        return lax.psum_scatter(
            term_fn(jnp.int32(0), share_rows * lax.axis_size("tensor")).astype(jnp.bfloat16),
            "tensor",
            scatter_dimension=0,
            tiled=True,
        ).astype(jnp.float32)

    def sum_backward(term_fn):
        return lax.psum_scatter(
            term_fn(jnp.int32(0), share_rows * lax.axis_size("tensor")).astype(jnp.bfloat16),
            "tensor",
            scatter_dimension=0,
            tiled=True,
        ).astype(jnp.float32)

    def gather_rows(own_rows):
        return lax.all_gather(own_rows, "tensor", axis=0, tiled=True)

    def gather_grads(own_rows):
        return lax.all_gather(own_rows, "tensor", axis=0, tiled=True)

    def own_cols(vector):
        return lax.dynamic_slice_in_dim(vector, tensor_index * head_cols, head_cols)

    def place_cols(part_sum, total_len, offset):
        return lax.dynamic_update_slice(jnp.zeros((total_len,), jnp.float32), part_sum, (offset,))

    def blocked(matrix):
        return matrix.reshape(block_count, block_len, head_cols)

    def headed(matrix):
        return matrix.reshape(block_len, heads_here, head_size)

    def block_scores(query_b, keys_b, earlier_b):
        raw = jnp.einsum(
            "ihe,jhe->hij", headed(query_b), headed(keys_b), preferred_element_type=jnp.float32
        )
        return raw * score_scale + earlier_b.astype(jnp.float32)

    def attend_block(inputs):
        query_b, keys_b, values_b, earlier_b, allowed_b = inputs
        scores = block_scores(query_b, keys_b, earlier_b)
        row_top = jnp.max(jnp.where(allowed_b[None], scores, NEG_FILL), axis=-1, keepdims=True)
        unscaled = jnp.exp(jnp.where(allowed_b[None], scores - row_top, NEG_FILL))
        row_total = jnp.sum(unscaled, axis=-1, keepdims=True)
        row_total = jnp.where(row_total > 0.5, row_total, 1.0)
        probs_low = (unscaled / row_total).astype(jnp.bfloat16)
        mixed = jnp.einsum(
            "hij,jhe->ihe", probs_low, headed(values_b), preferred_element_type=jnp.float32
        )
        return (
            mixed.reshape(block_len, head_cols).astype(jnp.bfloat16),
            scores.astype(jnp.bfloat16),
            row_top,
            row_total,
        )

    def attend_back(inputs):
        query_b, keys_b, values_b, earlier_b, allowed_b, row_top, row_total, dmixed_b, dlater_b = (
            inputs
        )
        scores = block_scores(query_b, keys_b, earlier_b)
        unscaled = jnp.exp(jnp.where(allowed_b[None], scores - row_top, NEG_FILL))
        probs = unscaled / row_total
        probs_low = probs.astype(jnp.bfloat16)
        dmixed_heads = headed(dmixed_b)
        dvalues = jnp.einsum(
            "hij,ihe->jhe", probs_low, dmixed_heads, preferred_element_type=jnp.float32
        )
        dprobs = jnp.einsum(
            "ihe,jhe->hij", dmixed_heads, headed(values_b), preferred_element_type=jnp.float32
        )
        dlocal = probs * (dprobs - jnp.sum(probs * dprobs, axis=-1, keepdims=True))
        dscores = (dlocal + dlater_b.astype(jnp.float32)).astype(jnp.bfloat16)
        dquery = (
            jnp.einsum("hij,jhe->ihe", dscores, headed(keys_b), preferred_element_type=jnp.float32)
            * score_scale
        )
        dkeys = (
            jnp.einsum("hij,ihe->jhe", dscores, headed(query_b), preferred_element_type=jnp.float32)
            * score_scale
        )
        return (
            dquery.reshape(block_len, head_cols),
            dkeys.reshape(block_len, head_cols),
            dvalues.reshape(block_len, head_cols),
            dscores,
        )

    full_in = hidden_in
    own_in = lax.dynamic_slice_in_dim(hidden_in, first_row, share_rows, 0)
    earlier = logits_in
    records = []
    for layer_at in range(LAYERS):
        fetched = (
            lax.all_gather(w_qkv[layer_at].astype(jnp.bfloat16), "dp", axis=1, tiled=True),
            lax.all_gather(w_out[layer_at].astype(jnp.bfloat16), "dp", axis=1, tiled=True),
            lax.all_gather(w_in[layer_at].astype(jnp.bfloat16), "dp", axis=0, tiled=True),
            lax.all_gather(w_back[layer_at].astype(jnp.bfloat16), "dp", axis=1, tiled=True),
        )
        forward_wqkv, forward_wout, forward_win, forward_wback = fetched
        forward_vector = vec_all[layer_at]
        forward_query = (
            jnp.dot(full_in, forward_wqkv[0], preferred_element_type=jnp.float32)
            + own_cols(forward_vector[2])
        ).astype(jnp.bfloat16)
        forward_keys = jnp.dot(full_in, forward_wqkv[1], preferred_element_type=jnp.float32).astype(
            jnp.bfloat16
        )
        forward_values = (
            jnp.dot(full_in, forward_wqkv[2], preferred_element_type=jnp.float32)
            + own_cols(forward_vector[3])
        ).astype(jnp.bfloat16)
        forward_attn_out, stored, forward_row_top, forward_row_total = lax.map(
            attend_block,
            (
                blocked(forward_query),
                blocked(forward_keys),
                blocked(forward_values),
                earlier,
                allowed,
            ),
        )
        forward_attn_out = forward_attn_out.reshape(tokens_here, head_cols)

        def attn_term(begin_row, row_count):
            return jnp.dot(forward_attn_out, forward_wout, preferred_element_type=jnp.float32)

        forward_mid_pre = sum_forward(attn_term) + forward_vector[4] + own_in.astype(jnp.float32)
        mid_own = layer_norm(forward_mid_pre, forward_vector[0], forward_vector[5]).astype(
            jnp.bfloat16
        )
        forward_mid_full = gather_rows(mid_own)
        bias_here = lax.dynamic_slice_in_dim(
            bin_all[layer_at], tensor_index * hidden_cols, hidden_cols
        )
        forward_pre_act = (
            jnp.dot(forward_mid_full, forward_win, preferred_element_type=jnp.float32) + bias_here
        )
        forward_active = gelu_exact(forward_pre_act).astype(jnp.bfloat16)

        def ffn_term(begin_row, row_count):
            return jnp.dot(forward_active, forward_wback, preferred_element_type=jnp.float32)

        forward_out_pre = sum_forward(ffn_term) + forward_vector[6] + mid_own.astype(jnp.float32)
        out_own = layer_norm(forward_out_pre, forward_vector[1], forward_vector[7]).astype(
            jnp.bfloat16
        )
        forward_state = (
            forward_query,
            forward_keys,
            forward_values,
            forward_attn_out,
            forward_row_top,
            forward_row_total,
            forward_mid_pre,
            forward_mid_full,
            forward_pre_act,
            forward_out_pre,
        )
        out_own, stored, state = (out_own, stored, forward_state)
        records.append((full_in, earlier, fetched, state))
        earlier = stored
        own_in = out_own
        if layer_at + 1 < LAYERS:
            full_in = gather_rows(out_own)
    logits_out = earlier
    d_own = cotangent.astype(jnp.float32)
    d_later = jnp.zeros_like(logits_in)
    mat_grads = [None] * LAYERS
    vec_grads = [None] * LAYERS
    bin_grads = [None] * LAYERS
    for layer_at in reversed(range(LAYERS)):
        full_in, earlier, fetched, state = records[layer_at]
        wqkv = lax.all_gather(w_qkv[layer_at].astype(jnp.bfloat16), "dp", axis=1, tiled=True)
        wout = lax.all_gather(w_out[layer_at].astype(jnp.bfloat16), "dp", axis=1, tiled=True)
        win = lax.all_gather(w_in[layer_at].astype(jnp.bfloat16), "dp", axis=0, tiled=True)
        wback = lax.all_gather(w_back[layer_at].astype(jnp.bfloat16), "dp", axis=1, tiled=True)
        (
            query,
            keys,
            values,
            attn_out,
            backward_row_top,
            backward_row_total,
            mid_pre,
            mid_full,
            pre_act,
            out_pre,
        ) = state
        backward_vector = vec_all[layer_at]
        out_grad, gain_two, shift_two = jax.vjp(
            layer_norm, out_pre, backward_vector[1], backward_vector[7]
        )[1](d_own)
        d_ffn = gather_grads(out_grad.astype(jnp.bfloat16))
        active = gelu_exact(pre_act).astype(jnp.bfloat16)
        grad_back = jnp.einsum("tf,td->fd", active, d_ffn, preferred_element_type=jnp.float32)
        d_active = jnp.einsum("td,fd->tf", d_ffn, wback, preferred_element_type=jnp.float32)
        d_pre = jax.vjp(gelu_exact, pre_act)[1](d_active)[0].astype(jnp.bfloat16)
        grad_in = jnp.einsum("td,tf->df", mid_full, d_pre, preferred_element_type=jnp.float32)

        def mid_term(begin_row, row_count):
            return jnp.einsum("tf,df->td", d_pre, win, preferred_element_type=jnp.float32)

        mid_grad = sum_backward(mid_term) + out_grad
        attn_grad, gain_one, shift_one = jax.vjp(
            layer_norm, mid_pre, backward_vector[0], backward_vector[5]
        )[1](mid_grad)
        d_attn = gather_grads(attn_grad.astype(jnp.bfloat16))
        grad_out_proj = jnp.einsum(
            "tc,td->cd", attn_out, d_attn, preferred_element_type=jnp.float32
        )
        d_mixed = jnp.einsum("td,cd->tc", d_attn, wout, preferred_element_type=jnp.float32).astype(
            jnp.bfloat16
        )
        backward_dquery, backward_dkeys, backward_dvalues, backward_dscores = lax.map(
            attend_back,
            (
                blocked(query),
                blocked(keys),
                blocked(values),
                earlier,
                allowed,
                backward_row_top,
                backward_row_total,
                blocked(d_mixed),
                d_later,
            ),
        )
        backward_dquery = backward_dquery.reshape(tokens_here, head_cols).astype(jnp.bfloat16)
        backward_dkeys = backward_dkeys.reshape(tokens_here, head_cols).astype(jnp.bfloat16)
        backward_dvalues = backward_dvalues.reshape(tokens_here, head_cols).astype(jnp.bfloat16)
        grad_qkv = jnp.stack(
            [
                jnp.einsum(
                    "td,tc->dc", full_in, backward_dquery, preferred_element_type=jnp.float32
                ),
                jnp.einsum(
                    "td,tc->dc", full_in, backward_dkeys, preferred_element_type=jnp.float32
                ),
                jnp.einsum(
                    "td,tc->dc", full_in, backward_dvalues, preferred_element_type=jnp.float32
                ),
            ]
        )

        def input_term(begin_row, row_count):
            total_term = jnp.einsum(
                "tc,dc->td", backward_dquery, wqkv[0], preferred_element_type=jnp.float32
            )
            total_term = total_term + jnp.einsum(
                "tc,dc->td", backward_dkeys, wqkv[1], preferred_element_type=jnp.float32
            )
            return total_term + jnp.einsum(
                "tc,dc->td", backward_dvalues, wqkv[2], preferred_element_type=jnp.float32
            )

        in_grad = sum_backward(input_term) + attn_grad
        col_offset = tensor_index * head_cols
        vec_grad = jnp.stack(
            [
                gain_one,
                gain_two,
                place_cols(
                    jnp.sum(backward_dquery.astype(jnp.float32), axis=0), model_width, col_offset
                ),
                place_cols(
                    jnp.sum(backward_dvalues.astype(jnp.float32), axis=0), model_width, col_offset
                ),
                jnp.sum(attn_grad, axis=0),
                shift_one,
                jnp.sum(out_grad, axis=0),
                shift_two,
            ]
        )
        bin_grad = place_cols(
            jnp.sum(d_pre.astype(jnp.float32), axis=0),
            hidden_cols * tensor_parts,
            tensor_index * hidden_cols,
        )
        d_own, d_later, mats, vec_grad, bin_grad = (
            in_grad,
            backward_dscores,
            (grad_qkv, grad_out_proj, grad_in, grad_back),
            vec_grad,
            bin_grad,
        )
        totals = (
            lax.psum(mats[0].astype(jnp.bfloat16), "dp").astype(jnp.float32),
            lax.psum(mats[1].astype(jnp.bfloat16), "dp").astype(jnp.float32),
            lax.psum(mats[2].astype(jnp.bfloat16), "dp").astype(jnp.float32),
            lax.psum(mats[3].astype(jnp.bfloat16), "dp").astype(jnp.float32),
        )
        data_index = lax.axis_index("dp")
        mat_grads[layer_at] = tuple(
            (
                lax.dynamic_slice_in_dim(
                    whole,
                    data_index * (whole.shape[axis_at] // data_parts),
                    whole.shape[axis_at] // data_parts,
                    axis_at,
                )
                for whole, axis_at in zip(totals, (1, 1, 0, 1))
            )
        )
        vec_grads[layer_at] = vec_grad
        bin_grads[layer_at] = bin_grad
    grad_logits = d_later.astype(jnp.float32)
    vec_sum, bin_sum = (
        lax.psum_scatter(jnp.stack(vec_grads), ("dp", "tensor"), scatter_dimension=2, tiled=True),
        lax.psum_scatter(jnp.stack(bin_grads), ("dp", "tensor"), scatter_dimension=1, tiled=True),
    )
    grads_all = (
        jnp.stack([mat_grads[level_at][0] for level_at in range(LAYERS)]),
        jnp.stack([mat_grads[level_at][1] for level_at in range(LAYERS)]),
        jnp.stack([mat_grads[level_at][2] for level_at in range(LAYERS)]),
        jnp.stack([mat_grads[level_at][3] for level_at in range(LAYERS)]),
        vec_sum,
        bin_sum,
    )
    masters = (w_qkv, w_out, w_in, w_back, vectors, bias_in)
    firsts = (m_qkv, m_out, m_in, m_back, m_vectors, m_bias)
    seconds = (v_qkv, v_out, v_in, v_back, v_vectors, v_bias)
    decays = (DECAY_RATE, DECAY_RATE, DECAY_RATE, DECAY_RATE, 0.0, 0.0)
    moved = []
    for master, gradient, first_prev, second_prev, decay_rate in zip(
        masters, grads_all, firsts, seconds, decays
    ):
        moment_one = BETA_ONE * first_prev + (1.0 - BETA_ONE) * gradient
        moment_two = BETA_TWO * second_prev + (1.0 - BETA_TWO) * gradient * gradient
        update = (
            moment_one / CORRECT_ONE / (jnp.sqrt(moment_two / CORRECT_TWO) + ADAM_EPS)
            + decay_rate * master
        )
        moved.append((moment_one, update))
    weight_sq = jnp.stack(
        [jnp.sum((master * master).reshape(LAYERS, -1), axis=1) for master in masters]
    )
    update_sq = jnp.stack(
        [jnp.sum((moved_one[1] * moved_one[1]).reshape(LAYERS, -1), axis=1) for moved_one in moved]
    )
    weight_tot, update_tot = lax.psum((weight_sq, update_sq), ("dp", "tensor"))
    trust_all = jnp.sqrt(weight_tot) / jnp.sqrt(update_tot)
    new_params = tuple(
        (
            master
            - LEARN_RATE
            * trust_all[group_at].reshape((LAYERS,) + (1,) * (master.ndim - 1))
            * moved_one[1]
            for group_at, (master, moved_one) in enumerate(zip(masters, moved))
        )
    )
    return (
        own_in,
        logits_out,
        d_own,
        grad_logits,
        grads_all[0],
        grads_all[1],
        grads_all[2],
        grads_all[3],
        grads_all[4],
        grads_all[5],
        new_params[0],
        new_params[1],
        new_params[2],
        new_params[3],
        new_params[4],
        new_params[5],
        moved[0][0],
        moved[1][0],
        moved[2][0],
        moved[3][0],
        moved[4][0],
        moved[5][0],
        trust_all.T,
    )


def solution(mesh):
    return jax.shard_map(
        shards,
        mesh=mesh,
        in_specs=(
            P("dp", None),
            P("dp", "tensor", None, None),
            P(("dp", "tensor"), None),
            P("dp"),
            P("dp"),
            P("dp"),
            P(None, None, "dp", "tensor"),
            P(None, "tensor", "dp"),
            P(None, "dp", "tensor"),
            P(None, "tensor", "dp"),
            P(None, None, ("dp", "tensor")),
            P(None, ("dp", "tensor")),
            P(None, None, "dp", "tensor"),
            P(None, "tensor", "dp"),
            P(None, "dp", "tensor"),
            P(None, "tensor", "dp"),
            P(None, None, ("dp", "tensor")),
            P(None, ("dp", "tensor")),
            P(None, None, "dp", "tensor"),
            P(None, "tensor", "dp"),
            P(None, "dp", "tensor"),
            P(None, "tensor", "dp"),
            P(None, None, ("dp", "tensor")),
            P(None, ("dp", "tensor")),
        ),
        out_specs=(
            P(("dp", "tensor"), None),
            P("dp", "tensor", None, None),
            P(("dp", "tensor"), None),
            P("dp", "tensor", None, None),
            P(None, None, "dp", "tensor"),
            P(None, "tensor", "dp"),
            P(None, "dp", "tensor"),
            P(None, "tensor", "dp"),
            P(None, None, ("dp", "tensor")),
            P(None, ("dp", "tensor")),
            P(None, None, "dp", "tensor"),
            P(None, "tensor", "dp"),
            P(None, "dp", "tensor"),
            P(None, "tensor", "dp"),
            P(None, None, ("dp", "tensor")),
            P(None, ("dp", "tensor")),
            P(None, None, "dp", "tensor"),
            P(None, "tensor", "dp"),
            P(None, "dp", "tensor"),
            P(None, "tensor", "dp"),
            P(None, None, ("dp", "tensor")),
            P(None, ("dp", "tensor")),
            P(),
        ),
        check_vma=False,
    )
```

profile of v0, /device:TPU:0, one launch (start us, length us, event | category | flops | bytes accessed | tf_op | source)
XLA Modules:
  0.0 1485.0 jit_solution(5706030259028779352)
XLA Ops:
  14.7 46.1 %all_gather.60 = bf16[2,8,1024]{1,0,2:T(2,128)(2,1)S(1)} all-gather(bf16[2,8,32]{1,0,2:T(2,128)(2,1)S(1)} %copy.122), channel_id=1, replica_groups=mesh['dp'=8,'tensor'=4] {'dp','tensor'}, dimensions={2}, use_global_device_ids=true | all-gather | bytes 33792 | tf_op jit(solution)/shard_map/all_gather | solution.py:80
  66.0 27.7 %all-gather.1 = bf16[1,256,1024]{2,1,0:T(8,128)(2,1)S(1)} all-gather(bf16[1,256,128]{2,1,0:T(8,128)(2,1)S(1)} %get-tuple-element.378), channel_id=3, replica_groups=mesh['dp'=8,'tensor'=4] {'dp'}, dimensions={2}, use_global_device_ids=true | all-gather | bytes 589824 | tf_op jit(solution)/shard_map/all_gather | solution.py:183
  107.2 45.8 %slice_reduce_fusion.2 = (f32[1024]{0:T(1024)S(1)}, f32[1024]{0:T(1024)S(1)}, f32[1024]{0:T(1024)S(1)}, f32[1024]{0:T(1024)S(1)}, f32[1024]{0:T(1024)S(1)}, /*in...) fusion(f32[2,8,1024]{1,0,2:T(2,128)S(1)} %convert_element_type.391), kind=kLoop, calls=%fused_computation.183 | loop fusion | bytes 98304 | tf_op jit(solution)/shard_map/slice | solution.py:231
  159.6 36.6 %all_gather.64 = bf16[2,4096]{1,0:T(2,128)(2,1)S(1)} all-gather(bf16[2,128]{1,0:T(2,128)(2,1)S(1)} %get-tuple-element.384), channel_id=1, replica_groups=mesh['dp'=8,'tensor'=4] {'dp','tensor'}, dimensions={1}, use_global_device_ids=true | all-gather | bytes 16896 | tf_op jit(solution)/shard_map/all_gather | solution.py:81
  204.8 45.2 %all-gather.40.cloned.1.call-done = bf16[1,1024,1024]{2,1,0:T(8,128)(2,1)} async-done(((bf16[1,1024,128]{2,1,0:T(8,128)(2,1)}), bf16[1,1024,1024]{2,1,0:T(8,128)(2,1)}) %all-gather.40.cloned.1.call-update) | async-done | bytes 2097168 | tf_op jit(solution)/shard_map/all_gather | solution.py:185
  254.7 22.4 %reduce-scatter.17.cloned.1.call-done = bf16[128,1024]{1,0:T(8,128)(2,1)} async-done(((bf16[512,1024]{1,0:T(8,128)(2,1)}), bf16[128,1024]{1,0:T(8,128)(2,1)}) %reduce-scatter.17.cloned.1.call-update) | async-done | bytes 262160 | tf_op jit(solution)/shard_map/reduce_scatter | solution.py:87
  283.3 29.1 %all-gather.5 = bf16[1,256,1024]{2,1,0:T(8,128)(2,1)S(1)} all-gather(bf16[1,256,128]{2,1,0:T(8,128)(2,1)S(1)} %get-tuple-element.377), channel_id=7, replica_groups=mesh['dp'=8,'tensor'=4] {'dp'}, dimensions={2}, use_global_device_ids=true | all-gather | bytes 589824 | tf_op jit(solution)/shard_map/all_gather | solution.py:183
  312.4 14.2 all-gather.42.cloned.1.call-done
  326.6 17.6 %all-gather.24.cloned.1.call-done = bf16[512,1024]{1,0:T(8,128)(2,1)} async-done(((bf16[128,1024]{1,0:T(8,128)(2,1)}), bf16[512,1024]{1,0:T(8,128)(2,1)}) %all-gather.24.cloned.1.call-update) | async-done | bytes 1048592 | tf_op jit(solution)/shard_map/all_gather | solution.py:103
  357.8 24.4 %reduce-scatter.19.cloned.1.call-done = bf16[128,1024]{1,0:T(8,128)(2,1)} async-done(((bf16[512,1024]{1,0:T(8,128)(2,1)}), bf16[128,1024]{1,0:T(8,128)(2,1)}) %reduce-scatter.19.cloned.1.call-update) | async-done | bytes 262160 | tf_op jit(solution)/shard_map/reduce_scatter | solution.py:87
  387.5 46.8 %all-gather.44.cloned.1.call-done = bf16[1,1024,1024]{2,1,0:T(8,128)(2,1)} async-done(((bf16[1,128,1024]{2,1,0:T(8,128)(2,1)}), bf16[1,1024,1024]{2,1,0:T(8,128)(2,1)}) %all-gather.44.cloned.1.call-update) | async-done | bytes 2097168 | tf_op jit(solution)/shard_map/all_gather | solution.py:184
  434.3 17.5 %all-gather.26.cloned.1.call-done = bf16[512,1024]{1,0:T(8,128)(2,1)} async-done(((bf16[128,1024]{1,0:T(8,128)(2,1)}), bf16[512,1024]{1,0:T(8,128)(2,1)}) %all-gather.26.cloned.1.call-update) | async-done | bytes 1048592 | tf_op jit(solution)/shard_map/all_gather | solution.py:103
  460.4 45.2 %all-gather.46.cloned.1.call-done = bf16[1,1024,1024]{2,1,0:T(8,128)(2,1)} async-done(((bf16[1,1024,128]{2,1,0:T(8,128)(2,1)}), bf16[1,1024,1024]{2,1,0:T(8,128)(2,1)}) %all-gather.46.cloned.1.call-update) | async-done | bytes 2097168 | tf_op jit(solution)/shard_map/all_gather | solution.py:185
  509.5 23.2 %reduce-scatter.21.cloned.1.call-done = bf16[128,1024]{1,0:T(8,128)(2,1)} async-done(((bf16[512,1024]{1,0:T(8,128)(2,1)}), bf16[128,1024]{1,0:T(8,128)(2,1)}) %reduce-scatter.21.cloned.1.call-update) | async-done | bytes 262160 | tf_op jit(solution)/shard_map/reduce_scatter | solution.py:87
  539.1 16.8 %all-gather.28.cloned.1.call-done = bf16[512,1024]{1,0:T(8,128)(2,1)} async-done(((bf16[128,1024]{1,0:T(8,128)(2,1)}), bf16[512,1024]{1,0:T(8,128)(2,1)}) %all-gather.28.cloned.1.call-update) | async-done | bytes 1048592 | tf_op jit(solution)/shard_map/all_gather | solution.py:106
  564.5 25.0 %reduce-scatter.23.cloned.1.call-done = bf16[128,1024]{1,0:T(8,128)(2,1)} async-done(((bf16[512,1024]{1,0:T(8,128)(2,1)}), bf16[128,1024]{1,0:T(8,128)(2,1)}) %reduce-scatter.23.cloned.1.call-update) | async-done | bytes 262160 | tf_op jit(solution)/shard_map/reduce_scatter | solution.py:95
  593.3 16.7 %all-gather.30.cloned.1.call-done = bf16[512,1024]{1,0:T(8,128)(2,1)} async-done(((bf16[128,1024]{1,0:T(8,128)(2,1)}), bf16[512,1024]{1,0:T(8,128)(2,1)}) %all-gather.30.cloned.1.call-update) | async-done | bytes 1048592 | tf_op jit(solution)/shard_map/all_gather | solution.py:106
  621.2 25.0 %reduce-scatter.25.cloned.1.call-done = bf16[128,1024]{1,0:T(8,128)(2,1)} async-done(((bf16[512,1024]{1,0:T(8,128)(2,1)}), bf16[128,1024]{1,0:T(8,128)(2,1)}) %reduce-scatter.25.cloned.1.call-update) | async-done | bytes 262160 | tf_op jit(solution)/shard_map/reduce_scatter | solution.py:95
  651.1 16.8 %all-gather.32.cloned.1.call-done = bf16[512,1024]{1,0:T(8,128)(2,1)} async-done(((bf16[128,1024]{1,0:T(8,128)(2,1)}), bf16[512,1024]{1,0:T(8,128)(2,1)}) %all-gather.32.cloned.1.call-update) | async-done | bytes 1048592 | tf_op jit(solution)/shard_map/all_gather | solution.py:106
  683.7 17.7 %reduce-scatter.27.cloned.1.call-done = bf16[128,1024]{1,0:T(8,128)(2,1)} async-done(((bf16[512,1024]{1,0:T(8,128)(2,1)}), bf16[128,1024]{1,0:T(8,128)(2,1)}) %reduce-scatter.27.cloned.1.call-update) | async-done | bytes 262160 | tf_op jit(solution)/shard_map/reduce_scatter | solution.py:95
  754.1 108.1 %reduce-scatter.33.cloned.1.call-done = f32[128,2]{1,0:T(8,128)} async-done(((f32[4096,2]{1,0:T(8,128)}), f32[128,2]{1,0:T(8,128)}) %reduce-scatter.33.cloned.1.call-update) | async-done | bytes 1040
  872.6 121.9 %reduce-scatter.31.cloned.1.call-done = f32[32,16]{1,0:T(8,128)} async-done(((f32[1024,16]{1,0:T(8,128)}), f32[32,16]{1,0:T(8,128)}) %reduce-scatter.31.cloned.1.call-update) | async-done | bytes 2064
  996.2 407.0 %all-reduce.4.cloned.1.call-done = (bf16[3,1024,256]{2,1,0:T(8,128)(2,1)}, bf16[3,1024,256]{1,2,0:T(8,128)(2,1)}, bf16[256,1024]{1,0:T(8,128)(2,1)}, bf16[256,10...) async-done(((bf16[3,1024,256]{2,1,0:T(8,128)(2,1)}, ...) | async-done | bytes 12582928 | tf_op jit(solution)/shard_map/psum | solution.py:375
  1431.5 39.3 %all-reduce = (f32[6,2]{0,1:T(2,128)S(1)}, f32[6,2]{0,1:T(2,128)S(1)}) all-reduce(f32[6,2]{0,1:T(2,128)S(1)} %stack.221, f32[6,2]{0,1:T(2,128)S(1)} %stack.214), channel_id=1, replica_groups=mesh['dp'=8,'tensor'=4] {'dp','tensor'}, use_global_device_ids=true, to_apply=%region_71.72 | all-reduce | flops 24 | bytes 192 | tf_op jit(solution)/shard_map/psum | solution.py:428
  (427 shorter events, 231.5 us)
Async XLA Ops:
  7.2 86.7 %all-gather.36.cloned.1.call-start = ((), (), s32[]{:S(2)}) async-start(), calls=%async_computation.25 | async-start | bytes 1769472 | tf_op jit(solution)/shard_map/all_gather | solution.py:182
  10.3 142.7 %reduce-scatter.15.cloned.1.call-start = ((), (), s32[]{:S(2)}) async-start(), calls=%async_computation.10 | async-start | bytes 1310720 | tf_op jit(solution)/shard_map/reduce_scatter | solution.py:87
  105.4 90.9 %all-gather.38.cloned.1.call-start = ((), (), s32[]{:S(2)}) async-start(), calls=%async_computation.26 | async-start | bytes 2359296 | tf_op jit(solution)/shard_map/all_gather | solution.py:184
  106.5 89.8 %all-gather.22.cloned.1.call-start = ((), (), s32[]{:S(2)}) async-start(), calls=%async_computation.11 | async-start | bytes 1310720 | tf_op jit(solution)/shard_map/all_gather | solution.py:103
  157.3 92.7 %all-gather.40.cloned.1.call-start = ((), (), s32[]{:S(2)}) async-start(), calls=%async_computation.27 | async-start | bytes 2359296 | tf_op jit(solution)/shard_map/all_gather | solution.py:185
  158.9 118.2 %reduce-scatter.17.cloned.1.call-start = ((), (), s32[]{:S(2)}) async-start(), calls=%async_computation.12 | async-start | bytes 1310720 | tf_op jit(solution)/shard_map/reduce_scatter | solution.py:87
  253.9 72.7 %all-gather.42.cloned.1.call-start = ((), (), s32[]{:S(2)}) async-start(), calls=%async_computation.28 | async-start | bytes 1769472 | tf_op jit(solution)/shard_map/all_gather | solution.py:182
  254.6 89.5 %all-gather.24.cloned.1.call-start = ((), (), s32[]{:S(2)}) async-start(), calls=%async_computation.13 | async-start | bytes 1310720 | tf_op jit(solution)/shard_map/all_gather | solution.py:103
  281.3 101.0 %reduce-scatter.19.cloned.1.call-start = ((), (), s32[]{:S(2)}) async-start(), calls=%async_computation.14 | async-start | bytes 1310720 | tf_op jit(solution)/shard_map/reduce_scatter | solution.py:87
  357.2 77.1 %all-gather.44.cloned.1.call-start = ((), (), s32[]{:S(2)}) async-start(), calls=%async_computation.29 | async-start | bytes 2359296 | tf_op jit(solution)/shard_map/all_gather | solution.py:184
  357.8 94.0 %all-gather.26.cloned.1.call-start = ((), (), s32[]{:S(2)}) async-start(), calls=%async_computation.15 | async-start | bytes 1310720 | tf_op jit(solution)/shard_map/all_gather | solution.py:103
  386.4 119.2 %all-gather.46.cloned.1.call-start = ((), (), s32[]{:S(2)}) async-start(), calls=%async_computation.30 | async-start | bytes 2359296 | tf_op jit(solution)/shard_map/all_gather | solution.py:185
  386.9 145.7 %reduce-scatter.21.cloned.1.call-start = ((), (), s32[]{:S(2)}) async-start(), calls=%async_computation.16 | async-start | bytes 1310720 | tf_op jit(solution)/shard_map/reduce_scatter | solution.py:87
  509.4 46.5 %all-gather.28.cloned.1.call-start = ((), (), s32[]{:S(2)}) async-start(), calls=%async_computation.17 | async-start | bytes 1310720 | tf_op jit(solution)/shard_map/all_gather | solution.py:106
  539.1 50.4 %reduce-scatter.23.cloned.1.call-start = ((), (), s32[]{:S(2)}) async-start(), calls=%async_computation.18 | async-start | bytes 1310720 | tf_op jit(solution)/shard_map/reduce_scatter | solution.py:95
  564.5 45.5 %all-gather.30.cloned.1.call-start = ((), (), s32[]{:S(2)}) async-start(), calls=%async_computation.19 | async-start | bytes 1310720 | tf_op jit(solution)/shard_map/all_gather | solution.py:106
  593.1 53.2 %reduce-scatter.25.cloned.1.call-start = ((), (), s32[]{:S(2)}) async-start(), calls=%async_computation.20 | async-start | bytes 1310720 | tf_op jit(solution)/shard_map/reduce_scatter | solution.py:95
  621.2 46.7 %all-gather.32.cloned.1.call-start = ((), (), s32[]{:S(2)}) async-start(), calls=%async_computation.21 | async-start | bytes 1310720 | tf_op jit(solution)/shard_map/all_gather | solution.py:106
  651.0 50.4 %reduce-scatter.27.cloned.1.call-start = ((), (), s32[]{:S(2)}) async-start(), calls=%async_computation.22 | async-start | bytes 1310720 | tf_op jit(solution)/shard_map/reduce_scatter | solution.py:95
  676.4 46.5 %all-gather.34.cloned.1.call-start = ((), (), s32[]{:S(2)}) async-start(), calls=%async_computation.23 | async-start | bytes 1310720 | tf_op jit(solution)/shard_map/all_gather | solution.py:106
  706.1 156.1 %reduce-scatter.33.cloned.1.call-start = ((), (), s32[]{:S(2)}) async-start(), calls=%async_computation.32 | async-start | bytes 2162688
  715.4 279.2 %reduce-scatter.31.cloned.1.call-start = ((), (), s32[]{:S(2)}) async-start(), calls=%async_computation.31 | async-start | bytes 540672
  744.0 659.2 %all-reduce.4.cloned.1.call-start = ((), (), s32[]{:S(2)}) async-start(), calls=%async_computation.33 | async-start | bytes 25165824 | tf_op jit(solution)/shard_map/psum | solution.py:375
  747.9 681.7 %reduce-scatter.29.cloned.1.call-start = ((), (), s32[]{:S(2)}) async-start(), calls=%async_computation.24 | async-start | bytes 1310720 | tf_op jit(solution)/shard_map/reduce_scatter | solution.py:95
  (95 other events, 3432.9 us)
Sparse Core Ops, SparseCore 0:
  10.8 47.0 all-gather.35
  105.5 21.0 reduce-scatter.14
  129.5 49.3 all-gather.37
  181.0 15.2 all-gather.21
  198.9 51.0 all-gather.39
  254.0 23.0 reduce-scatter.16
  279.9 46.6 all-gather.41
  328.7 15.3 all-gather.23
  357.3 24.8 reduce-scatter.18
  385.0 49.2 all-gather.43
  436.5 15.2 all-gather.25
  454.4 51.0 all-gather.45
  509.6 23.0 reduce-scatter.20
  539.2 16.7 all-gather.27
  564.6 24.8 reduce-scatter.22
  593.2 16.7 all-gather.29
  621.3 24.8 reduce-scatter.24
  651.2 16.7 all-gather.31
  676.6 24.8 reduce-scatter.26
  706.2 16.7 all-gather.33
  725.4 136.7 reduce-scatter.32
  865.0 129.5 reduce-scatter.30
  1002.3 400.8 all-reduce.3
  1406.1 23.4 reduce-scatter.28
where the time goes:
time: 1490 us
  waiting for transfers between devices  1020 us (68%)
  blocking collectives  179 us (12%)
  matrix products  110 us (7%)
  local copies, waits for them, and re-layouts  80.4 us (5%)
  other arithmetic  76 us (5%)
  between operations  17.4 us (1%)
    psum x1, waiting for transfers between devices, shards(): lax.psum(mats[0].astype(jnp.bfloat16), 'dp').astype(jnp.float32)  407 us
    unnamed x26, waiting for transfers between devices  232 us
    all_gather x2, waiting for transfers between devices, shards(): lax.all_gather(w_back[layer_at].astype(jnp.bfloat16), 'dp', axis=1, tiled...  90.4 us
    reduce_scatter x4, waiting for transfers between devices, sum_backward(): lax.psum_scatter(term_fn(jnp.int32(0), share_rows * lax.axis_size('tensor...  73.6 us
    reduce_scatter x4, waiting for transfers between devices, sum_forward(): lax.psum_scatter(term_fn(jnp.int32(0), share_rows * lax.axis_size('tensor...  70.1 us
    all_gather x2, blocking collectives, shards(): lax.all_gather(w_out[layer_at].astype(jnp.bfloat16), 'dp', axis=1, tiled=...  56.8 us
    all_gather x4, waiting for transfers between devices, gather_grads(): return lax.all_gather(own_rows, 'tensor', axis=0, tiled=True)  50.9 us
    all_gather x2, waiting for transfers between devices, shards(): lax.all_gather(w_in[layer_at].astype(jnp.bfloat16), 'dp', axis=0, tiled=T...  46.9 us
  transfers between devices with their start and end apart: 24, of which 20 were waited for; matrix products, arithmetic and copies ran while one was open for 12% of the time, Pallas kernels for 0%

commit v1 on v0

--- a/solution.py
+++ b/solution.py
@@ -1,6 +1,10 @@
+import functools
+
 import jax
 import jax.numpy as jnp
 from jax import lax
+from jax.experimental import pallas as pl
+from jax.experimental.pallas import tpu as pltpu
 from jax.sharding import PartitionSpec as P
 
 LAYERS = 2
@@ -27,7 +31,7 @@
     return jax.nn.gelu(values, approximate=False)
 
 
-def shards(
+def plain_shards(
     hidden_in,
     logits_in,
     cotangent,
@@ -463,9 +467,1070 @@
     )
 
 
+MESH = pl.DeviceIdType.MESH
+TILE = 256
+LANES = 128
+ROWS_MAT = 4
+
+
+def dot_nn(left, right):
+    return lax.dot_general(
+        left, right, (((1,), (0,)), ((), ())), preferred_element_type=jnp.float32
+    )
+
+
+def dot_nt(left, right):
+    return lax.dot_general(
+        left, right, (((1,), (1,)), ((), ())), preferred_element_type=jnp.float32
+    )
+
+
+def norm_parts(values):
+    center = values - jnp.mean(values, axis=-1, keepdims=True)
+    spread = jnp.mean(center * center, axis=-1, keepdims=True)
+    return center, lax.rsqrt(spread + NORM_EPS)
+
+
+def step_kernel(
+    data_parts,
+    hidden_in,
+    logits_in,
+    cotangent,
+    row_ids,
+    key_ids,
+    small_in,
+    own_qkv,
+    own_out,
+    own_in,
+    own_back,
+    hidden_out,
+    logits_out,
+    grad_hidden,
+    grad_scores,
+    sum_qkv,
+    sum_out,
+    sum_in,
+    sum_back,
+    small_out,
+    w_q,
+    w_o,
+    w_i,
+    w_b,
+    scores,
+    probs,
+    h_full,
+    m_full,
+    active,
+    attn,
+    h_turn,
+    m_turn,
+    g_turn,
+    o_turn,
+    slope,
+    qkv,
+    x_own,
+    y_own,
+    d_qkv,
+    d_attn,
+    d_own,
+    d_keep,
+    turn_v,
+    turn_k,
+    part,
+    got_core,
+    sum_chip,
+    got_y,
+    vec_got,
+    vec_all,
+    bin_all,
+    small_acc,
+    small_got,
+    small_send,
+    small_sum,
+    pk_q,
+    pk_o,
+    pk_i,
+    pk_b,
+    rx_q,
+    rx_o,
+    rx_i,
+    rx_b,
+    rz_q,
+    rz_o,
+    rz_i,
+    rz_b,
+    fin_q,
+    fin_o,
+    fin_i,
+    fin_b,
+    load_sem,
+    own_sem,
+    zs_sem,
+    zr_sem,
+    xs_sem,
+    xr_sem,
+    core_s,
+    core_r,
+    ys_sem,
+    yr_sem,
+    gat_s,
+    gat_r,
+    vec_s,
+    vec_r,
+    sml_s,
+    sml_r,
+    gxs_sem,
+    gxr_sem,
+    gzs_sem,
+    gzr_sem,
+    fin_sem,
+    out_sem,
+):
+    dp = lax.axis_index("dp")
+    ten = lax.axis_index("tensor")
+    cols_n = data_parts // 2
+    side = lax.rem(dp, 2)
+    place = dp // 2
+    row_y = ten // 2
+    core = lax.rem(ten, 2)
+    across = dp + 1 - 2 * side
+    core_mate = ten + 1 - 2 * core
+    y_mate = lax.rem(ten + 2, 4)
+    width = hidden_in.shape[1]
+    tokens = hidden_in.shape[0]
+    share = tokens // 4
+    half = share // 2
+    head_cols = qkv.shape[3]
+    hidden_cols = slope.shape[2]
+    cut = width // data_parts
+    tiles = width // TILE
+    f32 = jnp.float32
+    b16 = jnp.bfloat16
+
+    def along(step):
+        return lax.rem(place + step, cols_n) * 2 + side
+
+    def mult(value, by):
+        return pl.multiple_of(value, by)
+
+    def rdma(src, dst, send, recv, to_dp, to_ten):
+        return pltpu.make_async_remote_copy(
+            src_ref=src,
+            dst_ref=dst,
+            send_sem=send,
+            recv_sem=recv,
+            device_id=(to_dp, to_ten),
+            device_id_type=MESH,
+        )
+
+    def region(kind, layer, dev):
+        at = pl.ds(mult(dev * cut, cut), cut)
+        if kind == 0:
+            return w_q.at[layer, :, at, :]
+        if kind == 1:
+            return w_o.at[layer, :, at]
+        if kind == 2:
+            return w_i.at[layer, at, :]
+        return w_b.at[layer, :, at]
+
+    owns = (own_qkv, own_out, own_in, own_back)
+
+    load_h = pltpu.make_async_copy(hidden_in, h_full, load_sem.at[0])
+    load_s = pltpu.make_async_copy(logits_in.at[0], scores, load_sem.at[1])
+    load_h.start()
+    load_s.start()
+    own_loads = []
+    for layer in range(LAYERS):
+        for kind in range(ROWS_MAT):
+            copy = pltpu.make_async_copy(
+                owns[kind].at[layer], region(kind, layer, dp), own_sem.at[layer, kind]
+            )
+            copy.start()
+            own_loads.append(copy)
+
+    barrier = pltpu.get_barrier_semaphore()
+
+    def greet(step, carry):
+        pl.semaphore_signal(
+            barrier, inc=1, device_id=(lax.rem(dp + step, data_parts), ten), device_id_type=MESH
+        )
+        return carry
+
+    lax.fori_loop(1, data_parts, greet, 0)
+    for other in range(1, 4):
+        pl.semaphore_signal(
+            barrier, inc=1, device_id=(dp, lax.rem(ten + other, 4)), device_id_type=MESH
+        )
+    pl.semaphore_wait(barrier, data_parts + 2)
+
+    vec_got[ten, dp] = small_in[...]
+
+    def vec_one(step):
+        return rdma(
+            small_in,
+            vec_got.at[ten, dp],
+            vec_s.at[step - 1],
+            vec_r.at[step - 1],
+            lax.rem(dp + step, data_parts),
+            ten,
+        )
+
+    def vec_go(step, carry):
+        vec_one(step).start()
+        return carry
+
+    lax.fori_loop(1, data_parts, vec_go, 0)
+
+    def w_z(kind, layer, step):
+        return rdma(
+            owns[kind].at[layer],
+            region(kind, layer, dp),
+            zs_sem.at[layer, kind, step - 1],
+            zr_sem.at[layer, kind, step - 1],
+            along(step),
+            ten,
+        )
+
+    def w_x_own(kind, layer):
+        return rdma(
+            owns[kind].at[layer],
+            region(kind, layer, dp),
+            xs_sem.at[layer, kind, 0],
+            xr_sem.at[layer, kind, 0],
+            across,
+            ten,
+        )
+
+    def w_x_pass(kind, layer, step):
+        came = region(kind, layer, along(cols_n - step))
+        return rdma(
+            came,
+            came,
+            xs_sem.at[layer, kind, step],
+            xr_sem.at[layer, kind, step],
+            across,
+            ten,
+        )
+
+    order = [(kind, layer) for layer in range(LAYERS) for kind in range(ROWS_MAT)]
+    for kind, layer in order:
+        for step in range(1, cols_n):
+            w_z(kind, layer, step).start()
+        if (kind, layer) in order[:2]:
+            w_x_own(kind, layer).start()
+
+    def pass_on(index):
+        if index >= len(order):
+            return
+        kind, layer = order[index]
+        for step in range(1, cols_n):
+            w_z(kind, layer, step).wait_recv()
+            w_x_pass(kind, layer, step).start()
+        if index + 2 < len(order):
+            w_x_own(*order[index + 2]).start()
+
+    def have(index):
+        kind, layer = order[index]
+        w_x_own(kind, layer).wait_recv()
+        for step in range(1, cols_n):
+            w_x_pass(kind, layer, step).wait_recv()
+
+    def vec_wait(step, carry):
+        vec_one(step).wait_send()
+        vec_one(step).wait_recv()
+        return carry
+
+    lax.fori_loop(1, data_parts, vec_wait, 0)
+
+    def vec_two(step):
+        return rdma(
+            vec_got.at[ten],
+            vec_got.at[ten],
+            vec_s.at[data_parts - 2 + step],
+            vec_r.at[data_parts - 2 + step],
+            dp,
+            lax.rem(ten + step, 4),
+        )
+
+    for step in range(1, 4):
+        vec_two(step).start()
+    for step in range(1, 4):
+        vec_two(step).wait_send()
+        vec_two(step).wait_recv()
+    for dev in range(data_parts):
+        total = vec_got[0, dev].astype(f32)
+        for other in range(1, 4):
+            total = total + vec_got[other, dev].astype(f32)
+        vec_all[:, dev * LANES : (dev + 1) * LANES] = total[0 : LAYERS * 8]
+    for piece in range(hidden_cols // LANES):
+        got = vec_got[piece % 4, ten * 2 + piece // 4].astype(f32)
+        bin_all[:, piece * LANES : (piece + 1) * LANES] = got[LAYERS * 8 : LAYERS * 8 + 8]
+
+    def vec_row(layer, row):
+        return vec_all[layer * 8 + row : layer * 8 + row + 1, :]
+
+    def block_rows(which_y, which_core):
+        return pl.ds(mult((which_y * 2 + which_core) * share, share), share)
+
+    far_block = block_rows(1 - row_y, 1 - core)
+    mate_block = block_rows(row_y, 1 - core)
+    over_block = block_rows(1 - row_y, core)
+    own_block = block_rows(row_y, core)
+
+    def tile_cols(tile):
+        return pl.ds(mult(tile * TILE, TILE), TILE)
+
+    def send_core(tile, which):
+        rows = far_block if which == 0 else mate_block
+        return rdma(
+            part.at[rows, tile_cols(tile)],
+            got_core.at[which, :, tile_cols(tile)],
+            core_s.at[tile, which],
+            core_r.at[tile, which],
+            dp,
+            core_mate,
+        )
+
+    def send_y(tile):
+        return rdma(
+            sum_chip.at[:, tile_cols(tile)],
+            got_y.at[:, tile_cols(tile)],
+            ys_sem.at[tile],
+            yr_sem.at[tile],
+            dp,
+            y_mate,
+        )
+
+    def add_core(tile):
+        send_core(tile, 0).wait_recv()
+        at = tile_cols(tile)
+        sum_chip[:, at] = (
+            part[over_block, at].astype(f32) + got_core[0, :, at].astype(f32)
+        ).astype(b16)
+        send_y(tile).start()
+
+    def sum_start(tile_fn):
+        def one(tile, carry):
+            part[:, tile_cols(tile)] = tile_fn(tile).astype(b16)
+            send_core(tile, 0).start()
+            send_core(tile, 1).start()
+
+            @pl.when(tile > 0)
+            def _():
+                add_core(tile - 1)
+
+            return carry
+
+        lax.fori_loop(0, tiles, one, 0)
+        add_core(tiles - 1)
+
+    def sum_end():
+        for tile in range(tiles):
+            send_core(tile, 1).wait_recv()
+            send_y(tile).wait_recv()
+        for tile in range(tiles):
+            send_core(tile, 0).wait_send()
+            send_core(tile, 1).wait_send()
+            send_y(tile).wait_send()
+
+    def sum_rows(which):
+        at = pl.ds(which * half, half)
+        mine = pl.ds(mult(ten * share + which * half, half), half)
+        return (
+            part[mine, :].astype(f32) + got_core[1, at, :].astype(f32) + got_y[at, :].astype(f32)
+        )
+
+    def gat_copy(buf, which, kind):
+        if kind == 2:
+            rows = pl.ds(mult(y_mate * share + which * half, half), half)
+        else:
+            rows = pl.ds(mult(ten * share + which * half, half), half)
+        return rdma(
+            buf.at[rows],
+            buf.at[rows],
+            gat_s.at[which, kind],
+            gat_r.at[which, kind],
+            dp,
+            y_mate if kind == 1 else core_mate,
+        )
+
+    def gat_start(buf, which):
+        gat_copy(buf, which, 1).start()
+        gat_copy(buf, which, 0).start()
+
+    def gat_end(buf):
+        for which in range(2):
+            gat_copy(buf, which, 1).wait_recv()
+            gat_copy(buf, which, 2).start()
+        for which in range(2):
+            gat_copy(buf, which, 0).wait_recv()
+            gat_copy(buf, which, 2).wait_recv()
+        for which in range(2):
+            for kind in range(3):
+                gat_copy(buf, which, kind).wait_send()
+
+    def own_rows(which):
+        return pl.ds(mult(ten * share + which * half, half), half)
+
+    def turn(src, dst, layer):
+        def one(at, carry):
+            dst[layer, tile_cols(at), :] = src[:, tile_cols(at)].T
+            return carry
+
+        lax.fori_loop(0, src.shape[1] // TILE, one, 0)
+
+    lane = lax.broadcasted_iota(jnp.int32, (1, LANES), 1)
+    low_lanes = jnp.where(lane < 64, 1.0, 0.0).astype(b16)
+    high_lanes = jnp.where(lane < 64, 0.0, 1.0).astype(b16)
+    lane_masks = (low_lanes, high_lanes)
+    scale = 0.125
+    score_rows = 256
+    pairs = head_cols // LANES
+
+    def pair_cols(pair):
+        return pl.ds(mult(pair * LANES, LANES), LANES)
+
+    def attend(layer):
+        def one(step, carry):
+            pair = step // (tokens // score_rows)
+            rows = pl.ds(
+                mult(lax.rem(step, tokens // score_rows) * score_rows, score_rows), score_rows
+            )
+            at = pair_cols(pair)
+            queries = qkv[layer, 0, rows, at]
+            keys = qkv[layer, 1, :, at]
+            values = qkv[layer, 2, :, at]
+            allowed = row_ids[rows, 0:1] == key_ids[0:1, :]
+            mixed = jnp.zeros((score_rows, LANES), f32)
+            for head in range(2):
+                raw = dot_nt(queries, keys * lane_masks[head])
+                full = raw * scale + scores[pair * 2 + head, rows, :].astype(f32)
+                scores[pair * 2 + head, rows, :] = full.astype(b16)
+                top = jnp.max(jnp.where(allowed, full, NEG_FILL), axis=-1, keepdims=True)
+                weight = jnp.exp(jnp.where(allowed, full - top, NEG_FILL))
+                total = jnp.sum(weight, axis=-1, keepdims=True)
+                total = jnp.where(total > 0.5, total, 1.0)
+                low = (weight * (1.0 / total)).astype(b16)
+                probs[layer, pair * 2 + head, rows, :] = low
+                mixed = mixed + dot_nn(low, values * lane_masks[head])
+            attn[rows, at] = mixed.astype(b16)
+            return carry
+
+        lax.fori_loop(0, pairs * (tokens // score_rows), one, 0)
+
+    def attend_back(layer, first):
+        def pair_one(pair, carry):
+            at = pair_cols(pair)
+            turn_v[...] = jnp.zeros_like(turn_v)
+            turn_k[...] = jnp.zeros_like(turn_k)
+
+            def one(step, inner):
+                rows = pl.ds(mult(step * score_rows, score_rows), score_rows)
+                queries = qkv[layer, 0, rows, at]
+                keys = qkv[layer, 1, :, at]
+                values = qkv[layer, 2, :, at]
+                grads = d_attn[rows, at]
+                turned_q = queries.T
+                turned_g = grads.T
+                d_query = jnp.zeros((score_rows, LANES), f32)
+                for head in range(2):
+                    low = probs[layer, pair * 2 + head, rows, :]
+                    prob = low.astype(f32)
+                    d_prob = dot_nt(grads, values * lane_masks[head])
+                    inner_sum = jnp.sum(prob * d_prob, axis=-1, keepdims=True)
+                    d_score = prob * (d_prob - inner_sum)
+                    if not first:
+                        d_score = d_score + scores[pair * 2 + head, rows, :].astype(f32)
+                    d_low = d_score.astype(b16)
+                    scores[pair * 2 + head, rows, :] = d_low
+                    d_query = d_query + dot_nn(d_low, keys * lane_masks[head])
+                    part_rows = slice(head * 64, head * 64 + 64)
+                    turn_v[part_rows, :] += dot_nn(turned_g[part_rows, :], low)
+                    turn_k[part_rows, :] += dot_nn(turned_q[part_rows, :], d_low)
+                d_qkv[0, rows, at] = (d_query * scale).astype(b16)
+                return inner
+
+            lax.fori_loop(0, tokens // score_rows, one, 0)
+            d_qkv[1, :, at] = (turn_k[...] * scale).T.astype(b16)
+            d_qkv[2, :, at] = turn_v[...].T.astype(b16)
+            return carry
+
+        lax.fori_loop(0, pairs, pair_one, 0)
+
+    own_cols = pl.ds(mult(ten * head_cols, head_cols), head_cols)
+    small_acc[...] = jnp.zeros_like(small_acc)
+    load_h.wait()
+    for copy in own_loads:
+        copy.wait()
+    load_s.wait()
+    for layer in range(LAYERS):
+        base = layer * ROWS_MAT
+        if layer == 0:
+            pass_on(0)
+        have(base)
+        for which in range(3):
+            product = dot_nn(h_full[...], w_q[layer, which])
+            if which == 0:
+                product = product + vec_all[layer * 8 + 2 : layer * 8 + 3, own_cols]
+            if which == 2:
+                product = product + vec_all[layer * 8 + 3 : layer * 8 + 4, own_cols]
+            qkv[layer, which] = product.astype(b16)
+        pass_on(base + 1)
+        attend(layer)
+        have(base + 1)
+
+        sum_start(lambda tile: dot_nn(attn[...], w_o[layer, :, tile_cols(tile)]))
+        pass_on(base + 2)
+        sum_end()
+        for which in range(2):
+            at = pl.ds(which * half, half)
+            mid = sum_rows(which) + vec_row(layer, 4) + h_full[own_rows(which), :].astype(f32)
+            x_own[layer, at, :] = mid
+            center, rate = norm_parts(mid)
+            m_full[own_rows(which), :] = (
+                center * rate * vec_row(layer, 0) + vec_row(layer, 5)
+            ).astype(b16)
+            gat_start(m_full, which)
+        turn(attn, o_turn, layer)
+        turn(h_full, h_turn, layer)
+        gat_end(m_full)
+        have(base + 2)
+
+        def ffn_tile(tile, carry):
+            at = tile_cols(tile)
+            pre = dot_nn(m_full[...], w_i[layer, :, at]) + bin_all[layer : layer + 1, at]
+            cumul = 0.5 * (1.0 + lax.erf(pre * 0.7071067811865476))
+            dens = jnp.exp(-0.5 * pre * pre) * 0.3989422804014327
+            active[:, at] = (pre * cumul).astype(b16)
+            slope[layer, :, at] = (cumul + pre * dens).astype(b16)
+            return carry
+
+        lax.fori_loop(0, hidden_cols // TILE, ffn_tile, 0)
+        pass_on(base + 3)
+        turn(m_full, m_turn, layer)
+        have(base + 3)
+        sum_start(lambda tile: dot_nn(active[...], w_b[layer, :, tile_cols(tile)]))
+        turn(active, g_turn, layer)
+        pass_on(base + 4)
+        sum_end()
+        for which in range(2):
+            at = pl.ds(which * half, half)
+            late = sum_rows(which) + vec_row(layer, 6) + m_full[own_rows(which), :].astype(f32)
+            y_own[layer, at, :] = late
+            center, rate = norm_parts(late)
+            result = (center * rate * vec_row(layer, 1) + vec_row(layer, 7)).astype(b16)
+            if layer + 1 < LAYERS:
+                h_full[own_rows(which), :] = result
+                gat_start(h_full, which)
+            else:
+                hidden_out[at, :] = result
+        if layer + 1 < LAYERS:
+            gat_end(h_full)
+
+    out_logits = pltpu.make_async_copy(scores, logits_out, out_sem.at[0])
+    out_logits.start()
+    for kind, layer in order:
+        for step in range(1, cols_n):
+            w_z(kind, layer, step).wait_send()
+            w_x_pass(kind, layer, step).wait_send()
+        w_x_own(kind, layer).wait_send()
+
+    packs = (pk_q, pk_o, pk_i, pk_b)
+    got_x = (rx_q, rx_o, rx_i, rx_b)
+    got_z = (rz_q, rz_o, rz_i, rz_b)
+    fins = (fin_q, fin_o, fin_i, fin_b)
+    sums = (sum_qkv, sum_out, sum_in, sum_back)
+
+    def g_x(kind, layer, at):
+        return rdma(
+            packs[kind].at[at, 1 - side],
+            got_x[kind].at[layer, at],
+            gxs_sem.at[kind, at],
+            gxr_sem.at[layer, kind, at],
+            across,
+            ten,
+        )
+
+    def g_z(kind, layer, step):
+        to = lax.rem(place + step, cols_n)
+        return rdma(
+            packs[kind].at[to, side],
+            got_z[kind].at[layer, step - 1],
+            gzs_sem.at[kind, step - 1],
+            gzr_sem.at[layer, kind, step - 1],
+            to * 2 + side,
+            ten,
+        )
+
+    def g_free(kind, layer):
+        for at in range(cols_n):
+            g_x(kind, layer, at).wait_send()
+        for step in range(1, cols_n):
+            g_z(kind, layer, step).wait_send()
+
+    def chunks_of(kind):
+        if kind == 0:
+            return [(which,) for which in range(3)]
+        if kind == 3:
+            return [(pl.ds(piece * 256, 256),) for piece in range(hidden_cols // 256)]
+        return [()]
+
+    def g_mid(kind, layer):
+        for step in range(1, cols_n + 1):
+            to = lax.rem(place + step, cols_n)
+            g_x(kind, layer, to).wait_recv()
+            for piece in chunks_of(kind):
+                ours = (to, side) + piece
+                theirs = (layer, to) + piece
+                packs[kind][ours] = (
+                    packs[kind][ours].astype(f32) + got_x[kind][theirs].astype(f32)
+                ).astype(b16)
+            if step < cols_n:
+                g_z(kind, layer, step).start()
+
+    def g_end(kind, layer):
+        for step in range(1, cols_n):
+            g_z(kind, layer, step).wait_recv()
+        if layer + 1 < LAYERS:
+            fin_copy(kind, layer + 1).wait()
+        for piece in chunks_of(kind):
+            total = packs[kind][(place, side) + piece].astype(f32)
+            for step in range(1, cols_n):
+                total = total + got_z[kind][(layer, step - 1) + piece].astype(f32)
+            fins[kind][piece if piece else (slice(None),)] = total
+        fin_copy(kind, layer).start()
+
+    def fin_copy(kind, layer):
+        return pltpu.make_async_copy(fins[kind], sums[kind].at[layer], fin_sem.at[kind])
+
+    def pair_rows(at):
+        return pl.ds(mult(at * 2 * cut, 2 * cut), 2 * cut)
+
+    def grad_back(layer):
+        def one(at, carry):
+            for piece in range(hidden_cols // 512):
+                rows = slice(piece * 512, (piece + 1) * 512)
+                value = dot_nn(g_turn[layer, rows, :], m_full[:, pair_rows(at)]).astype(b16)
+                pk_b[at, 0, rows, :] = value[:, :cut]
+                pk_b[at, 1, rows, :] = value[:, cut:]
+            g_x(3, layer, at).start()
+            return carry
+
+        lax.fori_loop(0, cols_n, one, 0)
+
+    def grad_in(layer):
+        def one(at, carry):
+            for piece in range(hidden_cols // 512):
+                cols = slice(piece * 512, (piece + 1) * 512)
+                value = dot_nn(m_turn[layer, pair_rows(at), :], active[:, cols]).astype(b16)
+                pk_i[at, 0, :, cols] = value[:cut]
+                pk_i[at, 1, :, cols] = value[cut:]
+            g_x(2, layer, at).start()
+            return carry
+
+        lax.fori_loop(0, cols_n, one, 0)
+
+    def grad_out(layer):
+        def one(at, carry):
+            value = dot_nn(o_turn[layer], h_full[:, pair_rows(at)]).astype(b16)
+            pk_o[at, 0] = value[:, :cut]
+            pk_o[at, 1] = value[:, cut:]
+            g_x(1, layer, at).start()
+            return carry
+
+        lax.fori_loop(0, cols_n, one, 0)
+
+    def grad_qkv(layer):
+        def one(at, carry):
+            for which in range(3):
+                value = dot_nn(h_turn[layer, pair_rows(at), :], d_qkv[which]).astype(b16)
+                pk_q[at, 0, which] = value[:cut]
+                pk_q[at, 1, which] = value[cut:]
+            g_x(0, layer, at).start()
+            return carry
+
+        lax.fori_loop(0, cols_n, one, 0)
+
+    def norm_back(kept, upstream, gain):
+        center, rate = norm_parts(kept)
+        unit = center * rate
+        scaled = upstream * gain
+        down = rate * (
+            scaled
+            - jnp.mean(scaled, axis=-1, keepdims=True)
+            - unit * jnp.mean(scaled * unit, axis=-1, keepdims=True)
+        )
+        return down, unit
+
+    def note(row, values):
+        small_acc[row : row + 1, :] += jnp.sum(values, axis=0, keepdims=True)
+
+    for layer in reversed(range(LAYERS)):
+        last = layer + 1 == LAYERS
+        base = layer * 8
+        for which in range(2):
+            at = pl.ds(which * half, half)
+            upstream = cotangent[at, :].astype(f32) if last else d_own[at, :]
+            down, unit = norm_back(y_own[layer, at, :], upstream, vec_row(layer, 1))
+            note(base + 1, upstream * unit)
+            note(base + 7, upstream)
+            note(base + 6, down)
+            d_keep[at, :] = down
+            m_full[own_rows(which), :] = down.astype(b16)
+            gat_start(m_full, which)
+        if not last:
+            g_mid(0, layer + 1)
+        gat_end(m_full)
+        if not last:
+            g_free(3, layer + 1)
+            g_end(3, layer + 1)
+        grad_back(layer)
+
+        def slope_tile(tile, carry):
+            at = tile_cols(tile)
+            d_active = dot_nt(m_full[...], w_b[layer, at, :])
+            d_pre = (d_active * slope[layer, :, at].astype(f32)).astype(b16)
+            active[:, at] = d_pre
+            small_acc[LAYERS * 8 + layer : LAYERS * 8 + layer + 1, at] = jnp.sum(
+                d_pre.astype(f32), axis=0, keepdims=True
+            )
+            return carry
+
+        lax.fori_loop(0, hidden_cols // TILE, slope_tile, 0)
+        sum_start(lambda tile: dot_nt(active[...], w_i[layer, tile_cols(tile), :]))
+        if not last:
+            g_free(2, layer + 1)
+            g_end(2, layer + 1)
+        grad_in(layer)
+        g_mid(3, layer)
+        sum_end()
+        for which in range(2):
+            at = pl.ds(which * half, half)
+            upstream = sum_rows(which) + d_keep[at, :]
+            down, unit = norm_back(x_own[layer, at, :], upstream, vec_row(layer, 0))
+            note(base + 0, upstream * unit)
+            note(base + 5, upstream)
+            note(base + 4, down)
+            d_keep[at, :] = down
+            h_full[own_rows(which), :] = down.astype(b16)
+            gat_start(h_full, which)
+        if not last:
+            g_free(1, layer + 1)
+            g_end(1, layer + 1)
+        gat_end(h_full)
+        d_attn[...] = dot_nt(h_full[...], w_o[layer]).astype(b16)
+        grad_out(layer)
+        if last:
+            out_logits.wait()
+        g_mid(2, layer)
+        attend_back(layer, last)
+        small_acc[base + 2 : base + 3, own_cols] = jnp.sum(
+            d_qkv[0].astype(f32), axis=0, keepdims=True
+        )
+        small_acc[base + 3 : base + 4, own_cols] = jnp.sum(
+            d_qkv[2].astype(f32), axis=0, keepdims=True
+        )
+        if not last:
+            g_free(0, layer + 1)
+            g_end(0, layer + 1)
+
+        def input_tile(tile):
+            rows = tile_cols(tile)
+            total = dot_nt(d_qkv[0], w_q[layer, 0, rows, :])
+            total = total + dot_nt(d_qkv[1], w_q[layer, 1, rows, :])
+            return total + dot_nt(d_qkv[2], w_q[layer, 2, rows, :])
+
+        sum_start(input_tile)
+        grad_qkv(layer)
+        g_mid(1, layer)
+        sum_end()
+        for which in range(2):
+            at = pl.ds(which * half, half)
+            result = sum_rows(which) + d_keep[at, :]
+            if layer:
+                d_own[at, :] = result
+            else:
+                grad_hidden[at, :] = result
+
+    out_scores = pltpu.make_async_copy(scores, grad_scores, out_sem.at[1])
+    out_scores.start()
+
+    small_got[ten] = small_acc[...]
+
+    def small_one(step):
+        return rdma(
+            small_acc,
+            small_got.at[ten],
+            sml_s.at[step - 1],
+            sml_r.at[step - 1],
+            dp,
+            lax.rem(ten + step, 4),
+        )
+
+    for step in range(1, 4):
+        small_one(step).start()
+    g_mid(0, 0)
+    for step in range(1, 4):
+        small_one(step).wait_recv()
+    mat_rows = LAYERS * 8
+    for dev in range(data_parts):
+        cols = slice(dev * LANES, (dev + 1) * LANES)
+        total = small_got[0, 0:mat_rows, cols]
+        for other in range(1, 4):
+            total = total + small_got[other, 0:mat_rows, cols]
+        small_send[dev, 0:mat_rows, :] = total
+        from_cols = pl.ds(mult(((dev % 2) * 4 + ten) * LANES, LANES), LANES)
+        small_send[dev, mat_rows : mat_rows + 8, :] = small_got[
+            dev // 2, mat_rows : mat_rows + 8, from_cols
+        ]
+
+    def small_two(step):
+        to = lax.rem(dp + step, data_parts)
+        return rdma(
+            small_send.at[to],
+            small_sum.at[step - 1],
+            sml_s.at[2 + step],
+            sml_r.at[2 + step],
+            to,
+            ten,
+        )
+
+    def small_go(step, carry):
+        small_two(step).start()
+        return carry
+
+    lax.fori_loop(1, data_parts, small_go, 0)
+    g_end(3, 0)
+    g_end(2, 0)
+    g_end(1, 0)
+    small_out[...] = small_send[dp]
+
+    def small_wait(step, carry):
+        small_two(step).wait_recv()
+        small_two(step).wait_send()
+        small_out[...] += small_sum[step - 1]
+        return carry
+
+    lax.fori_loop(1, data_parts, small_wait, 0)
+    for step in range(1, 4):
+        small_one(step).wait_send()
+    g_end(0, 0)
+    for kind in range(ROWS_MAT):
+        g_free(kind, 0)
+        fin_copy(kind, 0).wait()
+    out_scores.wait()
+
+
+def fits(parts, head_cols, hidden_cols, heads_here, tokens, width, blocks):
+    data_parts, tensor_parts = parts
+    return (
+        tensor_parts == 4
+        and data_parts % 2 == 0
+        and data_parts > 2
+        and width // data_parts == LANES
+        and head_cols // heads_here == 64
+        and head_cols % TILE == 0
+        and hidden_cols == data_parts * LANES
+        and hidden_cols % 512 == 0
+        and blocks == 1
+        and tokens % 512 == 0
+    )
+
+
+def shards(*arrays, parts):
+    (
+        hidden_in,
+        logits_in,
+        cotangent,
+        bucket_ids,
+        seq_counts,
+        key_mask,
+        w_qkv,
+        w_out,
+        w_in,
+        w_back,
+        vectors,
+        bias_in,
+    ) = arrays[:12]
+    data_parts = parts[0]
+    tokens, width = hidden_in.shape
+    head_cols = w_qkv.shape[3]
+    hidden_cols = w_in.shape[2]
+    heads = logits_in.shape[1]
+    if not fits(parts, head_cols, hidden_cols, heads, tokens, width, logits_in.shape[0]):
+        return plain_shards(*arrays)
+    f32 = jnp.float32
+    b16 = jnp.bfloat16
+    ten = lax.axis_index("tensor")
+    share = tokens // 4
+    cut = width // data_parts
+    cols_n = data_parts // 2
+    bucket = bucket_ids[0]
+    seq_span = jnp.where(bucket == 0, tokens // 4, jnp.where(bucket == 1, tokens // 2, tokens))
+    seq_of = jnp.arange(tokens, dtype=jnp.int32) // seq_span
+    live = (key_mask == 1) & (seq_of < seq_counts[0])
+    row_ids = jnp.broadcast_to(seq_of.astype(f32)[:, None], (tokens, LANES))
+    key_ids = jnp.broadcast_to(jnp.where(live, seq_of, -1).astype(f32)[None, :], (8, tokens))
+    owned = vectors.shape[2]
+    spread = jnp.tile(vectors.reshape(LAYERS * 8, owned), (1, LANES // owned))
+    mine = (jnp.arange(LANES, dtype=jnp.int32) // owned) == ten
+    spread = jnp.where(mine[None, :], spread, 0.0)
+    small_in = jnp.concatenate(
+        [spread, bias_in, jnp.zeros((32 - LAYERS * 9, LANES), f32)], axis=0
+    ).astype(b16)
+
+    hbm = pl.BlockSpec(memory_space=pl.ANY)
+    vmem = pl.BlockSpec(memory_space=pltpu.VMEM)
+    dma = pltpu.SemaphoreType.DMA
+    shape = jax.ShapeDtypeStruct
+    n = LAYERS
+    grad_shapes = (
+        (3, cut, head_cols),
+        (head_cols, cut),
+        (cut, hidden_cols),
+        (hidden_cols, cut),
+    )
+    results = pl.pallas_call(
+        functools.partial(step_kernel, data_parts),
+        out_shape=(
+            shape((share, width), b16),
+            shape((heads, tokens, tokens), b16),
+            shape((share, width), f32),
+            shape((heads, tokens, tokens), b16),
+        )
+        + tuple(shape((n,) + size, f32) for size in grad_shapes)
+        + (shape((24, LANES), f32),),
+        in_specs=[hbm, hbm, vmem, vmem, vmem, vmem, hbm, hbm, hbm, hbm],
+        out_specs=(vmem, hbm, vmem, hbm, hbm, hbm, hbm, hbm, vmem),
+        scratch_shapes=[
+            pltpu.VMEM((n, 3, width, head_cols), b16),
+            pltpu.VMEM((n, head_cols, width), b16),
+            pltpu.VMEM((n, width, hidden_cols), b16),
+            pltpu.VMEM((n, hidden_cols, width), b16),
+            pltpu.VMEM((heads, tokens, tokens), b16),
+            pltpu.VMEM((n, heads, tokens, tokens), b16),
+            pltpu.VMEM((tokens, width), b16),
+            pltpu.VMEM((tokens, width), b16),
+            pltpu.VMEM((tokens, hidden_cols), b16),
+            pltpu.VMEM((tokens, head_cols), b16),
+            pltpu.VMEM((n, width, tokens), b16),
+            pltpu.VMEM((n, width, tokens), b16),
+            pltpu.VMEM((n, hidden_cols, tokens), b16),
+            pltpu.VMEM((n, head_cols, tokens), b16),
+            pltpu.VMEM((n, tokens, hidden_cols), b16),
+            pltpu.VMEM((n, 3, tokens, head_cols), b16),
+            pltpu.VMEM((n, share, width), f32),
+            pltpu.VMEM((n, share, width), f32),
+            pltpu.VMEM((3, tokens, head_cols), b16),
+            pltpu.VMEM((tokens, head_cols), b16),
+            pltpu.VMEM((share, width), f32),
+            pltpu.VMEM((share, width), f32),
+            pltpu.VMEM((LANES, tokens), f32),
+            pltpu.VMEM((LANES, tokens), f32),
+            pltpu.VMEM((tokens, width), b16),
+            pltpu.VMEM((2, share, width), b16),
+            pltpu.VMEM((share, width), b16),
+            pltpu.VMEM((share, width), b16),
+            pltpu.VMEM((4, data_parts, 32, LANES), b16),
+            pltpu.VMEM((n * 8, width), f32),
+            pltpu.VMEM((8, hidden_cols), f32),
+            pltpu.VMEM((n * 8 + 8, width), f32),
+            pltpu.VMEM((4, n * 8 + 8, width), f32),
+            pltpu.VMEM((data_parts, n * 8 + 8, LANES), f32),
+            pltpu.VMEM((data_parts - 1, n * 8 + 8, LANES), f32),
+        ]
+        + [pltpu.VMEM((cols_n, 2) + size, b16) for size in grad_shapes]
+        + [pltpu.VMEM((n, cols_n) + size, b16) for size in grad_shapes]
+        + [pltpu.VMEM((n, cols_n - 1) + size, b16) for size in grad_shapes]
+        + [pltpu.VMEM(size, f32) for size in grad_shapes]
+        + [
+            dma((2,)),
+            dma((n, 4)),
+            dma((n, 4, cols_n - 1)),
+            dma((n, 4, cols_n - 1)),
+            dma((n, 4, cols_n)),
+            dma((n, 4, cols_n)),
+            dma((width // TILE, 2)),
+            dma((width // TILE, 2)),
+            dma((width // TILE,)),
+            dma((width // TILE,)),
+            dma((2, 3)),
+            dma((2, 3)),
+            dma((data_parts + 2,)),
+            dma((data_parts + 2,)),
+            dma((data_parts + 2,)),
+            dma((data_parts + 2,)),
+            dma((4, cols_n)),
+            dma((n, 4, cols_n)),
+            dma((4, cols_n - 1)),
+            dma((n, 4, cols_n - 1)),
+            dma((4,)),
+            dma((2,)),
+        ],
+        compiler_params=pltpu.CompilerParams(
+            collective_id=0, has_side_effects=True, vmem_limit_bytes=63 * 1024 * 1024
+        ),
+    )(
+        hidden_in,
+        logits_in,
+        cotangent,
+        row_ids,
+        key_ids,
+        small_in,
+        w_qkv.astype(b16),
+        w_out.astype(b16),
+        w_in.astype(b16),
+        w_back.astype(b16),
+    )
+    hidden_out, logits_out, grad_hidden, grad_scores = results[:4]
+    small = results[8]
+    vec_sum = lax.dynamic_slice_in_dim(small[: LAYERS * 8], ten * owned, owned, 1)
+    bin_sum = small[LAYERS * 8 : LAYERS * 9]
+    grads_all = results[4:8] + (vec_sum.reshape(LAYERS, 8, owned), bin_sum)
+    masters = arrays[6:12]
+    firsts = arrays[12:18]
+    seconds = arrays[18:24]
+    decays = (DECAY_RATE, DECAY_RATE, DECAY_RATE, DECAY_RATE, 0.0, 0.0)
+    moved = []
+    for master, gradient, first_prev, second_prev, decay_rate in zip(
+        masters, grads_all, firsts, seconds, decays
+    ):
+        moment_one = BETA_ONE * first_prev + (1.0 - BETA_ONE) * gradient
+        moment_two = BETA_TWO * second_prev + (1.0 - BETA_TWO) * gradient * gradient
+        update = (
+            moment_one / CORRECT_ONE / (jnp.sqrt(moment_two / CORRECT_TWO) + ADAM_EPS)
+            + decay_rate * master
+        )
+        moved.append((moment_one, update))
+    weight_sq = jnp.stack(
+        [jnp.sum((master * master).reshape(LAYERS, -1), axis=1) for master in masters]
+    )
+    update_sq = jnp.stack(
+        [jnp.sum((moved_one[1] * moved_one[1]).reshape(LAYERS, -1), axis=1) for moved_one in moved]
+    )
+    weight_tot, update_tot = lax.psum((weight_sq, update_sq), ("dp", "tensor"))
+    trust_all = jnp.sqrt(weight_tot) / jnp.sqrt(update_tot)
+    new_params = tuple(
+        (
+            master
+            - LEARN_RATE
+            * trust_all[group_at].reshape((LAYERS,) + (1,) * (master.ndim - 1))
+            * moved_one[1]
+            for group_at, (master, moved_one) in enumerate(zip(masters, moved))
+        )
+    )
+    return (
+        (hidden_out, logits_out[None], grad_hidden, grad_scores[None].astype(f32))
+        + grads_all
+        + new_params
+        + tuple(moved_one[0] for moved_one in moved)
+        + (trust_all.T,)
+    )
+
+
 def solution(mesh):
     return jax.shard_map(
-        shards,
+        functools.partial(shards, parts=(mesh.shape["dp"], mesh.shape["tensor"])),
         mesh=mesh,
         in_specs=(
             P("dp", None),

time: 1490 us -> 461 us (0.31)
  waiting for transfers between devices: 1020 us -> 0 us
  Pallas kernels: 0 us -> 375 us
  blocking collectives: 179 us -> 38.7 us
  matrix products: 110 us -> 0 us
  local copies, waits for them, and re-layouts: 80.4 us -> 10.1 us
  other arithmetic: 76 us -> 34.2 us
  between operations: 17.4 us -> 2.32 us
    psum x1 -> x0, waiting for transfers between devices: 407 us -> none  [shards(): lax.psum(mats[0].astype(jnp.bfloat16), 'dp').astype(jnp.float32)]
    pallas_call x0 -> x1, Pallas kernels: none -> 375 us  [shards(): pl.pallas_call(functools.partial(step_kernel, data_parts), out_shape=(sha...]
    all_gather x13 -> x0, waiting for transfers between devices: 237 us -> none  [the longest x2 90.4 us: shards(): lax.all_gather(w_back[layer_at].astype(jnp.bfloat16), 'dp', axis=1, tiled...]
    unnamed x26 -> x0, waiting for transfers between devices: 232 us -> none
    reduce_scatter x8 -> x0, waiting for transfers between devices: 144 us -> none  [the longest x4 73.6 us: sum_backward(): lax.psum_scatter(term_fn(jnp.int32(0), share_rows * lax.axis_size('tensor...]
    all_gather x4 -> x0, blocking collectives: 139 us -> none  [the longest x2 56.8 us: shards(): lax.all_gather(w_out[layer_at].astype(jnp.bfloat16), 'dp', axis=1, tiled=...]
    dot_general x47 -> x0, matrix products: 102 us -> none  [the longest x2 17.1 us: shards(): jnp.dot(forward_mid_full, forward_win, preferred_element_type=jnp.float32)]
    slice x7 -> x1, local copies, waits for them, and re-layouts: 51.4 us -> 0.01 us  [shards(): small[:LAYERS * 8]]
  transfers between devices with their start and end apart: 24 -> 0, of which waited for: 20 -> 0; matrix products, arithmetic and copies ran while one was open for 12% -> 0% of each run, Pallas kernels for 0% -> 0%
where the time goes in v1:
time: 461 us
  Pallas kernels  375 us (81%)
  blocking collectives  38.7 us (8%)
  other arithmetic  34.2 us (7%)
  local copies, waits for them, and re-layouts  10.1 us (2%)
    pallas_call x1, Pallas kernels, shards(): pl.pallas_call(functools.partial(step_kernel, data_parts), out_shape=(sha...  375 us
    psum x1, blocking collectives, shards(): weight_tot, update_tot = lax.psum((weight_sq, update_sq), ('dp', 'tensor'))  38.7 us
    reduce_sum x6, other arithmetic, shards(): jnp.sum((moved_one[1] * moved_one[1]).reshape(LAYERS, -1), axis=1)  14.4 us

profile of v1, /device:TPU:0, one launch (start us, length us, event | category | flops | bytes accessed | tf_op | source)
XLA Modules:
  0.0 460.6 jit_solution(6205749088558657693)
XLA Ops:
  2.1 0.8 select_convert_fusion.1
  2.9 0.8 broadcast_in_dim.34.row_ids
  4.4 0.9 multiply_reduce_fusion.17
  5.2 0.7 tile.11
  6.8 2.4 multiply_reduce_fusion.5
  9.2 1.7 multiply_reduce_fusion.7
  10.9 1.0 multiply_reduce_fusion.3
  11.9 1.0 multiply_reduce_fusion.2
  12.9 375.2 %shard_map.407 = (bf16[128,1024]{1,0:T(8,128)(2,1)}, bf16[4,512,512]{2,1,0:T(8,128)(2,1)}, f32[128,1024]{1,0:T(8,128)}, bf16[4,512,512]{2,1,0:T(8,128)(2,1)}, f3...) custom-call(bf16[512,1024]{1,0:T(8,128)(2,1)} %hidden_in.1, ...), custom_call_target="tpu_custom_call" | custom-call | tf_op jit(solution)/shard_map/pallas_call | solution.py:1393
  388.3 4.3 bitcast_convert_fusion
  394.0 3.2 multiply_reduce_fusion.4
  397.3 1.9 multiply_reduce_fusion.6
  399.4 4.0 multiply_reduce_fusion.1
  403.5 3.9 multiply_reduce_fusion
  408.4 38.7 %all-reduce = (f32[6,2]{0,1:T(2,128)S(1)}, f32[6,2]{0,1:T(2,128)S(1)}) all-reduce(f32[6,2]{0,1:T(2,128)S(1)} %stack.55, f32[6,2]{0,1:T(2,128)S(1)} %stack.48), channel_id=1, replica_groups=mesh['dp'=8,'tensor'=4] {'dp','tensor'}, use_global_device_ids=true, to_apply=%region_13.14 | all-reduce | flops 24 | bytes 192 | tf_op jit(solution)/shard_map/psum | solution.py:1511
  447.4 2.3 multiply_subtract_fusion.2
  449.7 0.8 multiply_subtract_fusion.3
  450.5 1.2 multiply_subtract_fusion.1
  451.7 1.1 multiply_subtract_fusion
  454.9 1.3 copy.82
  456.3 0.8 copy.83
  457.1 0.9 copy.84
  458.6 1.0 copy.86
  459.6 1.0 copy.87
  (82 shorter events, 7.3 us)
Async XLA Ops:
  0.7 10.3 %copy-start = (f32[2,128,1024]{2,1,0:T(8,128)S(1)}, f32[2,128,1024]{2,1,0:T(8,128)}, u32[]{:S(2)}) copy-start(f32[2,128,1024]{2,1,0:T(8,128)} %param.32) | copy-start | bytes 3145732
  0.7 11.3 %copy-start.2 = (f32[2,1024,128]{2,1,0:T(8,128)S(1)}, f32[2,1024,128]{2,1,0:T(8,128)}, u32[]{:S(2)}) copy-start(f32[2,1024,128]{2,1,0:T(8,128)} %param.33) | copy-start | bytes 3145732
  388.2 4.4 copy-start.23
  388.2 4.4 copy-start.18
  388.2 4.4 copy-start.21
  388.2 4.4 copy-start.22
  388.2 5.1 %copy-start.20 = (f32[2,128]{1,0:T(2,128)S(1)}, f32[2,128]{1,0:T(2,128)}, u32[]{:S(2)}) copy-start(f32[2,128]{1,0:T(2,128)} %param.35) | copy-start | bytes 3076
  388.2 5.1 %copy-start.24 = (f32[2,128]{1,0:T(2,128)S(1)}, f32[2,128]{1,0:T(2,128)}, u32[]{:S(2)}) copy-start(f32[2,128]{1,0:T(2,128)} %param.47) | copy-start | bytes 3076
  388.2 5.1 %copy-start.25 = (f32[2,128]{1,0:T(2,128)S(1)}, f32[2,128]{1,0:T(2,128)}, u32[]{:S(2)}) copy-start(f32[2,128]{1,0:T(2,128)} %param.41) | copy-start | bytes 3076
  388.2 5.8 %copy-start.4 = (f32[2,3,128,256]{3,2,1,0:T(8,128)S(1)}, f32[2,3,128,256]{3,2,1,0:T(8,128)}, u32[]{:S(2)}) copy-start(f32[2,3,128,256]{3,2,1,0:T(8,128)} %param.30) | copy-start | bytes 2359300
  388.2 5.7 %copy-start.9 = (f32[2,3,128,256]{3,2,1,0:T(8,128)S(1)}, f32[2,3,128,256]{3,2,1,0:T(8,128)}, u32[]{:S(2)}) copy-start(f32[2,3,128,256]{3,2,1,0:T(8,128)} %get-tuple-element.132) | copy-start | bytes 2359300
  394.0 3.3 copy-start.11
  394.0 3.3 copy-start.13
  394.0 3.3 copy-start.17
  394.0 5.3 %copy-start.1 = (f32[2,128,1024]{2,1,0:T(8,128)S(1)}, f32[2,128,1024]{2,1,0:T(8,128)}, u32[]{:S(2)}) copy-start(f32[2,128,1024]{2,1,0:T(8,128)} %param.32) | copy-start | bytes 3145732
  399.4 4.1 copy-start.3
  447.2 2.6 copy-start.14
  447.2 3.4 copy-start.7
  447.2 4.5 copy-start.19
  451.7 2.5 copy-start.16
  451.7 3.2 copy-start.12
  454.9 2.2 copy-start.10
  456.3 2.4 copy-start.6
  457.1 2.6 copy-start.5
  (2 other events, 3.4 us)

commit v2 on v1

--- a/solution.py
+++ b/solution.py
@@ -471,6 +471,15 @@
 TILE = 256
 LANES = 128
 ROWS_MAT = 4
+X_FIRST = 9
+Z_AHEAD = 2
+X_AHEAD = 3
+SLOTS = ((1, 3), (2, 1), (2, 3), (3, 1), (3, 2), (4, 1), (5, 1))
+BACK_SLOTS = (
+    (-9, -9, 0, 1, 2, 3, 4, 5, 6),
+    (-9, -5, -4, -2, 0, 0, 1, 2, 3),
+    (4,),
+)
 
 
 def dot_nn(left, right):
@@ -496,13 +505,24 @@
     hidden_in,
     logits_in,
     cotangent,
-    row_ids,
     key_ids,
     small_in,
     own_qkv,
     own_out,
     own_in,
     own_back,
+    lw_qkv,
+    lw_out,
+    lw_in,
+    lw_back,
+    lm_qkv,
+    lm_out,
+    lm_in,
+    lm_back,
+    lv_qkv,
+    lv_out,
+    lv_in,
+    lv_back,
     hidden_out,
     logits_out,
     grad_hidden,
@@ -512,6 +532,7 @@
     sum_in,
     sum_back,
     small_out,
+    norm_out,
     w_q,
     w_o,
     w_i,
@@ -531,8 +552,6 @@
     x_own,
     y_own,
     d_qkv,
-    d_attn,
-    d_own,
     d_keep,
     turn_v,
     turn_k,
@@ -559,10 +578,23 @@
     rz_o,
     rz_i,
     rz_b,
-    fin_q,
-    fin_o,
-    fin_i,
-    fin_b,
+    fw_q,
+    fw_o,
+    fw_i,
+    fw_b,
+    fm_q,
+    fm_o,
+    fm_i,
+    fm_b,
+    fv_q,
+    fv_o,
+    fv_i,
+    fv_b,
+    norms,
+    norm_send,
+    norm_ten,
+    norm_mid,
+    norm_dp,
     load_sem,
     own_sem,
     zs_sem,
@@ -585,6 +617,9 @@
     gzr_sem,
     fin_sem,
     out_sem,
+    lamb_sem,
+    ns_sem,
+    nr_sem,
 ):
     dp = lax.axis_index("dp")
     ten = lax.axis_index("tensor")
@@ -663,11 +698,11 @@
         )
     pl.semaphore_wait(barrier, data_parts + 2)
 
-    vec_got[ten, dp] = small_in[...]
+    vec_got[ten, dp] = small_in[0].astype(b16)
 
     def vec_one(step):
         return rdma(
-            small_in,
+            vec_got.at[ten, dp],
             vec_got.at[ten, dp],
             vec_s.at[step - 1],
             vec_r.at[step - 1],
@@ -681,59 +716,112 @@
 
     lax.fori_loop(1, data_parts, vec_go, 0)
 
-    def w_z(kind, layer, step):
+    def w_x(kind, layer, from_place, col, own=False):
+        dst = region(kind, layer, from_place * 2 + col)
         return rdma(
-            owns[kind].at[layer],
-            region(kind, layer, dp),
-            zs_sem.at[layer, kind, step - 1],
-            zr_sem.at[layer, kind, step - 1],
-            along(step),
-            ten,
-        )
-
-    def w_x_own(kind, layer):
-        return rdma(
-            owns[kind].at[layer],
-            region(kind, layer, dp),
-            xs_sem.at[layer, kind, 0],
-            xr_sem.at[layer, kind, 0],
+            owns[kind].at[layer] if own else dst,
+            dst,
+            xs_sem.at[layer, kind, from_place],
+            xr_sem.at[layer, kind, from_place],
             across,
             ten,
         )
 
-    def w_x_pass(kind, layer, step):
-        came = region(kind, layer, along(cols_n - step))
+    def w_z(kind, layer, from_place, col, way, own=False):
+        dst = region(kind, layer, from_place * 2 + col)
+        which = lax.rem(col + side, 2)
         return rdma(
-            came,
-            came,
-            xs_sem.at[layer, kind, step],
-            xr_sem.at[layer, kind, step],
-            across,
+            owns[kind].at[layer] if own else dst,
+            dst,
+            zs_sem.at[layer, kind, from_place, which, (way + 1) // 2],
+            zr_sem.at[layer, kind, from_place, which],
+            dp + 2 * way,
             ten,
         )
 
+    can_go = {1: place < cols_n - 1, -1: place > 0}
+
+    def w_both_ways(kind, layer, col, own=False):
+        for way in (1, -1):
+
+            @pl.when(can_go[way])
+            def _():
+                w_z(kind, layer, place, col, way, own).start()
+
+    def w_event(kind, layer, hop):
+        if hop == 0:
+            w_x(kind, layer, place, 1 - side).wait_recv()
+            w_both_ways(kind, layer, 1 - side)
+            return
+        for way in (1, -1):
+            came = place - hop * way
+
+            @pl.when(came >= 0 if way == 1 else came < cols_n)
+            def _():
+                for col in (side, 1 - side) if kind == X_FIRST else (side,):
+                    w_z(kind, layer, came, col, way).wait_recv()
+
+                    @pl.when(can_go[way])
+                    def _():
+                        w_z(kind, layer, came, col, way).start()
+
+                    if kind != X_FIRST:
+                        w_x(kind, layer, came, side).start()
+
     order = [(kind, layer) for layer in range(LAYERS) for kind in range(ROWS_MAT)]
-    for kind, layer in order:
-        for step in range(1, cols_n):
-            w_z(kind, layer, step).start()
-        if (kind, layer) in order[:2]:
-            w_x_own(kind, layer).start()
-
-    def pass_on(index):
-        if index >= len(order):
-            return
-        kind, layer = order[index]
-        for step in range(1, cols_n):
-            w_z(kind, layer, step).wait_recv()
-            w_x_pass(kind, layer, step).start()
-        if index + 2 < len(order):
-            w_x_own(*order[index + 2]).start()
-
-    def have(index):
-        kind, layer = order[index]
-        w_x_own(kind, layer).wait_recv()
-        for step in range(1, cols_n):
-            w_x_pass(kind, layer, step).wait_recv()
+
+    def w_own_z(index):
+        if index < len(order):
+            w_both_ways(*order[index], side, True)
+
+    def w_own_x(index):
+        if index < len(order):
+            w_x(*order[index], place, side, True).start()
+
+    for index in range(Z_AHEAD):
+        w_own_z(index)
+    for index in range(X_AHEAD):
+        w_own_x(index)
+    events = [
+        (index, hop)
+        for index in range(len(order))
+        for hop in range(0 if order[index][0] == X_FIRST else 1, cols_n)
+    ]
+    passed = [0]
+
+    def pass_on(layer_at, kind_at, hop_at):
+        goal = (layer_at * ROWS_MAT + kind_at, hop_at)
+        while passed[0] < len(events) and events[passed[0]] <= goal:
+            index, hop = events[passed[0]]
+            w_event(*order[index], hop)
+            if hop == cols_n - 1:
+                w_own_z(index + Z_AHEAD)
+                w_own_x(index + X_AHEAD)
+            passed[0] += 1
+
+    def have(layer, kind):
+        pass_on(layer, kind, cols_n)
+        if kind != X_FIRST:
+            for from_place in range(cols_n):
+                w_x(kind, layer, from_place, 1 - side).wait_recv()
+
+    def w_finish():
+        for kind, layer in order:
+            for from_place in range(cols_n):
+                if kind != X_FIRST:
+                    w_x(kind, layer, from_place, side).wait_send()
+                for col in (side, 1 - side) if kind == X_FIRST else (side,):
+
+                    @pl.when(can_go[1] & (from_place <= place))
+                    def _():
+                        w_z(kind, layer, from_place, col, 1).wait_send()
+
+                    @pl.when(can_go[-1] & (from_place >= place))
+                    def _():
+                        w_z(kind, layer, from_place, col, -1).wait_send()
+
+            if kind == X_FIRST:
+                w_x(kind, layer, place, side).wait_send()
 
     def vec_wait(step, carry):
         vec_one(step).wait_send()
@@ -888,19 +976,17 @@
     pairs = head_cols // LANES
 
     def pair_cols(pair):
-        return pl.ds(mult(pair * LANES, LANES), LANES)
-
-    def attend(layer):
+        return slice(pair * LANES, (pair + 1) * LANES)
+
+    def attend(layer, pair):
         def one(step, carry):
-            pair = step // (tokens // score_rows)
-            rows = pl.ds(
-                mult(lax.rem(step, tokens // score_rows) * score_rows, score_rows), score_rows
-            )
-            at = pair_cols(pair)
+            rows = pl.ds(mult(step * score_rows, score_rows), score_rows)
+            at = slice(pair * LANES, (pair + 1) * LANES)
             queries = qkv[layer, 0, rows, at]
             keys = qkv[layer, 1, :, at]
             values = qkv[layer, 2, :, at]
-            allowed = row_ids[rows, 0:1] == key_ids[0:1, :]
+            row = lax.broadcasted_iota(jnp.int32, (score_rows, 1), 0) + step * score_rows
+            allowed = jnp.floor(row.astype(f32) * key_ids[8:9, 0:1]) == key_ids[0:1, :]
             mixed = jnp.zeros((score_rows, LANES), f32)
             for head in range(2):
                 raw = dot_nt(queries, keys * lane_masks[head])
@@ -916,9 +1002,9 @@
             attn[rows, at] = mixed.astype(b16)
             return carry
 
-        lax.fori_loop(0, pairs * (tokens // score_rows), one, 0)
-
-    def attend_back(layer, first):
+        lax.fori_loop(0, tokens // score_rows, one, 0)
+
+    def attend_back(layer, first, pairs_of):
         def pair_one(pair, carry):
             at = pair_cols(pair)
             turn_v[...] = jnp.zeros_like(turn_v)
@@ -929,7 +1015,7 @@
                 queries = qkv[layer, 0, rows, at]
                 keys = qkv[layer, 1, :, at]
                 values = qkv[layer, 2, :, at]
-                grads = d_attn[rows, at]
+                grads = attn[rows, at]
                 turned_q = queries.T
                 turned_g = grads.T
                 d_query = jnp.zeros((score_rows, LANES), f32)
@@ -955,7 +1041,8 @@
             d_qkv[2, :, at] = turn_v[...].T.astype(b16)
             return carry
 
-        lax.fori_loop(0, pairs, pair_one, 0)
+        for pair in pairs_of:
+            pair_one(pair, 0)
 
     own_cols = pl.ds(mult(ten * head_cols, head_cols), head_cols)
     small_acc[...] = jnp.zeros_like(small_acc)
@@ -964,10 +1051,7 @@
         copy.wait()
     load_s.wait()
     for layer in range(LAYERS):
-        base = layer * ROWS_MAT
-        if layer == 0:
-            pass_on(0)
-        have(base)
+        have(layer, 0)
         for which in range(3):
             product = dot_nn(h_full[...], w_q[layer, which])
             if which == 0:
@@ -975,12 +1059,15 @@
             if which == 2:
                 product = product + vec_all[layer * 8 + 3 : layer * 8 + 4, own_cols]
             qkv[layer, which] = product.astype(b16)
-        pass_on(base + 1)
-        attend(layer)
-        have(base + 1)
-
+        pass_on(layer, *SLOTS[0])
+        attend(layer, 0)
+        pass_on(layer, *SLOTS[1])
+        attend(layer, 1)
+        have(layer, 1)
         sum_start(lambda tile: dot_nn(attn[...], w_o[layer, :, tile_cols(tile)]))
-        pass_on(base + 2)
+        turn(attn, o_turn, layer)
+        turn(h_full, h_turn, layer)
+        pass_on(layer, *SLOTS[2])
         sum_end()
         for which in range(2):
             at = pl.ds(which * half, half)
@@ -991,10 +1078,8 @@
                 center * rate * vec_row(layer, 0) + vec_row(layer, 5)
             ).astype(b16)
             gat_start(m_full, which)
-        turn(attn, o_turn, layer)
-        turn(h_full, h_turn, layer)
+        pass_on(layer, *SLOTS[3])
         gat_end(m_full)
-        have(base + 2)
 
         def ffn_tile(tile, carry):
             at = tile_cols(tile)
@@ -1005,13 +1090,14 @@
             slope[layer, :, at] = (cumul + pre * dens).astype(b16)
             return carry
 
+        have(layer, 2)
+        pass_on(layer, *SLOTS[4])
         lax.fori_loop(0, hidden_cols // TILE, ffn_tile, 0)
-        pass_on(base + 3)
         turn(m_full, m_turn, layer)
-        have(base + 3)
+        have(layer, 3)
         sum_start(lambda tile: dot_nn(active[...], w_b[layer, :, tile_cols(tile)]))
         turn(active, g_turn, layer)
-        pass_on(base + 4)
+        pass_on(layer, *SLOTS[5])
         sum_end()
         for which in range(2):
             at = pl.ds(which * half, half)
@@ -1019,26 +1105,25 @@
             y_own[layer, at, :] = late
             center, rate = norm_parts(late)
             result = (center * rate * vec_row(layer, 1) + vec_row(layer, 7)).astype(b16)
+            h_full[own_rows(which), :] = result
             if layer + 1 < LAYERS:
-                h_full[own_rows(which), :] = result
                 gat_start(h_full, which)
-            else:
-                hidden_out[at, :] = result
         if layer + 1 < LAYERS:
+            pass_on(layer, *SLOTS[6])
             gat_end(h_full)
 
     out_logits = pltpu.make_async_copy(scores, logits_out, out_sem.at[0])
     out_logits.start()
-    for kind, layer in order:
-        for step in range(1, cols_n):
-            w_z(kind, layer, step).wait_send()
-            w_x_pass(kind, layer, step).wait_send()
-        w_x_own(kind, layer).wait_send()
+    all_own = pl.ds(mult(ten * share, share), share)
+    out_hidden = pltpu.make_async_copy(h_full.at[all_own], hidden_out, out_sem.at[2])
+    out_hidden.start()
+    load_c = pltpu.make_async_copy(cotangent, sum_chip, out_sem.at[3])
+    load_c.start()
+    w_finish()
 
     packs = (pk_q, pk_o, pk_i, pk_b)
     got_x = (rx_q, rx_o, rx_i, rx_b)
     got_z = (rz_q, rz_o, rz_i, rz_b)
-    fins = (fin_q, fin_o, fin_i, fin_b)
     sums = (sum_qkv, sum_out, sum_in, sum_back)
 
     def g_x(kind, layer, at):
@@ -1063,6 +1148,7 @@
         )
 
     def g_free(kind, layer):
+        add_upto(layer, (3 - kind) * cols_n + cols_n - 1)
         for at in range(cols_n):
             g_x(kind, layer, at).wait_send()
         for step in range(1, cols_n):
@@ -1075,9 +1161,22 @@
             return [(pl.ds(piece * 256, 256),) for piece in range(hidden_cols // 256)]
         return [()]
 
-    def g_mid(kind, layer):
-        for step in range(1, cols_n + 1):
-            to = lax.rem(place + step, cols_n)
+    g_order = [
+        (kind, layer, turn_at)
+        for layer in reversed(range(LAYERS))
+        for kind in (3, 2, 1, 0)
+        for turn_at in range(cols_n)
+    ]
+    added = [0]
+
+    def turn_of(turn_at):
+        return lax.rem(place + 1 + turn_at, cols_n)
+
+    def add_upto(layer_at, index):
+        index = (LAYERS - 1 - layer_at) * 4 * cols_n + index
+        while added[0] <= min(index, len(g_order) - 1):
+            kind, layer, turn_at = g_order[added[0]]
+            to = turn_of(turn_at)
             g_x(kind, layer, to).wait_recv()
             for piece in chunks_of(kind):
                 ours = (to, side) + piece
@@ -1085,29 +1184,72 @@
                 packs[kind][ours] = (
                     packs[kind][ours].astype(f32) + got_x[kind][theirs].astype(f32)
                 ).astype(b16)
-            if step < cols_n:
-                g_z(kind, layer, step).start()
+            if turn_at + 1 < cols_n:
+                g_z(kind, layer, turn_at + 1).start()
+            added[0] += 1
+
+    masters = (
+        (lw_qkv, lw_out, lw_in, lw_back),
+        (lm_qkv, lm_out, lm_in, lm_back),
+        (lv_qkv, lv_out, lv_in, lv_back),
+    )
+    held = ((fw_q, fw_o, fw_i, fw_b), (fm_q, fm_o, fm_i, fm_b), (fv_q, fv_o, fv_i, fv_b))
+
+    def lamb_load(kind, layer, which):
+        return pltpu.make_async_copy(
+            masters[which][kind].at[layer], held[which][kind], lamb_sem.at[which, kind]
+        )
+
+    def lamb_update(weight, first, second, gradient, decay):
+        moment_one = BETA_ONE * first + (1.0 - BETA_ONE) * gradient
+        moment_two = BETA_TWO * second + (1.0 - BETA_TWO) * gradient * gradient
+        return (
+            moment_one / CORRECT_ONE / (jnp.sqrt(moment_two / CORRECT_TWO) + ADAM_EPS)
+            + decay * weight
+        )
+
+    def note_norm(row, values):
+        norms[row : row + 1, 0 : values.shape[-1]] += jnp.sum(
+            values * values, axis=0, keepdims=True
+        )
 
     def g_end(kind, layer):
+        add_upto(layer, (3 - kind) * cols_n + cols_n - 1)
         for step in range(1, cols_n):
             g_z(kind, layer, step).wait_recv()
-        if layer + 1 < LAYERS:
-            fin_copy(kind, layer + 1).wait()
+        for which in range(3):
+            lamb_load(kind, layer, which).wait()
         for piece in chunks_of(kind):
             total = packs[kind][(place, side) + piece].astype(f32)
             for step in range(1, cols_n):
                 total = total + got_z[kind][(layer, step - 1) + piece].astype(f32)
-            fins[kind][piece if piece else (slice(None),)] = total
+            here = piece if piece else (slice(None),)
+            weight = held[0][kind][here]
+            step_by = lamb_update(
+                weight, held[1][kind][here], held[2][kind][here], total, DECAY_RATE
+            )
+            held[1][kind][here] = total
+            note_norm((layer * 4 + kind) * 2, weight)
+            note_norm((layer * 4 + kind) * 2 + 1, step_by)
         fin_copy(kind, layer).start()
+        if layer:
+            for which in (0, 2):
+                lamb_load(kind, layer - 1, which).start()
+
+    def lamb_more(kind, layer):
+        if layer + 1 < LAYERS:
+            fin_copy(kind, layer + 1).wait()
+            lamb_load(kind, layer, 1).start()
 
     def fin_copy(kind, layer):
-        return pltpu.make_async_copy(fins[kind], sums[kind].at[layer], fin_sem.at[kind])
+        return pltpu.make_async_copy(held[1][kind], sums[kind].at[layer], fin_sem.at[kind])
 
     def pair_rows(at):
         return pl.ds(mult(at * 2 * cut, 2 * cut), 2 * cut)
 
     def grad_back(layer):
-        def one(at, carry):
+        def one(turn_at, carry):
+            at = turn_of(turn_at)
             for piece in range(hidden_cols // 512):
                 rows = slice(piece * 512, (piece + 1) * 512)
                 value = dot_nn(g_turn[layer, rows, :], m_full[:, pair_rows(at)]).astype(b16)
@@ -1119,7 +1261,8 @@
         lax.fori_loop(0, cols_n, one, 0)
 
     def grad_in(layer):
-        def one(at, carry):
+        def one(turn_at, carry):
+            at = turn_of(turn_at)
             for piece in range(hidden_cols // 512):
                 cols = slice(piece * 512, (piece + 1) * 512)
                 value = dot_nn(m_turn[layer, pair_rows(at), :], active[:, cols]).astype(b16)
@@ -1131,7 +1274,8 @@
         lax.fori_loop(0, cols_n, one, 0)
 
     def grad_out(layer):
-        def one(at, carry):
+        def one(turn_at, carry):
+            at = turn_of(turn_at)
             value = dot_nn(o_turn[layer], h_full[:, pair_rows(at)]).astype(b16)
             pk_o[at, 0] = value[:, :cut]
             pk_o[at, 1] = value[:, cut:]
@@ -1141,7 +1285,8 @@
         lax.fori_loop(0, cols_n, one, 0)
 
     def grad_qkv(layer):
-        def one(at, carry):
+        def one(turn_at, carry):
+            at = turn_of(turn_at)
             for which in range(3):
                 value = dot_nn(h_turn[layer, pair_rows(at), :], d_qkv[which]).astype(b16)
                 pk_q[at, 0, which] = value[:cut]
@@ -1165,12 +1310,17 @@
     def note(row, values):
         small_acc[row : row + 1, :] += jnp.sum(values, axis=0, keepdims=True)
 
+    norms[...] = jnp.zeros_like(norms)
+    for kind in range(ROWS_MAT):
+        for which in range(3):
+            lamb_load(kind, LAYERS - 1, which).start()
+    load_c.wait()
     for layer in reversed(range(LAYERS)):
         last = layer + 1 == LAYERS
         base = layer * 8
         for which in range(2):
             at = pl.ds(which * half, half)
-            upstream = cotangent[at, :].astype(f32) if last else d_own[at, :]
+            upstream = sum_chip[at, :].astype(f32) if last else grad_hidden[at, :]
             down, unit = norm_back(y_own[layer, at, :], upstream, vec_row(layer, 1))
             note(base + 1, upstream * unit)
             note(base + 7, upstream)
@@ -1178,13 +1328,15 @@
             d_keep[at, :] = down
             m_full[own_rows(which), :] = down.astype(b16)
             gat_start(m_full, which)
-        if not last:
-            g_mid(0, layer + 1)
+        marks = BACK_SLOTS[0 if last else 1]
+        add_upto(layer, marks[0])
         gat_end(m_full)
         if not last:
             g_free(3, layer + 1)
             g_end(3, layer + 1)
         grad_back(layer)
+        lamb_more(3, layer)
+        add_upto(layer, marks[1])
 
         def slope_tile(tile, carry):
             at = tile_cols(tile)
@@ -1198,12 +1350,16 @@
 
         lax.fori_loop(0, hidden_cols // TILE, slope_tile, 0)
         sum_start(lambda tile: dot_nt(active[...], w_i[layer, tile_cols(tile), :]))
+        add_upto(layer, marks[2])
         if not last:
             g_free(2, layer + 1)
             g_end(2, layer + 1)
         grad_in(layer)
-        g_mid(3, layer)
+        lamb_more(2, layer)
+        add_upto(layer, marks[3])
         sum_end()
+        if last:
+            out_hidden.wait()
         for which in range(2):
             at = pl.ds(which * half, half)
             upstream = sum_rows(which) + d_keep[at, :]
@@ -1214,25 +1370,27 @@
             d_keep[at, :] = down
             h_full[own_rows(which), :] = down.astype(b16)
             gat_start(h_full, which)
+        add_upto(layer, marks[4])
+        gat_end(h_full)
         if not last:
             g_free(1, layer + 1)
             g_end(1, layer + 1)
-        gat_end(h_full)
-        d_attn[...] = dot_nt(h_full[...], w_o[layer]).astype(b16)
+        attn[...] = dot_nt(h_full[...], w_o[layer]).astype(b16)
         grad_out(layer)
+        lamb_more(1, layer)
         if last:
             out_logits.wait()
-        g_mid(2, layer)
-        attend_back(layer, last)
+        add_upto(layer, marks[5])
+        attend_back(layer, last, (0,))
+        add_upto(layer, marks[6])
+        attend_back(layer, last, (1,))
+        add_upto(layer, marks[7])
         small_acc[base + 2 : base + 3, own_cols] = jnp.sum(
             d_qkv[0].astype(f32), axis=0, keepdims=True
         )
         small_acc[base + 3 : base + 4, own_cols] = jnp.sum(
             d_qkv[2].astype(f32), axis=0, keepdims=True
         )
-        if not last:
-            g_free(0, layer + 1)
-            g_end(0, layer + 1)
 
         def input_tile(tile):
             rows = tile_cols(tile)
@@ -1241,16 +1399,17 @@
             return total + dot_nt(d_qkv[2], w_q[layer, 2, rows, :])
 
         sum_start(input_tile)
+        if not last:
+            g_free(0, layer + 1)
+            g_end(0, layer + 1)
         grad_qkv(layer)
-        g_mid(1, layer)
+        lamb_more(0, layer)
+        add_upto(layer, marks[8])
         sum_end()
         for which in range(2):
             at = pl.ds(which * half, half)
             result = sum_rows(which) + d_keep[at, :]
-            if layer:
-                d_own[at, :] = result
-            else:
-                grad_hidden[at, :] = result
+            grad_hidden[at, :] = result
 
     out_scores = pltpu.make_async_copy(scores, grad_scores, out_sem.at[1])
     out_scores.start()
@@ -1269,7 +1428,7 @@
 
     for step in range(1, 4):
         small_one(step).start()
-    g_mid(0, 0)
+    add_upto(0, BACK_SLOTS[2][0])
     for step in range(1, 4):
         small_one(step).wait_recv()
     mat_rows = LAYERS * 8
@@ -1315,10 +1474,72 @@
     for step in range(1, 4):
         small_one(step).wait_send()
     g_end(0, 0)
+
+    row_at = lax.broadcasted_iota(jnp.int32, (24, LANES), 0)
+    lane_at = lax.broadcasted_iota(jnp.int32, (24, LANES), 1)
+    in_share = (row_at >= mat_rows) | (lane_at // (width // data_parts // 4) == ten)
+    small_grad = jnp.where(in_share & (row_at < mat_rows + LAYERS), small_out[...], 0.0)
+    small_step = lamb_update(small_in[0, 0:24], small_in[1, 0:24], small_in[2, 0:24], small_grad, 0.0)
+    norm_send[0:mat_rows, :] = jnp.broadcast_to(
+        jnp.sum(norms[...], axis=-1, keepdims=True), (mat_rows, LANES)
+    )
+    for layer in range(LAYERS):
+        for group, rows in enumerate(
+            (slice(layer * 8, layer * 8 + 8), slice(mat_rows + layer, mat_rows + layer + 1))
+        ):
+            for which, values in enumerate((small_in[0, rows], small_step[rows])):
+                total = jnp.sum(
+                    jnp.sum(values * values, axis=0, keepdims=True), axis=1, keepdims=True
+                )
+                row = mat_rows + (layer * 2 + group) * 2 + which
+                norm_send[row : row + 1, :] = jnp.broadcast_to(total, (1, LANES))
+
+    def norm_one(step):
+        return rdma(
+            norm_send,
+            norm_ten.at[ten],
+            ns_sem.at[step - 1],
+            nr_sem.at[step - 1],
+            dp,
+            lax.rem(ten + step, 4),
+        )
+
+    def norm_two(step):
+        return rdma(
+            norm_mid,
+            norm_dp.at[dp],
+            ns_sem.at[2 + step],
+            nr_sem.at[2 + step],
+            lax.rem(dp + step, data_parts),
+            ten,
+        )
+
+    norm_ten[ten] = norm_send[...]
+    for step in range(1, 4):
+        norm_one(step).start()
+    for step in range(1, 4):
+        norm_one(step).wait_recv()
+    total = norm_ten[0]
+    for other in range(1, 4):
+        total = total + norm_ten[other]
+    norm_mid[...] = total
+    norm_dp[dp] = total
+    for step in range(1, data_parts):
+        norm_two(step).start()
     for kind in range(ROWS_MAT):
         g_free(kind, 0)
         fin_copy(kind, 0).wait()
     out_scores.wait()
+    for step in range(1, 4):
+        norm_one(step).wait_send()
+    for step in range(1, data_parts):
+        norm_two(step).wait_recv()
+    total = norm_dp[0]
+    for other in range(1, data_parts):
+        total = total + norm_dp[other]
+    norm_out[...] = total
+    for step in range(1, data_parts):
+        norm_two(step).wait_send()
 
 
 def fits(parts, head_cols, hidden_cols, heads_here, tokens, width, blocks):
@@ -1369,15 +1590,27 @@
     seq_span = jnp.where(bucket == 0, tokens // 4, jnp.where(bucket == 1, tokens // 2, tokens))
     seq_of = jnp.arange(tokens, dtype=jnp.int32) // seq_span
     live = (key_mask == 1) & (seq_of < seq_counts[0])
-    row_ids = jnp.broadcast_to(seq_of.astype(f32)[:, None], (tokens, LANES))
-    key_ids = jnp.broadcast_to(jnp.where(live, seq_of, -1).astype(f32)[None, :], (8, tokens))
+    key_ids = jnp.where(
+        jnp.arange(16, dtype=jnp.int32)[:, None] < 8,
+        jnp.where(live, seq_of, -1).astype(f32)[None, :],
+        1.0 / seq_span.astype(f32),
+    )
     owned = vectors.shape[2]
-    spread = jnp.tile(vectors.reshape(LAYERS * 8, owned), (1, LANES // owned))
     mine = (jnp.arange(LANES, dtype=jnp.int32) // owned) == ten
-    spread = jnp.where(mine[None, :], spread, 0.0)
-    small_in = jnp.concatenate(
-        [spread, bias_in, jnp.zeros((32 - LAYERS * 9, LANES), f32)], axis=0
-    ).astype(b16)
+
+    def small_rows(wide, narrow, fill):
+        rows = jnp.tile(wide.reshape(LAYERS * 8, owned), (1, LANES // owned))
+        rows = jnp.where(mine[None, :], rows, fill)
+        rest = jnp.full((32 - LAYERS * 9, LANES), fill, f32)
+        return jnp.concatenate([rows, narrow, rest], axis=0)
+
+    small_in = jnp.stack(
+        [
+            small_rows(vectors, bias_in, 0.0),
+            small_rows(arrays[16], arrays[17], 0.0),
+            small_rows(arrays[22], arrays[23], 1.0),
+        ]
+    )
 
     hbm = pl.BlockSpec(memory_space=pl.ANY)
     vmem = pl.BlockSpec(memory_space=pltpu.VMEM)
@@ -1399,9 +1632,9 @@
             shape((heads, tokens, tokens), b16),
         )
         + tuple(shape((n,) + size, f32) for size in grad_shapes)
-        + (shape((24, LANES), f32),),
-        in_specs=[hbm, hbm, vmem, vmem, vmem, vmem, hbm, hbm, hbm, hbm],
-        out_specs=(vmem, hbm, vmem, hbm, hbm, hbm, hbm, hbm, vmem),
+        + (shape((24, LANES), f32),) * 2,
+        in_specs=[hbm, hbm, hbm, vmem, vmem] + [hbm] * 16,
+        out_specs=(hbm, hbm, vmem, hbm, hbm, hbm, hbm, hbm, vmem, vmem),
         scratch_shapes=[
             pltpu.VMEM((n, 3, width, head_cols), b16),
             pltpu.VMEM((n, head_cols, width), b16),
@@ -1422,8 +1655,6 @@
             pltpu.VMEM((n, share, width), f32),
             pltpu.VMEM((n, share, width), f32),
             pltpu.VMEM((3, tokens, head_cols), b16),
-            pltpu.VMEM((tokens, head_cols), b16),
-            pltpu.VMEM((share, width), f32),
             pltpu.VMEM((share, width), f32),
             pltpu.VMEM((LANES, tokens), f32),
             pltpu.VMEM((LANES, tokens), f32),
@@ -1442,12 +1673,19 @@
         + [pltpu.VMEM((cols_n, 2) + size, b16) for size in grad_shapes]
         + [pltpu.VMEM((n, cols_n) + size, b16) for size in grad_shapes]
         + [pltpu.VMEM((n, cols_n - 1) + size, b16) for size in grad_shapes]
-        + [pltpu.VMEM(size, f32) for size in grad_shapes]
+        + [pltpu.VMEM(size, f32) for _ in range(3) for size in grad_shapes]
+        + [
+            pltpu.VMEM((n * 8, width), f32),
+            pltpu.VMEM((24, LANES), f32),
+            pltpu.VMEM((4, 24, LANES), f32),
+            pltpu.VMEM((24, LANES), f32),
+            pltpu.VMEM((data_parts, 24, LANES), f32),
+        ]
         + [
             dma((2,)),
             dma((n, 4)),
-            dma((n, 4, cols_n - 1)),
-            dma((n, 4, cols_n - 1)),
+            dma((n, 4, cols_n, 2, 2)),
+            dma((n, 4, cols_n, 2)),
             dma((n, 4, cols_n)),
             dma((n, 4, cols_n)),
             dma((width // TILE, 2)),
@@ -1465,7 +1703,10 @@
             dma((4, cols_n - 1)),
             dma((n, 4, cols_n - 1)),
             dma((4,)),
-            dma((2,)),
+            dma((4,)),
+            dma((3, 4)),
+            dma((data_parts + 2,)),
+            dma((data_parts + 2,)),
         ],
         compiler_params=pltpu.CompilerParams(
             collective_id=0, has_side_effects=True, vmem_limit_bytes=63 * 1024 * 1024
@@ -1474,13 +1715,15 @@
         hidden_in,
         logits_in,
         cotangent,
-        row_ids,
         key_ids,
         small_in,
         w_qkv.astype(b16),
         w_out.astype(b16),
         w_in.astype(b16),
         w_back.astype(b16),
+        *arrays[6:10],
+        *arrays[12:16],
+        *arrays[18:22],
     )
     hidden_out, logits_out, grad_hidden, grad_scores = results[:4]
     small = results[8]
@@ -1502,14 +1745,12 @@
             + decay_rate * master
         )
         moved.append((moment_one, update))
-    weight_sq = jnp.stack(
-        [jnp.sum((master * master).reshape(LAYERS, -1), axis=1) for master in masters]
-    )
-    update_sq = jnp.stack(
-        [jnp.sum((moved_one[1] * moved_one[1]).reshape(LAYERS, -1), axis=1) for moved_one in moved]
-    )
-    weight_tot, update_tot = lax.psum((weight_sq, update_sq), ("dp", "tensor"))
-    trust_all = jnp.sqrt(weight_tot) / jnp.sqrt(update_tot)
+    norms = jnp.sqrt(results[9][:, 0])
+    trust_rows = norms[0::2] / norms[1::2]
+    trust_all = jnp.concatenate(
+        [trust_rows[: LAYERS * 4].reshape(LAYERS, 4), trust_rows[LAYERS * 4 :].reshape(LAYERS, 2)],
+        axis=1,
+    ).T
     new_params = tuple(
         (
             master

time: 461 us -> 371 us (0.80)
  Pallas kernels: 375 us -> 334 us
  blocking collectives: 38.7 us -> 0 us
  other arithmetic: 34.2 us -> 22.8 us
    pallas_call x1, Pallas kernels: 375 us -> 334 us  [shards(): pl.pallas_call(functools.partial(step_kernel, data_parts), out_shape=(sha...]
    psum x1 -> x0, blocking collectives: 38.7 us -> none  [shards(): weight_tot, update_tot = lax.psum((weight_sq, update_sq), ('dp', 'tensor'))]
    reduce_sum x11 -> x0, other arithmetic: 21.4 us -> none  [the longest x6 14.4 us: shards(): jnp.sum((moved_one[1] * moved_one[1]).reshape(LAYERS, -1), axis=1)]
    convert_element_type x0 -> x4, other arithmetic: none -> 5.27 us  [the longest x1 1.92 us: shards(): w_qkv.astype(b16)]
where the time goes in v2:
time: 371 us; the launch traced here: 370 us
  Pallas kernels  334 us (90%)
  other arithmetic  22.8 us (6%)
  local copies, waits for them, and re-layouts  10.5 us (3%)
    pallas_call x1, Pallas kernels, shards(): pl.pallas_call(functools.partial(step_kernel, data_parts), out_shape=(sha...  334 us
    sub x6, other arithmetic, shards(): master - LEARN_RATE * trust_all[group_at].reshape((LAYERS,) + (1,) * (mas...  9.29 us

profile of v2, /device:TPU:0, one launch (start us, length us, event | category | flops | bytes accessed | tf_op | source)
XLA Modules:
  0.0 370.0 jit_solution(17224139383645068889)
XLA Ops:
  2.2 0.8 select_convert_fusion
  3.7 0.7 tile.31
  4.5 0.7 tile.34
  5.3 0.7 tile.37
  6.2 0.8 maximum_bitcast_fusion
  7.6 1.9 convert_element_type.26.own_qkv
  9.5 1.6 convert_element_type.27.own_out
  11.2 0.9 convert_element_type.28.own_in
  12.0 0.9 convert_element_type.29.own_back
  12.9 334.2 %shard_map.407 = (bf16[128,1024]{1,0:T(8,128)(2,1)}, bf16[4,512,512]{2,1,0:T(8,128)(2,1)}, f32[128,1024]{1,0:T(8,128)}, bf16[4,512,512]{2,1,0:T(8,128)(2,1)}, f3...) custom-call(bf16[512,1024]{1,0:T(8,128)(2,1)} %hidden_in.1, ...), custom_call_target="tpu_custom_call" | custom-call | tf_op jit(solution)/shard_map/pallas_call | solution.py:1626
  347.3 4.3 %bitcast_convert_fusion = f32[1,4,512,512]{3,2,1,0:T(8,128)} fusion(bf16[4,512,512]{2,1,0:T(8,128)(2,1)} %get-tuple-element.36), kind=kLoop, calls=%fused_computation | loop fusion | flops 1048576 | bytes 6291456 | tf_op jit(solution)/shard_map/convert_element_type | solution.py:1764
  352.6 0.7 fusion.31
  354.0 1.7 multiply_subtract_fusion.2
  355.8 2.1 multiply_subtract_fusion.3
  358.0 2.1 multiply_subtract_fusion.1
  360.1 0.7 copy-done.10
  360.8 2.1 multiply_subtract_fusion
  363.5 0.7 copy.56
  364.3 1.3 copy.57
  365.6 0.8 copy.58
  366.4 0.9 copy.59
  367.3 0.7 copy.60
  368.0 1.0 copy.61
  369.0 1.0 copy.62
  (81 shorter events, 4.2 us)
Async XLA Ops:
  0.7 10.5 %copy-start = (f32[2,128,1024]{2,1,0:T(8,128)S(1)}, f32[2,128,1024]{2,1,0:T(8,128)}, u32[]{:S(2)}) copy-start(f32[2,128,1024]{2,1,0:T(8,128)} %lw_in.1) | copy-start | bytes 3145732
  0.7 11.4 %copy-start.2 = (f32[2,1024,128]{2,1,0:T(8,128)S(1)}, f32[2,1024,128]{2,1,0:T(8,128)}, u32[]{:S(2)}) copy-start(f32[2,1024,128]{2,1,0:T(8,128)} %lw_back.1) | copy-start | bytes 3145732
  347.1 4.5 %copy-start.24 = (f32[24,128]{1,0:T(8,128)S(1)}, f32[24,128]{1,0:T(8,128)}, u32[]{:S(2)}) copy-start(f32[24,128]{1,0:T(8,128)} %get-tuple-element.42) | copy-start | bytes 36868
  347.1 5.4 %copy-start.25 = (f32[24,128]{1,0:T(8,128)S(1)}, f32[24,128]{1,0:T(8,128)}, u32[]{:S(2)}) copy-start(f32[24,128]{1,0:T(8,128)} %get-tuple-element.41) | copy-start | bytes 36868
  347.2 5.4 %copy-start.21 = (f32[2,8,32]{2,1,0:T(8,128)S(1)}, f32[2,8,32]{2,1,0:T(8,128)}, u32[]{:S(2)}) copy-start(f32[2,8,32]{2,1,0:T(8,128)} %param.34) | copy-start | bytes 6148
  347.2 5.4 %copy-start.22 = (f32[2,8,32]{2,1,0:T(8,128)S(1)}, f32[2,8,32]{2,1,0:T(8,128)}, u32[]{:S(2)}) copy-start(f32[2,8,32]{2,1,0:T(8,128)} %param.40) | copy-start | bytes 6148
  347.2 5.4 %copy-start.23 = (f32[2,8,32]{2,1,0:T(8,128)S(1)}, f32[2,8,32]{2,1,0:T(8,128)}, u32[]{:S(2)}) copy-start(f32[2,8,32]{2,1,0:T(8,128)} %param.46) | copy-start | bytes 6148
  347.2 6.1 %copy-start.26 = (f32[2,128]{1,0:T(2,128)S(1)}, f32[2,128]{1,0:T(2,128)}, u32[]{:S(2)}) copy-start(f32[2,128]{1,0:T(2,128)} %param.35) | copy-start | bytes 3076
  347.2 6.1 %copy-start.27 = (f32[2,128]{1,0:T(2,128)S(1)}, f32[2,128]{1,0:T(2,128)}, u32[]{:S(2)}) copy-start(f32[2,128]{1,0:T(2,128)} %param.41) | copy-start | bytes 3076
  347.2 6.1 %copy-start.28 = (f32[2,128]{1,0:T(2,128)S(1)}, f32[2,128]{1,0:T(2,128)}, u32[]{:S(2)}) copy-start(f32[2,128]{1,0:T(2,128)} %param.47) | copy-start | bytes 3076
  347.2 6.7 %copy-start.4 = (f32[2,3,128,256]{3,2,1,0:T(8,128)S(1)}, f32[2,3,128,256]{3,2,1,0:T(8,128)}, u32[]{:S(2)}) copy-start(f32[2,3,128,256]{3,2,1,0:T(8,128)} %lw_qkv.1) | copy-start | bytes 2359300
  347.2 6.7 %copy-start.11 = (f32[2,3,128,256]{3,2,1,0:T(8,128)S(1)}, f32[2,3,128,256]{3,2,1,0:T(8,128)}, u32[]{:S(2)}) copy-start(f32[2,3,128,256]{3,2,1,0:T(8,128)} %lm_qkv.1) | copy-start | bytes 2359300
  347.2 6.7 %copy-start.12 = (f32[2,3,128,256]{3,2,1,0:T(8,128)S(1)}, f32[2,3,128,256]{3,2,1,0:T(8,128)}, u32[]{:S(2)}) copy-start(f32[2,3,128,256]{3,2,1,0:T(8,128)} %lv_qkv.1) | copy-start | bytes 2359300
  347.3 6.7 %copy-start.13 = (f32[2,3,128,256]{3,2,1,0:T(8,128)S(1)}, f32[2,3,128,256]{3,2,1,0:T(8,128)}, u32[]{:S(2)}) copy-start(f32[2,3,128,256]{3,2,1,0:T(8,128)} %get-tuple-element.96) | copy-start | bytes 2359300
  347.3 8.5 %copy-start.17 = (f32[2,256,128]{2,1,0:T(8,128)S(1)}, f32[2,256,128]{2,1,0:T(8,128)}, u32[]{:S(2)}) copy-start(f32[2,256,128]{2,1,0:T(8,128)} %lv_out.1) | copy-start | bytes 786436
  354.0 3.9 %copy-start.1 = (f32[2,128,1024]{2,1,0:T(8,128)S(1)}, f32[2,128,1024]{2,1,0:T(8,128)}, u32[]{:S(2)}) copy-start(f32[2,128,1024]{2,1,0:T(8,128)} %lw_in.1) | copy-start | bytes 3145732
  354.0 3.9 %copy-start.6 = (f32[2,128,1024]{2,1,0:T(8,128)S(1)}, f32[2,128,1024]{2,1,0:T(8,128)}, u32[]{:S(2)}) copy-start(f32[2,128,1024]{2,1,0:T(8,128)} %get-tuple-element.98) | copy-start | bytes 3145732
  354.0 3.9 %copy-start.7 = (f32[2,128,1024]{2,1,0:T(8,128)S(1)}, f32[2,128,1024]{2,1,0:T(8,128)}, u32[]{:S(2)}) copy-start(f32[2,128,1024]{2,1,0:T(8,128)} %lm_in.1) | copy-start | bytes 3145732
  354.0 3.9 %copy-start.8 = (f32[2,128,1024]{2,1,0:T(8,128)S(1)}, f32[2,128,1024]{2,1,0:T(8,128)}, u32[]{:S(2)}) copy-start(f32[2,128,1024]{2,1,0:T(8,128)} %lv_in.1) | copy-start | bytes 3145732
  357.9 2.1 copy-start.3
  357.9 2.2 copy-start.9
  357.9 2.9 copy-start.10
  360.8 2.7 copy-start.20
  360.8 3.4 copy-start.15
  (5 other events, 8.7 us)

commit v3 on v2

--- a/solution.py
+++ b/solution.py
@@ -471,10 +471,11 @@
 TILE = 256
 LANES = 128
 ROWS_MAT = 4
-X_FIRST = 9
+X_FIRST = (1,)
 Z_AHEAD = 2
 X_AHEAD = 3
 SLOTS = ((1, 3), (2, 1), (2, 3), (3, 1), (3, 2), (4, 1), (5, 1))
+Z_FIRST = ()
 BACK_SLOTS = (
     (-9, -9, 0, 1, 2, 3, 4, 5, 6),
     (-9, -5, -4, -2, 0, 0, 1, 2, 3),
@@ -505,12 +506,15 @@
     hidden_in,
     logits_in,
     cotangent,
-    key_ids,
-    small_in,
-    own_qkv,
-    own_out,
-    own_in,
-    own_back,
+    bucket,
+    count,
+    key_mask,
+    vec_w,
+    bias_w,
+    vec_m,
+    bias_m,
+    vec_v,
+    bias_v,
     lw_qkv,
     lw_out,
     lw_in,
@@ -533,6 +537,8 @@
     sum_back,
     small_out,
     norm_out,
+    key_ids,
+    small_in,
     w_q,
     w_o,
     w_i,
@@ -620,6 +626,7 @@
     lamb_sem,
     ns_sem,
     nr_sem,
+    credit,
 ):
     dp = lax.axis_index("dp")
     ten = lax.axis_index("tensor")
@@ -668,20 +675,29 @@
             return w_i.at[layer, at, :]
         return w_b.at[layer, :, at]
 
-    owns = (own_qkv, own_out, own_in, own_back)
-
     load_h = pltpu.make_async_copy(hidden_in, h_full, load_sem.at[0])
     load_s = pltpu.make_async_copy(logits_in.at[0], scores, load_sem.at[1])
     load_h.start()
     load_s.start()
-    own_loads = []
+    masters = (
+        (lw_qkv, lw_out, lw_in, lw_back),
+        (lm_qkv, lm_out, lm_in, lm_back),
+        (lv_qkv, lv_out, lv_in, lv_back),
+    )
+    held = ((fw_q, fw_o, fw_i, fw_b), (fm_q, fm_o, fm_i, fm_b), (fv_q, fv_o, fv_i, fv_b))
+
+    def lamb_load(kind, layer, which):
+        return pltpu.make_async_copy(
+            masters[which][kind].at[layer], held[which][kind], lamb_sem.at[which, kind]
+        )
+
+    def own_load(kind, layer):
+        to = LAYERS - 1 - layer
+        return pltpu.make_async_copy(masters[0][kind].at[layer], held[to][kind], own_sem.at[layer, kind])
+
     for layer in range(LAYERS):
         for kind in range(ROWS_MAT):
-            copy = pltpu.make_async_copy(
-                owns[kind].at[layer], region(kind, layer, dp), own_sem.at[layer, kind]
-            )
-            copy.start()
-            own_loads.append(copy)
+            own_load(kind, layer).start()
 
     barrier = pltpu.get_barrier_semaphore()
 
@@ -696,10 +712,139 @@
         pl.semaphore_signal(
             barrier, inc=1, device_id=(dp, lax.rem(ten + other, 4)), device_id_type=MESH
         )
+
+    def w_x(kind, layer, from_place, col):
+        dst = region(kind, layer, from_place * 2 + col)
+        return rdma(
+            dst,
+            dst,
+            xs_sem.at[layer, kind, from_place],
+            xr_sem.at[layer, kind, from_place],
+            across,
+            ten,
+        )
+
+    def w_z(kind, layer, from_place, col, way):
+        dst = region(kind, layer, from_place * 2 + col)
+        which = lax.rem(col + side, 2)
+        return rdma(
+            dst,
+            dst,
+            zs_sem.at[layer, kind, from_place, which, (way + 1) // 2],
+            zr_sem.at[layer, kind, from_place, which],
+            dp + 2 * way,
+            ten,
+        )
+
+    can_go = {1: place < cols_n - 1, -1: place > 0}
+
+    def w_both_ways(kind, layer, col):
+        for way in (1, -1):
+
+            @pl.when(can_go[way])
+            def _():
+                w_z(kind, layer, place, col, way).start()
+
+    def w_far(kind, layer, col, step):
+        dst = region(kind, layer, place * 2 + col)
+        which = lax.rem(col + side, 2)
+        return rdma(
+            dst,
+            dst,
+            zs_sem.at[layer, kind, step, which, 0],
+            zr_sem.at[layer, kind, step, which],
+            along(step),
+            ten,
+        )
+
+    def w_event(kind, layer, hop):
+        if kind in X_FIRST:
+            w_x(kind, layer, place, 1 - side).wait_recv()
+            for step in range(1, cols_n):
+                w_far(kind, layer, 1 - side, step).start()
+            return
+        for way in (1, -1):
+            came = place - hop * way
+
+            @pl.when(came >= 0 if way == 1 else came < cols_n)
+            def _():
+                w_z(kind, layer, came, side, way).wait_recv()
+
+                @pl.when(can_go[way])
+                def _():
+                    w_z(kind, layer, came, side, way).start()
+
+                w_x(kind, layer, came, side).start()
+
+    order = [(kind, layer) for layer in range(LAYERS) for kind in range(ROWS_MAT)]
+
+    def w_own_z(index):
+        if index < len(order):
+            kind, layer = order[index]
+            if kind in X_FIRST:
+                for step in range(1, cols_n):
+                    w_far(kind, layer, side, step).start()
+            else:
+                w_both_ways(kind, layer, side)
+
+    def w_own_x(index):
+        if index < len(order):
+            w_x(*order[index], place, side).start()
+
+    def w_own(index):
+        kind, layer = order[index]
+        own_load(kind, layer).wait()
+        mine = region(kind, layer, dp)
+        mine[...] = held[LAYERS - 1 - layer][kind][...].astype(b16)
+
+    for index in range(X_AHEAD):
+        w_own(index)
+    for kind, slots in enumerate((rz_q, rz_o, rz_i, rz_b)):
+        if kind in Z_FIRST:
+            continue
+
+        @pl.when(place == 0)
+        def _():
+            slots[1 : cols_n + 1] = jnp.zeros((cols_n,) + slots.shape[1:], b16)
+
+        @pl.when(place == cols_n - 1)
+        def _():
+            slots[0:cols_n] = jnp.zeros((cols_n,) + slots.shape[1:], b16)
+
+    owned = vec_w.shape[2]
+    spread_row = lax.broadcasted_iota(jnp.int32, (owned, LANES), 0)
+    spread_col = lax.broadcasted_iota(jnp.int32, (owned, LANES), 1)
+    spread = jnp.where(spread_row + ten * owned == spread_col, 1.0, 0.0)
+    lane_row = lax.broadcasted_iota(jnp.int32, (1, LANES), 1)
+    not_owned = jnp.where(lane_row // owned == ten, 0.0, 1.0)
+    small_in[...] = jnp.zeros_like(small_in)
+    small_in[2] = jnp.ones_like(small_in[2])
+    for which, (wide, narrow) in enumerate(((vec_w, bias_w), (vec_m, bias_m), (vec_v, bias_v))):
+        for layer in range(LAYERS):
+            rows = lax.dot_general(
+                wide[layer],
+                spread,
+                (((1,), (0,)), ((), ())),
+                precision=lax.Precision.HIGHEST,
+                preferred_element_type=jnp.float32,
+            )
+            if which == 2:
+                rows = rows + not_owned
+            small_in[which, layer * 8 : layer * 8 + 8, :] = rows
+            small_in[which, LAYERS * 8 + layer : LAYERS * 8 + layer + 1, :] = narrow[
+                layer : layer + 1, :
+            ]
+    vec_got[ten, dp] = small_in[0].astype(b16)
+    span_of = (tokens // 4, tokens // 2, tokens)
+    per_key = jnp.where(
+        bucket[0] == 0, 1.0 / span_of[0], jnp.where(bucket[0] == 1, 1.0 / span_of[1], 1.0 / span_of[2])
+    ).astype(f32)
+    key_at = lax.broadcasted_iota(jnp.int32, (1, tokens), 1).astype(f32)
+    key_seq = jnp.floor(key_at * per_key)
+    alive = (key_mask[...] == 1) & (key_seq < count[0].astype(f32))
+    key_ids[0:1, :] = jnp.where(alive, key_seq, -1.0)
+
     pl.semaphore_wait(barrier, data_parts + 2)
-
-    vec_got[ten, dp] = small_in[0].astype(b16)
-
     def vec_one(step):
         return rdma(
             vec_got.at[ten, dp],
@@ -716,76 +861,18 @@
 
     lax.fori_loop(1, data_parts, vec_go, 0)
 
-    def w_x(kind, layer, from_place, col, own=False):
-        dst = region(kind, layer, from_place * 2 + col)
-        return rdma(
-            owns[kind].at[layer] if own else dst,
-            dst,
-            xs_sem.at[layer, kind, from_place],
-            xr_sem.at[layer, kind, from_place],
-            across,
-            ten,
-        )
-
-    def w_z(kind, layer, from_place, col, way, own=False):
-        dst = region(kind, layer, from_place * 2 + col)
-        which = lax.rem(col + side, 2)
-        return rdma(
-            owns[kind].at[layer] if own else dst,
-            dst,
-            zs_sem.at[layer, kind, from_place, which, (way + 1) // 2],
-            zr_sem.at[layer, kind, from_place, which],
-            dp + 2 * way,
-            ten,
-        )
-
-    can_go = {1: place < cols_n - 1, -1: place > 0}
-
-    def w_both_ways(kind, layer, col, own=False):
-        for way in (1, -1):
-
-            @pl.when(can_go[way])
-            def _():
-                w_z(kind, layer, place, col, way, own).start()
-
-    def w_event(kind, layer, hop):
-        if hop == 0:
-            w_x(kind, layer, place, 1 - side).wait_recv()
-            w_both_ways(kind, layer, 1 - side)
-            return
-        for way in (1, -1):
-            came = place - hop * way
-
-            @pl.when(came >= 0 if way == 1 else came < cols_n)
-            def _():
-                for col in (side, 1 - side) if kind == X_FIRST else (side,):
-                    w_z(kind, layer, came, col, way).wait_recv()
-
-                    @pl.when(can_go[way])
-                    def _():
-                        w_z(kind, layer, came, col, way).start()
-
-                    if kind != X_FIRST:
-                        w_x(kind, layer, came, side).start()
-
-    order = [(kind, layer) for layer in range(LAYERS) for kind in range(ROWS_MAT)]
-
-    def w_own_z(index):
-        if index < len(order):
-            w_both_ways(*order[index], side, True)
-
-    def w_own_x(index):
-        if index < len(order):
-            w_x(*order[index], place, side, True).start()
-
-    for index in range(Z_AHEAD):
-        w_own_z(index)
     for index in range(X_AHEAD):
+        if index < Z_AHEAD:
+            w_own_z(index)
         w_own_x(index)
+
+    for index in range(X_AHEAD, len(order)):
+        w_own(index)
+
     events = [
         (index, hop)
         for index in range(len(order))
-        for hop in range(0 if order[index][0] == X_FIRST else 1, cols_n)
+        for hop in range(1, 2 if order[index][0] in X_FIRST else cols_n)
     ]
     passed = [0]
 
@@ -794,34 +881,39 @@
         while passed[0] < len(events) and events[passed[0]] <= goal:
             index, hop = events[passed[0]]
             w_event(*order[index], hop)
-            if hop == cols_n - 1:
+            if hop == cols_n - 1 or order[index][0] in X_FIRST:
                 w_own_z(index + Z_AHEAD)
                 w_own_x(index + X_AHEAD)
             passed[0] += 1
 
     def have(layer, kind):
         pass_on(layer, kind, cols_n)
-        if kind != X_FIRST:
+        if kind in X_FIRST:
+            for step in range(1, cols_n):
+                for col in (side, 1 - side):
+                    w_far(kind, layer, col, step).wait_recv()
+        else:
             for from_place in range(cols_n):
                 w_x(kind, layer, from_place, 1 - side).wait_recv()
 
     def w_finish():
         for kind, layer in order:
+            if kind in X_FIRST:
+                w_x(kind, layer, place, side).wait_send()
+                for step in range(1, cols_n):
+                    for col in (side, 1 - side):
+                        w_far(kind, layer, col, step).wait_send()
+                continue
             for from_place in range(cols_n):
-                if kind != X_FIRST:
-                    w_x(kind, layer, from_place, side).wait_send()
-                for col in (side, 1 - side) if kind == X_FIRST else (side,):
-
-                    @pl.when(can_go[1] & (from_place <= place))
-                    def _():
-                        w_z(kind, layer, from_place, col, 1).wait_send()
-
-                    @pl.when(can_go[-1] & (from_place >= place))
-                    def _():
-                        w_z(kind, layer, from_place, col, -1).wait_send()
-
-            if kind == X_FIRST:
-                w_x(kind, layer, place, side).wait_send()
+                w_x(kind, layer, from_place, side).wait_send()
+
+                @pl.when(can_go[1] & (from_place <= place))
+                def _():
+                    w_z(kind, layer, from_place, side, 1).wait_send()
+
+                @pl.when(can_go[-1] & (from_place >= place))
+                def _():
+                    w_z(kind, layer, from_place, side, -1).wait_send()
 
     def vec_wait(step, carry):
         vec_one(step).wait_send()
@@ -986,7 +1078,7 @@
             keys = qkv[layer, 1, :, at]
             values = qkv[layer, 2, :, at]
             row = lax.broadcasted_iota(jnp.int32, (score_rows, 1), 0) + step * score_rows
-            allowed = jnp.floor(row.astype(f32) * key_ids[8:9, 0:1]) == key_ids[0:1, :]
+            allowed = jnp.floor(row.astype(f32) * per_key) == key_ids[0:1, :]
             mixed = jnp.zeros((score_rows, LANES), f32)
             for head in range(2):
                 raw = dot_nt(queries, keys * lane_masks[head])
@@ -1047,8 +1139,6 @@
     own_cols = pl.ds(mult(ten * head_cols, head_cols), head_cols)
     small_acc[...] = jnp.zeros_like(small_acc)
     load_h.wait()
-    for copy in own_loads:
-        copy.wait()
     load_s.wait()
     for layer in range(LAYERS):
         have(layer, 0)
@@ -1126,33 +1216,112 @@
     got_z = (rz_q, rz_o, rz_i, rz_b)
     sums = (sum_qkv, sum_out, sum_in, sum_back)
 
-    def g_x(kind, layer, at):
+    def turn_of(turn_at):
+        upper = place // 2
+        near = upper * (cols_n - 1) + (1 - 2 * upper) * place
+        swing = lax.rem(3 + turn_at + turn_at * (turn_at - 1) // 2, 4)
+        at = (1 - near) * (3 - turn_at) + near * swing
+        return upper * (cols_n - 1) + (1 - 2 * upper) * at
+
+    def is_up(at):
+        return (at - place + cols_n) // cols_n
+
+    def g_x(kind, at):
+        first = kind not in Z_FIRST
         return rdma(
             packs[kind].at[at, 1 - side],
-            got_x[kind].at[layer, at],
+            got_x[kind].at[at if first else 0],
             gxs_sem.at[kind, at],
-            gxr_sem.at[layer, kind, at],
+            gxr_sem.at[kind, at],
             across,
             ten,
         )
 
-    def g_z(kind, layer, step):
+    def g_z(kind, at):
+        up = is_up(at)
+        return rdma(
+            packs[kind].at[at, side],
+            got_z[kind].at[at + up],
+            gzs_sem.at[kind, at],
+            gzr_sem.at[kind, at + up],
+            dp + 2 * (2 * up - 1),
+            ten,
+        )
+
+    def g_z_came(kind, at, up):
+        copy = rdma(
+            packs[kind].at[at, side],
+            got_z[kind].at[at + up],
+            gzs_sem.at[kind, at],
+            gzr_sem.at[kind, at + up],
+            dp,
+            ten,
+        )
+
+        @pl.when(((up == 1) & (place > 0)) | ((up == 0) & (place < cols_n - 1)))
+        def _():
+            copy.wait_recv()
+
+    def g_far(kind, step):
         to = lax.rem(place + step, cols_n)
         return rdma(
-            packs[kind].at[to, side],
-            got_z[kind].at[layer, step - 1],
-            gzs_sem.at[kind, step - 1],
-            gzr_sem.at[layer, kind, step - 1],
+            packs[kind].at[to],
+            got_z[kind].at[step - 1],
+            gzs_sem.at[kind, step],
+            gzr_sem.at[kind, step - 1],
             to * 2 + side,
             ten,
         )
 
     def g_free(kind, layer):
         add_upto(layer, (3 - kind) * cols_n + cols_n - 1)
-        for at in range(cols_n):
-            g_x(kind, layer, at).wait_send()
-        for step in range(1, cols_n):
-            g_z(kind, layer, step).wait_send()
+        for turn_at in range(cols_n - 1):
+            at = turn_of(turn_at)
+            if kind in Z_FIRST:
+                g_far(kind, turn_at + 1).wait_send()
+            else:
+                g_z(kind, at).wait_send()
+                g_x(kind, at).wait_send()
+        g_x(kind, place).wait_send()
+
+    def give_credit(kind):
+        pl.semaphore_signal(
+            credit.at[0, kind], inc=1, device_id=(across, ten), device_id_type=MESH
+        )
+        if kind in Z_FIRST:
+            for step in range(1, cols_n):
+                pl.semaphore_signal(
+                    credit.at[1, kind], inc=1, device_id=(along(step), ten), device_id_type=MESH
+                )
+            return
+
+        @pl.when(place > 0)
+        def _():
+            pl.semaphore_signal(
+                credit.at[1, kind], inc=1, device_id=(dp - 2, ten), device_id_type=MESH
+            )
+
+        @pl.when(place < cols_n - 1)
+        def _():
+            pl.semaphore_signal(
+                credit.at[2, kind], inc=1, device_id=(dp + 2, ten), device_id_type=MESH
+            )
+
+    def take_credit_x(kind):
+        pl.semaphore_wait(credit.at[0, kind], 1)
+
+    def take_credit_z(kind):
+        if kind in Z_FIRST:
+            pl.semaphore_wait(credit.at[1, kind], cols_n - 1)
+            return
+
+        @pl.when(place < cols_n - 1)
+        def _():
+            pl.semaphore_wait(credit.at[1, kind], 1)
+
+        @pl.when(place > 0)
+        def _():
+            pl.semaphore_wait(credit.at[2, kind], 1)
 
     def chunks_of(kind):
         if kind == 0:
@@ -1169,36 +1338,44 @@
     ]
     added = [0]
 
-    def turn_of(turn_at):
-        return lax.rem(place + 1 + turn_at, cols_n)
+    def add_event(kind, layer, turn_at):
+        if layer + 1 < LAYERS and turn_at == 0 and kind not in Z_FIRST:
+            take_credit_z(kind)
+        at = turn_of(turn_at)
+        last = turn_at + 1 == cols_n
+        if kind in Z_FIRST:
+            if last:
+                if layer + 1 < LAYERS:
+                    take_credit_x(kind)
+                for step in range(1, cols_n):
+                    g_far(kind, step).wait_recv()
+                for piece in chunks_of(kind):
+                    ours = (at, 1 - side) + piece
+                    total = packs[kind][ours].astype(f32)
+                    for step in range(1, cols_n):
+                        total = total + got_z[kind][(step - 1, 1 - side) + piece].astype(f32)
+                    packs[kind][ours] = total.astype(b16)
+                g_x(kind, at).start()
+            return
+        if last:
+            return
+        up = is_up(at)
+        g_x(kind, at).wait_recv()
+        g_z_came(kind, at, up)
+        for piece in chunks_of(kind):
+            ours = (at, side) + piece
+            packs[kind][ours] = (
+                packs[kind][ours].astype(f32)
+                + got_x[kind][(at,) + piece].astype(f32)
+                + got_z[kind][(at + up,) + piece].astype(f32)
+            ).astype(b16)
+        g_z(kind, at).start()
 
     def add_upto(layer_at, index):
         index = (LAYERS - 1 - layer_at) * 4 * cols_n + index
         while added[0] <= min(index, len(g_order) - 1):
-            kind, layer, turn_at = g_order[added[0]]
-            to = turn_of(turn_at)
-            g_x(kind, layer, to).wait_recv()
-            for piece in chunks_of(kind):
-                ours = (to, side) + piece
-                theirs = (layer, to) + piece
-                packs[kind][ours] = (
-                    packs[kind][ours].astype(f32) + got_x[kind][theirs].astype(f32)
-                ).astype(b16)
-            if turn_at + 1 < cols_n:
-                g_z(kind, layer, turn_at + 1).start()
+            add_event(*g_order[added[0]])
             added[0] += 1
-
-    masters = (
-        (lw_qkv, lw_out, lw_in, lw_back),
-        (lm_qkv, lm_out, lm_in, lm_back),
-        (lv_qkv, lv_out, lv_in, lv_back),
-    )
-    held = ((fw_q, fw_o, fw_i, fw_b), (fm_q, fm_o, fm_i, fm_b), (fv_q, fv_o, fv_i, fv_b))
-
-    def lamb_load(kind, layer, which):
-        return pltpu.make_async_copy(
-            masters[which][kind].at[layer], held[which][kind], lamb_sem.at[which, kind]
-        )
 
     def lamb_update(weight, first, second, gradient, decay):
         moment_one = BETA_ONE * first + (1.0 - BETA_ONE) * gradient
@@ -1215,39 +1392,52 @@
 
     def g_end(kind, layer):
         add_upto(layer, (3 - kind) * cols_n + cols_n - 1)
-        for step in range(1, cols_n):
-            g_z(kind, layer, step).wait_recv()
+        g_x(kind, place).wait_recv()
+        if kind not in Z_FIRST:
+            for up in (0, 1):
+                g_z_came(kind, place, up)
         for which in range(3):
-            lamb_load(kind, layer, which).wait()
+            if which or layer + 1 < LAYERS:
+                lamb_load(kind, layer, which).wait()
         for piece in chunks_of(kind):
             total = packs[kind][(place, side) + piece].astype(f32)
-            for step in range(1, cols_n):
-                total = total + got_z[kind][(layer, step - 1) + piece].astype(f32)
+            if kind in Z_FIRST:
+                total = total + got_x[kind][(0,) + piece].astype(f32)
+            else:
+                total = total + got_x[kind][(place,) + piece].astype(f32)
+            if kind in Z_FIRST:
+                for step in range(1, cols_n):
+                    total = total + got_z[kind][(step - 1, side) + piece].astype(f32)
+            else:
+                for up in (0, 1):
+                    total = total + got_z[kind][(place + up,) + piece].astype(f32)
             here = piece if piece else (slice(None),)
             weight = held[0][kind][here]
             step_by = lamb_update(
                 weight, held[1][kind][here], held[2][kind][here], total, DECAY_RATE
             )
-            held[1][kind][here] = total
+            packs[kind][(place, side) + piece] = total.astype(b16)
             note_norm((layer * 4 + kind) * 2, weight)
             note_norm((layer * 4 + kind) * 2 + 1, step_by)
         fin_copy(kind, layer).start()
         if layer:
-            for which in (0, 2):
+            give_credit(kind)
+            for which in range(3):
                 lamb_load(kind, layer - 1, which).start()
 
-    def lamb_more(kind, layer):
-        if layer + 1 < LAYERS:
-            fin_copy(kind, layer + 1).wait()
-            lamb_load(kind, layer, 1).start()
-
     def fin_copy(kind, layer):
-        return pltpu.make_async_copy(held[1][kind], sums[kind].at[layer], fin_sem.at[kind])
+        return pltpu.make_async_copy(
+            packs[kind].at[place, side], sums[kind].at[layer], fin_sem.at[kind]
+        )
 
     def pair_rows(at):
         return pl.ds(mult(at * 2 * cut, 2 * cut), 2 * cut)
 
     def grad_back(layer):
+        if layer + 1 < LAYERS:
+            fin_copy(3, layer + 1).wait()
+            (take_credit_z if 3 in Z_FIRST else take_credit_x)(3)
+
         def one(turn_at, carry):
             at = turn_of(turn_at)
             for piece in range(hidden_cols // 512):
@@ -1255,12 +1445,20 @@
                 value = dot_nn(g_turn[layer, rows, :], m_full[:, pair_rows(at)]).astype(b16)
                 pk_b[at, 0, rows, :] = value[:, :cut]
                 pk_b[at, 1, rows, :] = value[:, cut:]
-            g_x(3, layer, at).start()
+            if 3 not in Z_FIRST:
+                g_x(3, at).start()
             return carry
 
         lax.fori_loop(0, cols_n, one, 0)
+        if 3 in Z_FIRST:
+            for step in range(1, cols_n):
+                g_far(3, step).start()
 
     def grad_in(layer):
+        if layer + 1 < LAYERS:
+            fin_copy(2, layer + 1).wait()
+            (take_credit_z if 2 in Z_FIRST else take_credit_x)(2)
+
         def one(turn_at, carry):
             at = turn_of(turn_at)
             for piece in range(hidden_cols // 512):
@@ -1268,33 +1466,53 @@
                 value = dot_nn(m_turn[layer, pair_rows(at), :], active[:, cols]).astype(b16)
                 pk_i[at, 0, :, cols] = value[:cut]
                 pk_i[at, 1, :, cols] = value[cut:]
-            g_x(2, layer, at).start()
+            if 2 not in Z_FIRST:
+                g_x(2, at).start()
             return carry
 
         lax.fori_loop(0, cols_n, one, 0)
+        if 2 in Z_FIRST:
+            for step in range(1, cols_n):
+                g_far(2, step).start()
 
     def grad_out(layer):
+        if layer + 1 < LAYERS:
+            fin_copy(1, layer + 1).wait()
+            (take_credit_z if 1 in Z_FIRST else take_credit_x)(1)
+
         def one(turn_at, carry):
             at = turn_of(turn_at)
             value = dot_nn(o_turn[layer], h_full[:, pair_rows(at)]).astype(b16)
             pk_o[at, 0] = value[:, :cut]
             pk_o[at, 1] = value[:, cut:]
-            g_x(1, layer, at).start()
+            if 1 not in Z_FIRST:
+                g_x(1, at).start()
             return carry
 
         lax.fori_loop(0, cols_n, one, 0)
+        if 1 in Z_FIRST:
+            for step in range(1, cols_n):
+                g_far(1, step).start()
 
     def grad_qkv(layer):
+        if layer + 1 < LAYERS:
+            fin_copy(0, layer + 1).wait()
+            (take_credit_z if 0 in Z_FIRST else take_credit_x)(0)
+
         def one(turn_at, carry):
             at = turn_of(turn_at)
             for which in range(3):
                 value = dot_nn(h_turn[layer, pair_rows(at), :], d_qkv[which]).astype(b16)
                 pk_q[at, 0, which] = value[:cut]
                 pk_q[at, 1, which] = value[cut:]
-            g_x(0, layer, at).start()
+            if 0 not in Z_FIRST:
+                g_x(0, at).start()
             return carry
 
         lax.fori_loop(0, cols_n, one, 0)
+        if 0 in Z_FIRST:
+            for step in range(1, cols_n):
+                g_far(0, step).start()
 
     def norm_back(kept, upstream, gain):
         center, rate = norm_parts(kept)
@@ -1312,7 +1530,7 @@
 
     norms[...] = jnp.zeros_like(norms)
     for kind in range(ROWS_MAT):
-        for which in range(3):
+        for which in (1, 2):
             lamb_load(kind, LAYERS - 1, which).start()
     load_c.wait()
     for layer in reversed(range(LAYERS)):
@@ -1330,12 +1548,11 @@
             gat_start(m_full, which)
         marks = BACK_SLOTS[0 if last else 1]
         add_upto(layer, marks[0])
-        gat_end(m_full)
         if not last:
             g_free(3, layer + 1)
             g_end(3, layer + 1)
+        gat_end(m_full)
         grad_back(layer)
-        lamb_more(3, layer)
         add_upto(layer, marks[1])
 
         def slope_tile(tile, carry):
@@ -1355,7 +1572,6 @@
             g_free(2, layer + 1)
             g_end(2, layer + 1)
         grad_in(layer)
-        lamb_more(2, layer)
         add_upto(layer, marks[3])
         sum_end()
         if last:
@@ -1377,7 +1593,6 @@
             g_end(1, layer + 1)
         attn[...] = dot_nt(h_full[...], w_o[layer]).astype(b16)
         grad_out(layer)
-        lamb_more(1, layer)
         if last:
             out_logits.wait()
         add_upto(layer, marks[5])
@@ -1403,7 +1618,6 @@
             g_free(0, layer + 1)
             g_end(0, layer + 1)
         grad_qkv(layer)
-        lamb_more(0, layer)
         add_upto(layer, marks[8])
         sum_end()
         for which in range(2):
@@ -1546,8 +1760,7 @@
     data_parts, tensor_parts = parts
     return (
         tensor_parts == 4
-        and data_parts % 2 == 0
-        and data_parts > 2
+        and data_parts == 8
         and width // data_parts == LANES
         and head_cols // heads_here == 64
         and head_cols % TILE == 0
@@ -1586,34 +1799,10 @@
     share = tokens // 4
     cut = width // data_parts
     cols_n = data_parts // 2
-    bucket = bucket_ids[0]
-    seq_span = jnp.where(bucket == 0, tokens // 4, jnp.where(bucket == 1, tokens // 2, tokens))
-    seq_of = jnp.arange(tokens, dtype=jnp.int32) // seq_span
-    live = (key_mask == 1) & (seq_of < seq_counts[0])
-    key_ids = jnp.where(
-        jnp.arange(16, dtype=jnp.int32)[:, None] < 8,
-        jnp.where(live, seq_of, -1).astype(f32)[None, :],
-        1.0 / seq_span.astype(f32),
-    )
     owned = vectors.shape[2]
-    mine = (jnp.arange(LANES, dtype=jnp.int32) // owned) == ten
-
-    def small_rows(wide, narrow, fill):
-        rows = jnp.tile(wide.reshape(LAYERS * 8, owned), (1, LANES // owned))
-        rows = jnp.where(mine[None, :], rows, fill)
-        rest = jnp.full((32 - LAYERS * 9, LANES), fill, f32)
-        return jnp.concatenate([rows, narrow, rest], axis=0)
-
-    small_in = jnp.stack(
-        [
-            small_rows(vectors, bias_in, 0.0),
-            small_rows(arrays[16], arrays[17], 0.0),
-            small_rows(arrays[22], arrays[23], 1.0),
-        ]
-    )
-
     hbm = pl.BlockSpec(memory_space=pl.ANY)
     vmem = pl.BlockSpec(memory_space=pltpu.VMEM)
+    smem = pl.BlockSpec(memory_space=pltpu.SMEM)
     dma = pltpu.SemaphoreType.DMA
     shape = jax.ShapeDtypeStruct
     n = LAYERS
@@ -1631,11 +1820,13 @@
             shape((share, width), f32),
             shape((heads, tokens, tokens), b16),
         )
-        + tuple(shape((n,) + size, f32) for size in grad_shapes)
+        + tuple(shape((n,) + size, b16) for size in grad_shapes)
         + (shape((24, LANES), f32),) * 2,
-        in_specs=[hbm, hbm, hbm, vmem, vmem] + [hbm] * 16,
+        in_specs=[hbm] * 3 + [smem] * 2 + [vmem] * 7 + [hbm] * 12,
         out_specs=(hbm, hbm, vmem, hbm, hbm, hbm, hbm, hbm, vmem, vmem),
         scratch_shapes=[
+            pltpu.VMEM((8, tokens), f32),
+            pltpu.VMEM((3, 32, LANES), f32),
             pltpu.VMEM((n, 3, width, head_cols), b16),
             pltpu.VMEM((n, head_cols, width), b16),
             pltpu.VMEM((n, width, hidden_cols), b16),
@@ -1671,8 +1862,14 @@
             pltpu.VMEM((data_parts - 1, n * 8 + 8, LANES), f32),
         ]
         + [pltpu.VMEM((cols_n, 2) + size, b16) for size in grad_shapes]
-        + [pltpu.VMEM((n, cols_n) + size, b16) for size in grad_shapes]
-        + [pltpu.VMEM((n, cols_n - 1) + size, b16) for size in grad_shapes]
+        + [
+            pltpu.VMEM((1 if kind in Z_FIRST else cols_n,) + size, b16)
+            for kind, size in enumerate(grad_shapes)
+        ]
+        + [
+            pltpu.VMEM(((cols_n - 1, 2) if kind in Z_FIRST else (cols_n + 1,)) + size, b16)
+            for kind, size in enumerate(grad_shapes)
+        ]
         + [pltpu.VMEM(size, f32) for _ in range(3) for size in grad_shapes]
         + [
             pltpu.VMEM((n * 8, width), f32),
@@ -1699,14 +1896,15 @@
             dma((data_parts + 2,)),
             dma((data_parts + 2,)),
             dma((4, cols_n)),
-            dma((n, 4, cols_n)),
-            dma((4, cols_n - 1)),
-            dma((n, 4, cols_n - 1)),
+            dma((4, cols_n)),
+            dma((4, cols_n)),
+            dma((4, cols_n + 1)),
             dma((4,)),
             dma((4,)),
             dma((3, 4)),
             dma((data_parts + 2,)),
             dma((data_parts + 2,)),
+            pltpu.SemaphoreType.REGULAR((3, 4)),
         ],
         compiler_params=pltpu.CompilerParams(
             collective_id=0, has_side_effects=True, vmem_limit_bytes=63 * 1024 * 1024
@@ -1715,12 +1913,15 @@
         hidden_in,
         logits_in,
         cotangent,
-        key_ids,
-        small_in,
-        w_qkv.astype(b16),
-        w_out.astype(b16),
-        w_in.astype(b16),
-        w_back.astype(b16),
+        bucket_ids,
+        seq_counts,
+        key_mask.reshape(1, tokens),
+        vectors,
+        bias_in,
+        arrays[16],
+        arrays[17],
+        arrays[22],
+        arrays[23],
         *arrays[6:10],
         *arrays[12:16],
         *arrays[18:22],
@@ -1729,7 +1930,7 @@
     small = results[8]
     vec_sum = lax.dynamic_slice_in_dim(small[: LAYERS * 8], ten * owned, owned, 1)
     bin_sum = small[LAYERS * 8 : LAYERS * 9]
-    grads_all = results[4:8] + (vec_sum.reshape(LAYERS, 8, owned), bin_sum)
+    grads_all = tuple(one.astype(f32) for one in results[4:8]) + (vec_sum.reshape(LAYERS, 8, owned), bin_sum)
     masters = arrays[6:12]
     firsts = arrays[12:18]
     seconds = arrays[18:24]

time: 371 us -> 353 us (0.951)
  other arithmetic: 22.8 us -> 13 us
  local copies, waits for them, and re-layouts: 10.5 us -> 5.61 us
    convert_element_type x5 -> x0, other arithmetic: 6.08 us -> none  [the longest x1 1.92 us: shards(): w_qkv.astype(b16)]
where the time goes in v3:
time: 353 us
  Pallas kernels  332 us (94%)
  other arithmetic  13 us (4%)
  local copies, waits for them, and re-layouts  5.61 us (2%)
    pallas_call x1, Pallas kernels, shards(): pl.pallas_call(functools.partial(step_kernel, data_parts), out_shape=(sha...  332 us
    sub x6, other arithmetic, shards(): master - LEARN_RATE * trust_all[group_at].reshape((LAYERS,) + (1,) * (mas...  7.71 us

profile of v3, /device:TPU:0, one launch (start us, length us, event | category | flops | bytes accessed | tf_op | source)
XLA Modules:
  0.0 353.2 jit_solution(9085729271521880560)
XLA Ops:
  1.9 332.4 %shard_map.407 = (bf16[128,1024]{1,0:T(8,128)(2,1)}, bf16[4,512,512]{2,1,0:T(8,128)(2,1)}, f32[128,1024]{1,0:T(8,128)}, bf16[4,512,512]{2,1,0:T(8,128)(2,1)}, bf...) custom-call(bf16[512,1024]{1,0:T(8,128)(2,1)} %hidden_in.1, ...), custom_call_target="tpu_custom_call" | custom-call | tf_op jit(solution)/shard_map/pallas_call | solution.py:1815
  334.4 4.3 %bitcast_convert_fusion = f32[1,4,512,512]{3,2,1,0:T(8,128)} fusion(bf16[4,512,512]{2,1,0:T(8,128)(2,1)} %get-tuple-element.36), kind=kLoop, calls=%fused_computation | loop fusion | flops 1048576 | bytes 6291456 | tf_op jit(solution)/shard_map/convert_element_type | solution.py:1965
  338.7 0.1 sqrt_reduce_fusion
  338.8 0.1 slice.62
  338.9 0.1 slice.63
  339.1 0.1 slice.67
  339.2 0.1 slice.65
  339.3 0.1 fusion.35
  339.4 0.3 multiply_reduce_fusion
  339.8 1.6 multiply_subtract_fusion.2
  341.4 0.9 multiply_subtract_fusion.3
  342.4 0.4 copy-done.15
  342.8 0.4 copy-done
  343.2 2.0 multiply_subtract_fusion.1
  345.2 0.3 copy-done.4
  345.5 0.7 copy-done.5
  346.2 0.1 copy-done.14
  346.4 1.9 multiply_subtract_fusion
  348.3 0.7 fusion.31
  349.0 0.6 multiply_subtract_fusion.4
  349.7 0.6 pad_maximum_fusion
  350.3 0.7 copy.52
  351.0 1.3 copy.53
  352.4 0.8 copy.54
  (52 shorter events, 0.3 us)
Async XLA Ops:
  334.3 4.4 %copy-start.22 = (f32[24,128]{1,0:T(8,128)S(1)}, f32[24,128]{1,0:T(8,128)}, u32[]{:S(2)}) copy-start(f32[24,128]{1,0:T(8,128)} %get-tuple-element.42) | copy-start | bytes 36868
  334.3 5.3 %copy-start.6 = (f32[2,3,128,256]{3,2,1,0:T(8,128)S(1)}, f32[2,3,128,256]{3,2,1,0:T(8,128)}, u32[]{:S(2)}) copy-start(f32[2,3,128,256]{3,2,1,0:T(8,128)} %lw_qkv.1) | copy-start | bytes 2359300
  334.3 5.3 %copy-start.7 = (f32[2,3,128,256]{3,2,1,0:T(8,128)S(1)}, f32[2,3,128,256]{3,2,1,0:T(8,128)}, u32[]{:S(2)}) copy-start(f32[2,3,128,256]{3,2,1,0:T(8,128)} %lm_qkv.1) | copy-start | bytes 2359300
  334.4 5.3 %copy-start.8 = (f32[2,3,128,256]{3,2,1,0:T(8,128)S(1)}, f32[2,3,128,256]{3,2,1,0:T(8,128)}, u32[]{:S(2)}) copy-start(f32[2,3,128,256]{3,2,1,0:T(8,128)} %lv_qkv.1) | copy-start | bytes 2359300
  334.4 5.3 %copy-start.16 = (bf16[2,3,128,256]{3,2,1,0:T(8,128)(2,1)S(1)}, bf16[2,3,128,256]{3,2,1,0:T(8,128)(2,1)}, u32[]{:S(2)}) copy-start(bf16[2,3,128,256]{3,2,1,0:T(8,128)(2,1)} %get-tuple-element.37) | copy-start | bytes 1179652
  339.7 1.7 copy-start.10
  339.7 1.7 copy-start.11
  339.7 2.6 copy-start.1
  339.7 2.6 copy-start.2
  339.8 3.0 copy-start.15
  341.4 1.9 copy-start
  343.2 2.0 copy-start.3
  343.2 2.2 copy-start.4
  343.2 3.0 copy-start.5
  343.2 3.1 copy-start.14
  346.4 1.9 copy-start.23
  346.4 1.9 copy-start.19
  346.4 1.9 copy-start.20
  346.4 1.9 copy-start.21
  346.4 2.6 copy-start.24
  346.4 2.6 copy-start.25
  346.4 2.6 copy-start.26
  346.4 3.9 %copy-start.17 = (bf16[128,1024]{1,0:T(8,128)(2,1)S(1)}, bf16[128,1024]{1,0:T(8,128)(2,1)}, u32[]{:S(2)}) copy-start(bf16[128,1024]{1,0:T(8,128)(2,1)} %get-tuple-element.90) | copy-start | bytes 786436
  346.4 4.6 %copy-start.9 = (bf16[4,512,512]{2,1,0:T(8,128)(2,1)S(1)}, bf16[4,512,512]{2,1,0:T(8,128)(2,1)}, u32[]{:S(2)}) copy-start(bf16[4,512,512]{2,1,0:T(8,128)(2,1)} %get-tuple-element.34) | copy-start | bytes 6291460
  (3 other events, 4.7 us)

commit v4 on v3

--- a/solution.py
+++ b/solution.py
@@ -479,7 +479,7 @@
 BACK_SLOTS = (
     (-9, -9, 0, 1, 2, 3, 4, 5, 6),
     (-9, -5, -4, -2, 0, 0, 1, 2, 3),
-    (4,),
+    (8,),
 )
 
 
@@ -805,11 +805,13 @@
 
         @pl.when(place == 0)
         def _():
-            slots[1 : cols_n + 1] = jnp.zeros((cols_n,) + slots.shape[1:], b16)
+            slots[0] = jnp.zeros(slots.shape[1:], b16)
+            slots[3] = jnp.zeros(slots.shape[1:], b16)
 
         @pl.when(place == cols_n - 1)
         def _():
-            slots[0:cols_n] = jnp.zeros((cols_n,) + slots.shape[1:], b16)
+            slots[2] = jnp.zeros(slots.shape[1:], b16)
+            slots[3] = jnp.zeros(slots.shape[1:], b16)
 
     owned = vec_w.shape[2]
     spread_row = lax.broadcasted_iota(jnp.int32, (owned, LANES), 0)
@@ -1218,13 +1220,13 @@
 
     def turn_of(turn_at):
         upper = place // 2
-        near = upper * (cols_n - 1) + (1 - 2 * upper) * place
-        swing = lax.rem(3 + turn_at + turn_at * (turn_at - 1) // 2, 4)
-        at = (1 - near) * (3 - turn_at) + near * swing
+        inner = upper * (cols_n - 1) + (1 - 2 * upper) * place
+        pairs_of = turn_at * (turn_at - 1)
+        swing = 2 * turn_at - pairs_of // 2 - pairs_of * (turn_at - 2) // 3
+        at = (1 - inner) * (3 - turn_at) + inner * swing
         return upper * (cols_n - 1) + (1 - 2 * upper) * at
 
-    def is_up(at):
-        return (at - place + cols_n) // cols_n
+    at_end = (place == 0) | (place == cols_n - 1)
 
     def g_x(kind, at):
         first = kind not in Z_FIRST
@@ -1238,27 +1240,30 @@
         )
 
     def g_z(kind, at):
-        up = is_up(at)
+        far = (at - place) * (at - place) // 9
+        to = (1 - far) * at + far * (place + 1 - 2 * (place // 2))
+        slot = (1 - far) * (lax.rem(at - place + cols_n, cols_n) - 1) + far * 3
         return rdma(
             packs[kind].at[at, side],
-            got_z[kind].at[at + up],
+            got_z[kind].at[slot],
             gzs_sem.at[kind, at],
-            gzr_sem.at[kind, at + up],
-            dp + 2 * (2 * up - 1),
+            gzr_sem.at[kind, slot],
+            to * 2 + side,
             ten,
         )
 
-    def g_z_came(kind, at, up):
+    def g_z_came(kind, slot):
         copy = rdma(
-            packs[kind].at[at, side],
-            got_z[kind].at[at + up],
-            gzs_sem.at[kind, at],
-            gzr_sem.at[kind, at + up],
+            packs[kind].at[0, side],
+            got_z[kind].at[slot],
+            gzs_sem.at[kind, 0],
+            gzr_sem.at[kind, slot],
             dp,
             ten,
         )
-
-        @pl.when(((up == 1) & (place > 0)) | ((up == 0) & (place < cols_n - 1)))
+        comes = (place > 0, place >= 0, place < cols_n - 1, jnp.logical_not(at_end))[slot]
+
+        @pl.when(comes)
         def _():
             copy.wait_recv()
 
@@ -1295,17 +1300,13 @@
                 )
             return
 
-        @pl.when(place > 0)
-        def _():
-            pl.semaphore_signal(
-                credit.at[1, kind], inc=1, device_id=(dp - 2, ten), device_id_type=MESH
-            )
-
-        @pl.when(place < cols_n - 1)
-        def _():
-            pl.semaphore_signal(
-                credit.at[2, kind], inc=1, device_id=(dp + 2, ten), device_id_type=MESH
-            )
+        for hop in (2, -2, 1, -1):
+
+            @pl.when(place < cols_n - hop if hop > 0 else place >= -hop)
+            def _():
+                pl.semaphore_signal(
+                    credit.at[1, kind], inc=1, device_id=(dp + 2 * hop, ten), device_id_type=MESH
+                )
 
     def take_credit_x(kind):
         pl.semaphore_wait(credit.at[0, kind], 1)
@@ -1315,13 +1316,13 @@
             pl.semaphore_wait(credit.at[1, kind], cols_n - 1)
             return
 
-        @pl.when(place < cols_n - 1)
+        @pl.when(at_end)
         def _():
-            pl.semaphore_wait(credit.at[1, kind], 1)
-
-        @pl.when(place > 0)
+            pl.semaphore_wait(credit.at[1, kind], 2)
+
+        @pl.when(jnp.logical_not(at_end))
         def _():
-            pl.semaphore_wait(credit.at[2, kind], 1)
+            pl.semaphore_wait(credit.at[1, kind], 3)
 
     def chunks_of(kind):
         if kind == 0:
@@ -1359,16 +1360,16 @@
             return
         if last:
             return
-        up = is_up(at)
         g_x(kind, at).wait_recv()
-        g_z_came(kind, at, up)
+        passing = turn_at == cols_n - 2
+        if passing:
+            g_z_came(kind, 3)
         for piece in chunks_of(kind):
             ours = (at, side) + piece
-            packs[kind][ours] = (
-                packs[kind][ours].astype(f32)
-                + got_x[kind][(at,) + piece].astype(f32)
-                + got_z[kind][(at + up,) + piece].astype(f32)
-            ).astype(b16)
+            total = packs[kind][ours].astype(f32) + got_x[kind][(at,) + piece].astype(f32)
+            if passing:
+                total = total + got_z[kind][(3,) + piece].astype(f32)
+            packs[kind][ours] = total.astype(b16)
         g_z(kind, at).start()
 
     def add_upto(layer_at, index):
@@ -1394,8 +1395,8 @@
         add_upto(layer, (3 - kind) * cols_n + cols_n - 1)
         g_x(kind, place).wait_recv()
         if kind not in Z_FIRST:
-            for up in (0, 1):
-                g_z_came(kind, place, up)
+            for slot in range(3):
+                g_z_came(kind, slot)
         for which in range(3):
             if which or layer + 1 < LAYERS:
                 lamb_load(kind, layer, which).wait()
@@ -1409,8 +1410,8 @@
                 for step in range(1, cols_n):
                     total = total + got_z[kind][(step - 1, side) + piece].astype(f32)
             else:
-                for up in (0, 1):
-                    total = total + got_z[kind][(place + up,) + piece].astype(f32)
+                for slot in range(3):
+                    total = total + got_z[kind][(slot,) + piece].astype(f32)
             here = piece if piece else (slice(None),)
             weight = held[0][kind][here]
             step_by = lamb_update(
@@ -1430,6 +1431,17 @@
             packs[kind].at[place, side], sums[kind].at[layer], fin_sem.at[kind]
         )
 
+    def g_x_go(kind, layer, turn_at, at):
+        if kind in Z_FIRST:
+            return
+        if layer:
+            g_x(kind, at).start()
+            return
+
+        @pl.when(turn_at < cols_n - 1)
+        def _():
+            g_x(kind, at).start()
+
     def pair_rows(at):
         return pl.ds(mult(at * 2 * cut, 2 * cut), 2 * cut)
 
@@ -1445,8 +1457,7 @@
                 value = dot_nn(g_turn[layer, rows, :], m_full[:, pair_rows(at)]).astype(b16)
                 pk_b[at, 0, rows, :] = value[:, :cut]
                 pk_b[at, 1, rows, :] = value[:, cut:]
-            if 3 not in Z_FIRST:
-                g_x(3, at).start()
+            g_x_go(3, layer, turn_at, at)
             return carry
 
         lax.fori_loop(0, cols_n, one, 0)
@@ -1466,8 +1477,7 @@
                 value = dot_nn(m_turn[layer, pair_rows(at), :], active[:, cols]).astype(b16)
                 pk_i[at, 0, :, cols] = value[:cut]
                 pk_i[at, 1, :, cols] = value[cut:]
-            if 2 not in Z_FIRST:
-                g_x(2, at).start()
+            g_x_go(2, layer, turn_at, at)
             return carry
 
         lax.fori_loop(0, cols_n, one, 0)
@@ -1485,8 +1495,7 @@
             value = dot_nn(o_turn[layer], h_full[:, pair_rows(at)]).astype(b16)
             pk_o[at, 0] = value[:, :cut]
             pk_o[at, 1] = value[:, cut:]
-            if 1 not in Z_FIRST:
-                g_x(1, at).start()
+            g_x_go(1, layer, turn_at, at)
             return carry
 
         lax.fori_loop(0, cols_n, one, 0)
@@ -1505,8 +1514,7 @@
                 value = dot_nn(h_turn[layer, pair_rows(at), :], d_qkv[which]).astype(b16)
                 pk_q[at, 0, which] = value[:cut]
                 pk_q[at, 1, which] = value[cut:]
-            if 0 not in Z_FIRST:
-                g_x(0, at).start()
+            g_x_go(0, layer, turn_at, at)
             return carry
 
         lax.fori_loop(0, cols_n, one, 0)
@@ -1618,6 +1626,10 @@
             g_free(0, layer + 1)
             g_end(0, layer + 1)
         grad_qkv(layer)
+        if layer == 0:
+            for kind in (3, 2, 1, 0):
+                if kind not in Z_FIRST:
+                    g_x(kind, place).start()
         add_upto(layer, marks[8])
         sum_end()
         for which in range(2):
@@ -1673,6 +1685,7 @@
         return carry
 
     lax.fori_loop(1, data_parts, small_go, 0)
+    add_upto(0, 4 * cols_n - 1)
     g_end(3, 0)
     g_end(2, 0)
     g_end(1, 0)
@@ -1867,7 +1880,7 @@
             for kind, size in enumerate(grad_shapes)
         ]
         + [
-            pltpu.VMEM(((cols_n - 1, 2) if kind in Z_FIRST else (cols_n + 1,)) + size, b16)
+            pltpu.VMEM(((cols_n - 1, 2) if kind in Z_FIRST else (cols_n,)) + size, b16)
             for kind, size in enumerate(grad_shapes)
         ]
         + [pltpu.VMEM(size, f32) for _ in range(3) for size in grad_shapes]
@@ -1898,7 +1911,7 @@
             dma((4, cols_n)),
             dma((4, cols_n)),
             dma((4, cols_n)),
-            dma((4, cols_n + 1)),
+            dma((4, cols_n)),
             dma((4,)),
             dma((4,)),
             dma((3, 4)),

time: 353 us -> 336 us (0.952)
  Pallas kernels: 332 us -> 315 us
    pallas_call x1, Pallas kernels: 332 us -> 315 us  [shards(): pl.pallas_call(functools.partial(step_kernel, data_parts), out_shape=(sha...]
where the time goes in v4:
time: 336 us
  Pallas kernels  315 us (94%)
  other arithmetic  13 us (4%)
  local copies, waits for them, and re-layouts  5.61 us (2%)
    pallas_call x1, Pallas kernels, shards(): pl.pallas_call(functools.partial(step_kernel, data_parts), out_shape=(sha...  315 us
    sub x6, other arithmetic, shards(): master - LEARN_RATE * trust_all[group_at].reshape((LAYERS,) + (1,) * (mas...  7.71 us

profile of v4, /device:TPU:0, one launch (start us, length us, event | category | flops | bytes accessed | tf_op | source)
XLA Modules:
  0.0 335.7 jit_solution(1651338678095781742)
XLA Ops:
  1.9 314.9 %shard_map.407 = (bf16[128,1024]{1,0:T(8,128)(2,1)}, bf16[4,512,512]{2,1,0:T(8,128)(2,1)}, f32[128,1024]{1,0:T(8,128)}, bf16[4,512,512]{2,1,0:T(8,128)(2,1)}, bf...) custom-call(bf16[512,1024]{1,0:T(8,128)(2,1)} %hidden_in.1, ...), custom_call_target="tpu_custom_call" | custom-call | tf_op jit(solution)/shard_map/pallas_call | solution.py:1828
  316.9 4.3 %bitcast_convert_fusion = f32[1,4,512,512]{3,2,1,0:T(8,128)} fusion(bf16[4,512,512]{2,1,0:T(8,128)(2,1)} %get-tuple-element.36), kind=kLoop, calls=%fused_computation | loop fusion | flops 1048576 | bytes 6291456 | tf_op jit(solution)/shard_map/convert_element_type | solution.py:1978
  321.3 0.1 sqrt_reduce_fusion
  321.4 0.1 slice.62
  321.5 0.1 slice.63
  321.7 0.1 slice.67
  321.8 0.1 slice.65
  321.8 0.1 fusion.35
  321.9 0.3 multiply_reduce_fusion
  322.3 1.6 multiply_subtract_fusion.2
  323.9 0.9 multiply_subtract_fusion.3
  324.9 0.4 copy-done.15
  325.3 0.4 copy-done
  325.8 2.0 multiply_subtract_fusion.1
  327.8 0.3 copy-done.4
  328.0 0.7 copy-done.5
  328.8 0.1 copy-done.14
  329.0 1.9 multiply_subtract_fusion
  330.9 0.7 fusion.31
  331.6 0.6 multiply_subtract_fusion.4
  332.2 0.6 pad_maximum_fusion
  332.8 0.7 copy.52
  333.6 1.3 copy.53
  335.0 0.8 copy.54
  (52 shorter events, 0.3 us)
Async XLA Ops:
  316.9 4.4 %copy-start.22 = (f32[24,128]{1,0:T(8,128)S(1)}, f32[24,128]{1,0:T(8,128)}, u32[]{:S(2)}) copy-start(f32[24,128]{1,0:T(8,128)} %get-tuple-element.42) | copy-start | bytes 36868
  316.9 5.3 %copy-start.6 = (f32[2,3,128,256]{3,2,1,0:T(8,128)S(1)}, f32[2,3,128,256]{3,2,1,0:T(8,128)}, u32[]{:S(2)}) copy-start(f32[2,3,128,256]{3,2,1,0:T(8,128)} %lw_qkv.1) | copy-start | bytes 2359300
  316.9 5.3 %copy-start.7 = (f32[2,3,128,256]{3,2,1,0:T(8,128)S(1)}, f32[2,3,128,256]{3,2,1,0:T(8,128)}, u32[]{:S(2)}) copy-start(f32[2,3,128,256]{3,2,1,0:T(8,128)} %lm_qkv.1) | copy-start | bytes 2359300
  316.9 5.3 %copy-start.8 = (f32[2,3,128,256]{3,2,1,0:T(8,128)S(1)}, f32[2,3,128,256]{3,2,1,0:T(8,128)}, u32[]{:S(2)}) copy-start(f32[2,3,128,256]{3,2,1,0:T(8,128)} %lv_qkv.1) | copy-start | bytes 2359300
  316.9 5.3 %copy-start.16 = (bf16[2,3,128,256]{3,2,1,0:T(8,128)(2,1)S(1)}, bf16[2,3,128,256]{3,2,1,0:T(8,128)(2,1)}, u32[]{:S(2)}) copy-start(bf16[2,3,128,256]{3,2,1,0:T(8,128)(2,1)} %get-tuple-element.37) | copy-start | bytes 1179652
  322.2 1.7 copy-start.10
  322.2 1.7 copy-start.11
  322.3 2.6 copy-start.1
  322.3 2.6 copy-start.2
  322.3 3.0 copy-start.15
  323.9 1.9 copy-start
  325.8 2.0 copy-start.3
  325.8 2.2 copy-start.4
  325.8 3.0 copy-start.5
  325.8 3.1 copy-start.14
  328.9 1.9 copy-start.23
  328.9 1.9 copy-start.19
  328.9 1.9 copy-start.20
  328.9 1.9 copy-start.21
  328.9 2.6 copy-start.24
  328.9 2.6 copy-start.25
  328.9 2.6 copy-start.26
  329.0 3.9 %copy-start.17 = (bf16[128,1024]{1,0:T(8,128)(2,1)S(1)}, bf16[128,1024]{1,0:T(8,128)(2,1)}, u32[]{:S(2)}) copy-start(bf16[128,1024]{1,0:T(8,128)(2,1)} %get-tuple-element.90) | copy-start | bytes 786436
  329.0 4.6 %copy-start.9 = (bf16[4,512,512]{2,1,0:T(8,128)(2,1)S(1)}, bf16[4,512,512]{2,1,0:T(8,128)(2,1)}, u32[]{:S(2)}) copy-start(bf16[4,512,512]{2,1,0:T(8,128)(2,1)} %get-tuple-element.34) | copy-start | bytes 6291460
  (3 other events, 4.7 us)

commit v5 on v4

--- a/solution.py
+++ b/solution.py
@@ -724,7 +724,7 @@
             ten,
         )
 
-    def w_z(kind, layer, from_place, col, way):
+    def w_z(kind, layer, from_place, col, way, send=True):
         dst = region(kind, layer, from_place * 2 + col)
         which = lax.rem(col + side, 2)
         return rdma(
@@ -732,7 +732,7 @@
             dst,
             zs_sem.at[layer, kind, from_place, which, (way + 1) // 2],
             zr_sem.at[layer, kind, from_place, which],
-            dp + 2 * way,
+            dp + 2 * way if send else dp,
             ten,
         )
 
@@ -768,7 +768,7 @@
 
             @pl.when(came >= 0 if way == 1 else came < cols_n)
             def _():
-                w_z(kind, layer, came, side, way).wait_recv()
+                w_z(kind, layer, came, side, way, False).wait_recv()
 
                 @pl.when(can_go[way])
                 def _():
@@ -1548,12 +1548,12 @@
             at = pl.ds(which * half, half)
             upstream = sum_chip[at, :].astype(f32) if last else grad_hidden[at, :]
             down, unit = norm_back(y_own[layer, at, :], upstream, vec_row(layer, 1))
+            m_full[own_rows(which), :] = down.astype(b16)
+            gat_start(m_full, which)
             note(base + 1, upstream * unit)
             note(base + 7, upstream)
             note(base + 6, down)
             d_keep[at, :] = down
-            m_full[own_rows(which), :] = down.astype(b16)
-            gat_start(m_full, which)
         marks = BACK_SLOTS[0 if last else 1]
         add_upto(layer, marks[0])
         if not last:
@@ -1588,12 +1588,12 @@
             at = pl.ds(which * half, half)
             upstream = sum_rows(which) + d_keep[at, :]
             down, unit = norm_back(x_own[layer, at, :], upstream, vec_row(layer, 0))
+            h_full[own_rows(which), :] = down.astype(b16)
+            gat_start(h_full, which)
             note(base + 0, upstream * unit)
             note(base + 5, upstream)
             note(base + 4, down)
             d_keep[at, :] = down
-            h_full[own_rows(which), :] = down.astype(b16)
-            gat_start(h_full, which)
         add_upto(layer, marks[4])
         gat_end(h_full)
         if not last:

time: 336 us -> 336 us (level)
  no operation moved by 1% of the time
where the time goes in v5:
time: 336 us
  Pallas kernels  315 us (94%)
  other arithmetic  13 us (4%)
  local copies, waits for them, and re-layouts  5.61 us (2%)
    pallas_call x1, Pallas kernels, shards(): pl.pallas_call(functools.partial(step_kernel, data_parts), out_shape=(sha...  315 us
    sub x6, other arithmetic, shards(): master - LEARN_RATE * trust_all[group_at].reshape((LAYERS,) + (1,) * (mas...  7.71 us

profile of v5, /device:TPU:0, one launch (start us, length us, event | category | flops | bytes accessed | tf_op | source)
XLA Modules:
  0.0 335.7 jit_solution(518472610688495133)
XLA Ops:
  1.9 314.9 %shard_map.407 = (bf16[128,1024]{1,0:T(8,128)(2,1)}, bf16[4,512,512]{2,1,0:T(8,128)(2,1)}, f32[128,1024]{1,0:T(8,128)}, bf16[4,512,512]{2,1,0:T(8,128)(2,1)}, bf...) custom-call(bf16[512,1024]{1,0:T(8,128)(2,1)} %hidden_in.1, ...), custom_call_target="tpu_custom_call" | custom-call | tf_op jit(solution)/shard_map/pallas_call | solution.py:1828
  316.9 4.3 %bitcast_convert_fusion = f32[1,4,512,512]{3,2,1,0:T(8,128)} fusion(bf16[4,512,512]{2,1,0:T(8,128)(2,1)} %get-tuple-element.36), kind=kLoop, calls=%fused_computation | loop fusion | flops 1048576 | bytes 6291456 | tf_op jit(solution)/shard_map/convert_element_type | solution.py:1978
  321.3 0.1 sqrt_reduce_fusion
  321.4 0.1 slice.62
  321.5 0.1 slice.63
  321.7 0.1 slice.67
  321.7 0.1 slice.65
  321.8 0.1 fusion.35
  321.9 0.3 multiply_reduce_fusion
  322.3 1.6 multiply_subtract_fusion.2
  323.9 0.9 multiply_subtract_fusion.3
  324.9 0.4 copy-done.15
  325.3 0.4 copy-done
  325.8 2.0 multiply_subtract_fusion.1
  327.8 0.3 copy-done.4
  328.0 0.7 copy-done.5
  328.8 0.1 copy-done.14
  329.0 1.9 multiply_subtract_fusion
  330.8 0.7 fusion.31
  331.6 0.6 multiply_subtract_fusion.4
  332.2 0.6 pad_maximum_fusion
  332.8 0.7 copy.52
  333.5 1.3 copy.53
  334.9 0.8 copy.54
  (52 shorter events, 0.3 us)
Async XLA Ops:
  316.8 4.4 %copy-start.22 = (f32[24,128]{1,0:T(8,128)S(1)}, f32[24,128]{1,0:T(8,128)}, u32[]{:S(2)}) copy-start(f32[24,128]{1,0:T(8,128)} %get-tuple-element.42) | copy-start | bytes 36868
  316.9 5.3 %copy-start.6 = (f32[2,3,128,256]{3,2,1,0:T(8,128)S(1)}, f32[2,3,128,256]{3,2,1,0:T(8,128)}, u32[]{:S(2)}) copy-start(f32[2,3,128,256]{3,2,1,0:T(8,128)} %lw_qkv.1) | copy-start | bytes 2359300
  316.9 5.3 %copy-start.7 = (f32[2,3,128,256]{3,2,1,0:T(8,128)S(1)}, f32[2,3,128,256]{3,2,1,0:T(8,128)}, u32[]{:S(2)}) copy-start(f32[2,3,128,256]{3,2,1,0:T(8,128)} %lm_qkv.1) | copy-start | bytes 2359300
  316.9 5.3 %copy-start.8 = (f32[2,3,128,256]{3,2,1,0:T(8,128)S(1)}, f32[2,3,128,256]{3,2,1,0:T(8,128)}, u32[]{:S(2)}) copy-start(f32[2,3,128,256]{3,2,1,0:T(8,128)} %lv_qkv.1) | copy-start | bytes 2359300
  316.9 5.3 %copy-start.16 = (bf16[2,3,128,256]{3,2,1,0:T(8,128)(2,1)S(1)}, bf16[2,3,128,256]{3,2,1,0:T(8,128)(2,1)}, u32[]{:S(2)}) copy-start(bf16[2,3,128,256]{3,2,1,0:T(8,128)(2,1)} %get-tuple-element.37) | copy-start | bytes 1179652
  322.2 1.7 copy-start.10
  322.2 1.7 copy-start.11
  322.3 2.6 copy-start.1
  322.3 2.6 copy-start.2
  322.3 3.0 copy-start.15
  323.9 1.9 copy-start
  325.8 2.0 copy-start.3
  325.8 2.2 copy-start.4
  325.8 3.0 copy-start.5
  325.8 3.1 copy-start.14
  328.9 1.9 copy-start.23
  328.9 1.9 copy-start.19
  328.9 1.9 copy-start.20
  328.9 1.9 copy-start.21
  328.9 2.6 copy-start.24
  328.9 2.6 copy-start.25
  328.9 2.6 copy-start.26
  328.9 3.9 %copy-start.17 = (bf16[128,1024]{1,0:T(8,128)(2,1)S(1)}, bf16[128,1024]{1,0:T(8,128)(2,1)}, u32[]{:S(2)}) copy-start(bf16[128,1024]{1,0:T(8,128)(2,1)} %get-tuple-element.90) | copy-start | bytes 786436
  328.9 4.6 %copy-start.9 = (bf16[4,512,512]{2,1,0:T(8,128)(2,1)S(1)}, bf16[4,512,512]{2,1,0:T(8,128)(2,1)}, u32[]{:S(2)}) copy-start(bf16[4,512,512]{2,1,0:T(8,128)(2,1)} %get-tuple-element.34) | copy-start | bytes 6291460
  (3 other events, 4.7 us)
